TPU v7x, 32 devices: a whole 2x2x4 slice. The times are simulated.
32 devices in a mesh: seq: 8 (over y, x, core), tp: 4 (over z).
Axes of the slice: x: 2, y: 2, z: 4, core: 2. Of those that a mesh axis runs over, the one named last changes fastest.
Arguments:
- layer_input: bfloat16 [8192, 2048], P(('seq', 'tp')), may hold values from -6 to 6
- output_grad: bfloat16 [8192, 2048], P(('seq', 'tp')), may hold values from -6 to 6
- segment_ids: int32 [8192], P('seq'), may hold values from 0 to 41, as said below
- positions: int32 [8192], P('seq'), may hold values from 0 to 1999, as said below
- qkv_weight: float32 [2048, 3072], P('seq', 'tp'), may hold values from -0.125 to 0.125
- qkv_moment: float32 [2048, 3072], P('seq', 'tp'), may hold values from -192 to 192
- qkv_square: float32 [2048, 3072], P('seq', 'tp'), may hold values from 65536 to 2097152
- out_weight: float32 [2048, 2048], P('tp', 'seq'), may hold values from -2 to 2
- out_moment: float32 [2048, 2048], P('tp', 'seq'), may hold values from -192 to 192
- out_square: float32 [2048, 2048], P('tp', 'seq'), may hold values from 128 to 4096
- gate_up_weight: float32 [2, 2048, 8192], P(None, 'seq', 'tp'), may hold values from -0.125 to 0.125
- gate_up_moment: float32 [2, 2048, 8192], P(None, 'seq', 'tp'), may hold values from -192 to 192
- gate_up_square: float32 [2, 2048, 8192], P(None, 'seq', 'tp'), may hold values from 128 to 4096
- down_weight: float32 [8192, 2048], P('tp', 'seq'), may hold values from -0.0625 to 0.0625
- down_moment: float32 [8192, 2048], P('tp', 'seq'), may hold values from -192 to 192
- down_square: float32 [8192, 2048], P('tp', 'seq'), may hold values from 128 to 4096
- norm_gains: float32 [2, 2048], replicated, may hold values from 0.5 to 1.5
- gains_moment: float32 [2, 2048], replicated, may hold values from -1024 to 1024
- gains_square: float32 [2, 2048], replicated, may hold values from 4096 to 65536
Outputs:
- outputs: bfloat16 [8192, 2048], P(('seq', 'tp'))
- input_grad: float32 [8192, 2048], P(('seq', 'tp'))
- qkv_grad: float32 [2048, 3072], P('seq', 'tp')
- qkv_master: float32 [2048, 3072], P('seq', 'tp')
- qkv_moment_new: float32 [2048, 3072], P('seq', 'tp')
- qkv_square_new: float32 [2048, 3072], P('seq', 'tp')
- qkv_copy: bfloat16 [2048, 3072], P('seq', 'tp')
- out_grad: float32 [2048, 2048], P('tp', 'seq')
- out_update: float32 [2048, 2048], P('tp', 'seq')
- out_moment_new: float32 [2048, 2048], P('tp', 'seq')
- out_square_new: float32 [2048, 2048], P('tp', 'seq')
- gate_up_grad: float32 [2, 2048, 8192], P(None, 'seq', 'tp')
- gate_up_master: float32 [2, 2048, 8192], P(None, 'seq', 'tp')
- gate_up_moment_new: float32 [2, 2048, 8192], P(None, 'seq', 'tp')
- gate_up_square_new: float32 [2, 2048, 8192], P(None, 'seq', 'tp')
- gate_up_copy: bfloat16 [2, 2048, 8192], P(None, 'seq', 'tp')
- down_grad: float32 [8192, 2048], P('tp', 'seq')
- down_master: float32 [8192, 2048], P('tp', 'seq')
- down_moment_new: float32 [8192, 2048], P('tp', 'seq')
- down_square_new: float32 [8192, 2048], P('tp', 'seq')
- down_copy: bfloat16 [8192, 2048], P('tp', 'seq')
- gains_grad: float32 [2, 2048], replicated
- gains_update: float32 [2, 2048], replicated
- gains_moment_new: float32 [2, 2048], replicated
- gains_square_new: float32 [2, 2048], replicated
Inputs may be any that keep to these rules, and one draw needn't show every extreme that they name: `segment_ids`: documents are runs of equal numbers that never fall; each is 1 to 2000 tokens long and lies within one sequence of 4096 tokens; every sequence begins with a document of exactly 2000 tokens. In the k-th sequence the first document has number k * 21 and the last k * 21 + 20. `positions`: each token's position counted from the start of its document.
All inputs are finite; a program needn't handle non-finite values.
Results may differ from a plain program's by a relative error of at most 0.025.
Values may be sent and summed in bfloat16 or wider, within the bound.
No kernel may reach another device: no remote copies, remote signals or barrier semaphores. Data moves between devices by JAX's collectives and lax.ppermute only.
A program may use at most 384 MiB of HBM per device.

v0:
```python
import jax
import jax.numpy as jnp
from jax import lax
from jax.sharding import PartitionSpec as P

HD = 64
QPK = 4
REACH = 2


NORM_EPS = 1e-05
ROPE_BASE = 500000.0
BETA = 0.5
RATE = 0.02
DECAY = 0.1
ADAM_EPS = 1e-08
NEG_FILL = -1e30


def passed_along(block, axis, distance):
    devices = range(lax.axis_size(axis))
    route = [(i - distance, i) for i in devices if i - distance in devices]
    return lax.ppermute(block, axis, route)


def rope_tables(positions):
    half_size = HD // 2
    freq = ROPE_BASE ** (-(jnp.arange(half_size).astype(jnp.float32) * 2.0 / HD))
    angle = positions.astype(jnp.float32)[:, None] * freq[None, :]
    return (jnp.cos(angle), jnp.sin(angle))


def rotate(vector, cos_part, sin_part):
    half_size = vector.shape[-1] // 2
    front_half = vector[..., :half_size]
    back_half = vector[..., half_size:]
    return jnp.concatenate(
        [
            front_half * cos_part - back_half * sin_part,
            back_half * cos_part + front_half * sin_part,
        ],
        axis=-1,
    )


def unrotate(vector, cos_part, sin_part):
    half_size = vector.shape[-1] // 2
    front_half = vector[..., :half_size]
    back_half = vector[..., half_size:]
    return jnp.concatenate(
        [
            front_half * cos_part + back_half * sin_part,
            back_half * cos_part - front_half * sin_part,
        ],
        axis=-1,
    )


def score_block(queries, key_vals, key_mask):
    scores = jnp.einsum(
        "tgqd,sgd->gqts", queries, key_vals[:, :, :HD], preferred_element_type=jnp.float32
    ) * HD ** (-0.5)
    return jnp.where(key_mask, scores, NEG_FILL)


def norm_back(vector, inverse, gain, grad_in):
    scaled = grad_in * gain
    grad_out = inverse * scaled - vector * inverse**3 * jnp.mean(
        vector * scaled, axis=1, keepdims=True
    )
    return (grad_out, jnp.sum(grad_in * vector * inverse, axis=0))


def contract_rows(left, right):
    return lax.dot_general(
        left, right, (((0,), (0,)), ((), ())), preferred_element_type=jnp.float32
    )


def contract_cols(left, right):
    return lax.dot_general(
        left, right, (((1,), (1,)), ((), ())), preferred_element_type=jnp.float32
    )


def adam_step(weight_old, grad_new, moment_one, moment_two):
    moment_next = BETA * moment_one + (1.0 - BETA) * grad_new
    square_next = BETA * moment_two + (1.0 - BETA) * grad_new * grad_new
    change = -RATE * (moment_next / (jnp.sqrt(square_next) + ADAM_EPS) + DECAY * weight_old)
    return (weight_old + change, moment_next, square_next, change)


def local(
    layer_input,
    output_grad,
    segment_ids,
    positions,
    qkv_weight,
    qkv_moment,
    qkv_square,
    out_weight,
    out_moment,
    out_square,
    gate_up_weight,
    gate_up_moment,
    gate_up_square,
    down_weight,
    down_moment,
    down_square,
    norm_gains,
    gains_moment,
    gains_square,
):
    low_weights = (
        qkv_weight.astype(jnp.bfloat16),
        out_weight.astype(jnp.bfloat16),
        gate_up_weight.astype(jnp.bfloat16),
        down_weight.astype(jnp.bfloat16),
    )
    w_qkv, w_out, w_gate_up, w_down = (
        lax.all_gather(low_weights[0], "seq", axis=0, tiled=True),
        lax.all_gather(low_weights[1], "seq", axis=1, tiled=True),
        lax.all_gather(low_weights[2], "seq", axis=1, tiled=True),
        lax.all_gather(low_weights[3], "seq", axis=1, tiled=True),
    )
    resid_in = layer_input.astype(jnp.float32)
    gain_one = norm_gains[0]
    gain_two = norm_gains[1]
    inverse_one = lax.rsqrt(jnp.mean(resid_in * resid_in, axis=1, keepdims=True) + NORM_EPS)
    normed_one = (resid_in * inverse_one * gain_one).astype(jnp.bfloat16)
    rows_one = lax.all_gather(normed_one, "tp", axis=0, tiled=True)
    tokens = rows_one.shape[0]
    groups = w_qkv.shape[1] // ((QPK + 2) * HD)
    qkv_mixed = jnp.dot(rows_one, w_qkv, preferred_element_type=jnp.float32).reshape(
        tokens, groups, QPK + 2, HD
    )
    cos_table, sin_table = rope_tables(positions)
    cos_four = cos_table[:, None, None, :]
    sin_four = sin_table[:, None, None, :]
    cos_three = cos_table[:, None, :]
    sin_three = sin_table[:, None, :]
    queries = rotate(qkv_mixed[:, :, :QPK], cos_four, sin_four).astype(jnp.bfloat16)
    key_rows = rotate(qkv_mixed[:, :, QPK], cos_three, sin_three).astype(jnp.bfloat16)
    value_rows = qkv_mixed[:, :, QPK + 1].astype(jnp.bfloat16)
    key_vals = jnp.concatenate([key_rows, value_rows], axis=2)
    token_index = jnp.arange(tokens)
    local_mask = (segment_ids[:, None] == segment_ids[None, :]) & (
        token_index[None, :] <= token_index[:, None]
    )
    sources = [(key_vals, local_mask)]
    for offset_back in range(1, REACH + 1):
        far_vals, far_segments = passed_along((key_vals, segment_ids), "seq", offset_back)
        far_mask = (segment_ids[:, None] == far_segments[None, :]) & (
            lax.axis_index("seq") >= offset_back
        )
        sources.append((far_vals, far_mask))
    run_max = jnp.full((groups, QPK, tokens), NEG_FILL, jnp.float32)
    run_sum = jnp.zeros((groups, QPK, tokens), jnp.float32)
    for source_vals, source_mask in sources:
        scores = score_block(queries, source_vals, source_mask)
        next_max = jnp.maximum(run_max, jnp.max(scores, axis=3))
        run_sum = run_sum * jnp.exp(run_max - next_max) + jnp.sum(
            jnp.exp(scores - next_max[..., None]), axis=3
        )
        run_max = next_max
    log_total = run_max + jnp.log(run_sum)
    attn_sum = jnp.zeros((groups, QPK, tokens, HD), jnp.float32)
    for source_vals, source_mask in sources:
        soft_probs = jnp.exp(score_block(queries, source_vals, source_mask) - log_total[..., None])
        attn_sum = attn_sum + jnp.einsum(
            "gqts,sgd->gqtd",
            soft_probs.astype(jnp.bfloat16),
            source_vals[:, :, HD:],
            preferred_element_type=jnp.float32,
        )
    attn_in = attn_sum.transpose(2, 0, 1, 3).astype(jnp.bfloat16).reshape(tokens, groups * QPK * HD)
    resid_mid = resid_in + lax.psum_scatter(
        jnp.dot(attn_in, w_out, preferred_element_type=jnp.float32).astype(jnp.bfloat16),
        "tp",
        scatter_dimension=0,
        tiled=True,
    ).astype(jnp.float32)
    inverse_two = lax.rsqrt(jnp.mean(resid_mid * resid_mid, axis=1, keepdims=True) + NORM_EPS)
    normed_two = (resid_mid * inverse_two * gain_two).astype(jnp.bfloat16)
    rows_two = lax.all_gather(normed_two, "tp", axis=0, tiled=True)
    gate_up = jnp.einsum("td,kdf->ktf", rows_two, w_gate_up, preferred_element_type=jnp.float32)
    gate_pre = gate_up[0]
    up_pre = gate_up[1]
    sigmoid_gate = jax.nn.sigmoid(gate_pre)
    hidden = (gate_pre * sigmoid_gate * up_pre).astype(jnp.bfloat16)
    result = resid_mid + lax.psum_scatter(
        jnp.dot(hidden, w_down, preferred_element_type=jnp.float32).astype(jnp.bfloat16),
        "tp",
        scatter_dimension=0,
        tiled=True,
    ).astype(jnp.float32)
    outputs = result.astype(jnp.bfloat16)
    back_weights = (
        lax.all_gather(low_weights[0], "seq", axis=0, tiled=True),
        lax.all_gather(low_weights[1], "seq", axis=1, tiled=True),
        lax.all_gather(low_weights[2], "seq", axis=1, tiled=True),
        lax.all_gather(low_weights[3], "seq", axis=1, tiled=True),
    )
    back_qkv, back_out, back_gate_up, back_down = back_weights
    grad_rows = lax.all_gather(output_grad, "tp", axis=0, tiled=True)
    d_hidden = contract_cols(grad_rows, back_down).astype(jnp.bfloat16)
    down_grad = contract_rows(hidden, grad_rows)
    d_gate = (d_hidden * up_pre * sigmoid_gate * (1.0 + gate_pre * (1.0 - sigmoid_gate))).astype(
        jnp.bfloat16
    )
    d_up = (d_hidden * gate_pre * sigmoid_gate).astype(jnp.bfloat16)
    d_gate_up = jnp.stack([d_gate, d_up])
    gate_up_grad = jnp.einsum(
        "td,ktf->kdf", rows_two, d_gate_up, preferred_element_type=jnp.float32
    )
    d_normed_two = jnp.einsum(
        "ktf,kdf->td", d_gate_up, back_gate_up, preferred_element_type=jnp.float32
    )
    d_normed_two = lax.psum_scatter(
        d_normed_two.astype(jnp.bfloat16), "tp", scatter_dimension=0, tiled=True
    ).astype(jnp.float32)
    norm_two_grad, gain_two_grad = norm_back(resid_mid, inverse_two, gain_two, d_normed_two)
    d_mid = output_grad.astype(jnp.float32) + norm_two_grad
    branch_rows = lax.all_gather(d_mid.astype(jnp.bfloat16), "tp", axis=0, tiled=True)
    d_attn_in = contract_cols(branch_rows, back_out).astype(jnp.bfloat16)
    out_grad = contract_rows(attn_in, branch_rows)
    d_attn = d_attn_in.reshape(tokens, groups, QPK, HD).transpose(1, 2, 0, 3)
    row_delta = jnp.sum(d_attn.astype(jnp.float32) * attn_sum, axis=3)
    d_query = jnp.zeros((groups, QPK, tokens, HD), jnp.float32)
    key_grads = []
    for source_vals, source_mask in sources:
        soft_probs = jnp.exp(score_block(queries, source_vals, source_mask) - log_total[..., None])
        d_probs = jnp.einsum(
            "gqtd,sgd->gqts", d_attn, source_vals[:, :, HD:], preferred_element_type=jnp.float32
        )
        d_scores = (soft_probs * (d_probs - row_delta[..., None])).astype(jnp.bfloat16)
        d_query = d_query + jnp.einsum(
            "gqts,sgd->gqtd", d_scores, source_vals[:, :, :HD], preferred_element_type=jnp.float32
        ) * HD ** (-0.5)
        d_keys = jnp.einsum(
            "gqts,tgqd->sgd", d_scores, queries, preferred_element_type=jnp.float32
        ) * HD ** (-0.5)
        d_values = jnp.einsum(
            "gqts,gqtd->sgd",
            soft_probs.astype(jnp.bfloat16),
            d_attn,
            preferred_element_type=jnp.float32,
        )
        key_grads.append(jnp.concatenate([d_keys, d_values], axis=2))
    key_grad_sum = key_grads[0]
    for offset_back in range(1, REACH + 1):
        key_grad_sum = key_grad_sum + passed_along(
            key_grads[offset_back].astype(jnp.bfloat16), "seq", -offset_back
        ).astype(jnp.float32)
    d_query_rows = unrotate(d_query.transpose(2, 0, 1, 3), cos_four, sin_four)
    d_key_rows = unrotate(key_grad_sum[:, :, :HD], cos_three, sin_three)
    d_mixed = jnp.concatenate(
        [d_query_rows, d_key_rows[:, :, None, :], key_grad_sum[:, :, None, HD:]], axis=2
    )
    d_mixed = d_mixed.astype(jnp.bfloat16).reshape(tokens, groups * (QPK + 2) * HD)
    qkv_grad = contract_rows(rows_one, d_mixed)
    d_normed_one = lax.psum_scatter(
        contract_cols(d_mixed, back_qkv).astype(jnp.bfloat16), "tp", scatter_dimension=0, tiled=True
    ).astype(jnp.float32)
    norm_one_grad, gain_one_grad = norm_back(resid_in, inverse_one, gain_one, d_normed_one)
    input_grad = d_mid + norm_one_grad
    gains_grad = lax.psum(jnp.stack([gain_one_grad, gain_two_grad]), ("seq", "tp"))
    qkv_grad, out_grad, gate_up_grad, down_grad = (
        lax.psum_scatter(
            qkv_grad.astype(jnp.bfloat16), "seq", scatter_dimension=0, tiled=True
        ).astype(jnp.float32),
        lax.psum_scatter(
            out_grad.astype(jnp.bfloat16), "seq", scatter_dimension=1, tiled=True
        ).astype(jnp.float32),
        lax.psum_scatter(
            gate_up_grad.astype(jnp.bfloat16), "seq", scatter_dimension=1, tiled=True
        ).astype(jnp.float32),
        lax.psum_scatter(
            down_grad.astype(jnp.bfloat16), "seq", scatter_dimension=1, tiled=True
        ).astype(jnp.float32),
    )
    qkv_new = adam_step(qkv_weight, qkv_grad, qkv_moment, qkv_square)
    out_new = adam_step(out_weight, out_grad, out_moment, out_square)
    gate_up_new = adam_step(gate_up_weight, gate_up_grad, gate_up_moment, gate_up_square)
    down_new = adam_step(down_weight, down_grad, down_moment, down_square)
    gains_new = adam_step(norm_gains, gains_grad, gains_moment, gains_square)
    return (
        outputs,
        input_grad,
        qkv_grad,
        qkv_new[0],
        qkv_new[1],
        qkv_new[2],
        qkv_new[0].astype(jnp.bfloat16),
        out_grad,
        out_new[3],
        out_new[1],
        out_new[2],
        gate_up_grad,
        gate_up_new[0],
        gate_up_new[1],
        gate_up_new[2],
        gate_up_new[0].astype(jnp.bfloat16),
        down_grad,
        down_new[0],
        down_new[1],
        down_new[2],
        down_new[0].astype(jnp.bfloat16),
        gains_grad,
        gains_new[3],
        gains_new[1],
        gains_new[2],
    )


def solution(mesh):
    placed = (
        P(("seq", "tp"), None),
        P(("seq", "tp"), None),
        P("seq"),
        P("seq"),
        P("seq", "tp"),
        P("seq", "tp"),
        P("seq", "tp"),
        P("tp", "seq"),
        P("tp", "seq"),
        P("tp", "seq"),
        P(None, "seq", "tp"),
        P(None, "seq", "tp"),
        P(None, "seq", "tp"),
        P("tp", "seq"),
        P("tp", "seq"),
        P("tp", "seq"),
        P(),
        P(),
        P(),
    )
    return jax.shard_map(
        local,
        mesh=mesh,
        in_specs=placed,
        out_specs=(
            P(("seq", "tp"), None),
            P(("seq", "tp"), None),
            P("seq", "tp"),
            P("seq", "tp"),
            P("seq", "tp"),
            P("seq", "tp"),
            P("seq", "tp"),
            P("tp", "seq"),
            P("tp", "seq"),
            P("tp", "seq"),
            P("tp", "seq"),
            P(None, "seq", "tp"),
            P(None, "seq", "tp"),
            P(None, "seq", "tp"),
            P(None, "seq", "tp"),
            P(None, "seq", "tp"),
            P("tp", "seq"),
            P("tp", "seq"),
            P("tp", "seq"),
            P("tp", "seq"),
            P("tp", "seq"),
            P(),
            P(),
            P(),
            P(),
        ),
        check_vma=False,
    )
```

profile of v0, /device:TPU:10, one launch (start us, length us, event | category | flops | bytes accessed | tf_op | source)
XLA Modules:
  0.0 1446.6 jit_solution(14403504281341215731)
XLA Ops:
  25.8 18.2 %all-gather.11.cloned.1.call-done = bf16[2048,768]{1,0:T(8,128)(2,1)} async-done(((bf16[256,768]{1,0:T(8,128)(2,1)}), bf16[2048,768]{1,0:T(8,128)(2,1)}) %all-gather.11.cloned.1.call-update) | async-done | bytes 3145744 | tf_op jit(solution)/shard_map/all_gather | solution.py:121
  44.0 80.5 %all-gather.9.cloned.1.call-done = bf16[1024,2048]{1,0:T(8,128)(2,1)} async-done(((bf16[256,2048]{1,0:T(8,128)(2,1)}), bf16[1024,2048]{1,0:T(8,128)(2,1)}) %all-gather.9.cloned.1.call-update) | async-done | bytes 4194320 | tf_op jit(solution)/shard_map/all_gather | solution.py:131
  192.9 23.8 %exponential_reduce_fusion = (f32[2,4,1024]{2,1,0:T(4,128)S(1)}, f32[2,4,1024]{2,1,0:T(4,128)S(1)}) fusion(f32[2,1024,1024,4]{2,1,3,0:T(8,128)} %get-tuple-element.103, f32[2,4,1024]{2,1,0:T(4,128)S(1)} %get-tuple-element.75, pred[1024,1024]{0,1:T(8,128)(4,1)S(1)} %get-tuple-element.96, f32[2,4,1024]{2,1,0:T(4,128)S(1)} %get-tuple-element.76, ...), kind=kLoop, calls=%fused_computation.9 | loop fusion | flops 67092480 | bytes 69337088 | tf_op jit(solution)/shard_map/reduce_sum | solution.py:162
  216.7 16.3 %fusion.53 = f32[2,4,1024,64]{2,3,1,0:T(8,128)} fusion(f32[1024,2,6,64]{0,3,2,1:T(8,128)S(1)} %bitcast.234, f32[2,1024,1024,4]{2,1,3,0:T(8,128)} %get-tuple-element.107, f32[2,4,1024]{2,1,0:T(4,128)S(1)} %log_add_fusion, pred[1024,1024]{0,1:T(8,128)(4,1)S(1)} %get-tuple-element.95), kind=kOutput, calls=%fused_computation.138 | convolution fusion | flops 1107296256 | bytes 36995072 | tf_op jit(solution)/shard_map/gqts,sgd->gqtd/dot_general | solution.py:170
  233.1 16.2 %fusion.58 = f32[2,4,1024,64]{2,3,1,0:T(8,128)} fusion(bf16[1024,2,128]{0,2,1:T(8,128)(2,1)S(1)} %copy-done.39, f32[2,1024,1024,4]{2,1,3,0:T(8,128)} %get-tuple-element.105, f32[2,4,1024]{2,1,0:T(4,128)S(1)} %log_add_fusion, pred[1024,1024]{0,1:T(8,128)(4,1)S(1)} %get-tuple-element.97), kind=kOutput, calls=%fused_computation.147 | convolution fusion | flops 1107296256 | bytes 36995072 | tf_op jit(solution)/shard_map/gqts,sgd->gqtd/dot_general | solution.py:170
  249.2 18.0 %fusion.86 = (bf16[2,4,1024,64]{2,3,1,0:T(8,128)(2,1)S(1)}, f32[2,4,1024,64]{2,3,1,0:T(8,128)}) fusion(f32[2,1024,1024,4]{2,1,3,0:T(8,128)} %get-tuple-element.103, f32[2,4,1024]{2,1,0:T(4,128)S(1)} %log_add_fusion, pred[1024,1024]{0,1:T(8,128)(4,1)S(1)} %get-tuple-element.96, bf16[1024,2,128]{0,2,1:T(8,128)(2,1)S(1)} %copy-done.35, ...), kind=kOutput, calls=%fused_computation.178 | convolution fusion | flops 1108869120 | bytes 42237952 | tf_op jit(solution)/shard_map/gqts,sgd->gqtd/dot_general | solution.py:170
  274.3 77.6 %reduce-scatter.9.cloned.1.call-done = bf16[256,2048]{1,0:T(8,128)(2,1)} async-done(((bf16[1024,2048]{1,0:T(8,128)(2,1)}), bf16[256,2048]{1,0:T(8,128)(2,1)}) %reduce-scatter.9.cloned.1.call-update) | async-done | bytes 1048592 | tf_op jit(solution)/shard_map/reduce_scatter | solution.py:177
  362.2 73.0 %all-gather.15.cloned.1.call-done = bf16[1024,2048]{1,0:T(8,128)(2,1)} async-done(((bf16[256,2048]{1,0:T(8,128)(2,1)}), bf16[1024,2048]{1,0:T(8,128)(2,1)}) %all-gather.15.cloned.1.call-update) | async-done | bytes 4194320 | tf_op jit(solution)/shard_map/all_gather | solution.py:185
  435.2 93.4 %all-gather.17.cloned.1.call-done = bf16[2,2048,2048]{2,1,0:T(8,128)(2,1)} async-done(((bf16[2,256,2048]{2,1,0:T(8,128)(2,1)}), bf16[2,2048,2048]{2,1,0:T(8,128)(2,1)}) %all-gather.17.cloned.1.call-update) | async-done | bytes 16777232 | tf_op jit(solution)/shard_map/all_gather | solution.py:123
  528.6 23.6 %convolution_bitcast_fusion = f32[2,1024,2048]{2,1,0:T(8,128)} fusion(bf16[2,2048,2048]{2,1,0:T(8,128)(2,1)} %all-gather.17.cloned.1.call-done, bf16[1024,2048]{1,0:T(8,128)(2,1)} %all-gather.15.cloned.1.call-done), kind=kOutput, calls=%fused_computation.33 | convolution fusion | flops 17179869184 | bytes 37748736 | tf_op jit(solution)/shard_map/td,kdf->ktf/dot_general | solution.py:186
  552.2 56.4 %all-gather.21.cloned.1.call-done = bf16[1024,2048]{1,0:T(8,128)(2,1)} async-done(((bf16[256,2048]{1,0:T(8,128)(2,1)}), bf16[1024,2048]{1,0:T(8,128)(2,1)}) %all-gather.21.cloned.1.call-update) | async-done | bytes 4194320 | tf_op jit(solution)/shard_map/all_gather | solution.py:205
  608.6 59.5 %all-gather.19.cloned.1.call-done = bf16[2048,2048]{1,0:T(8,128)(2,1)} async-done(((bf16[2048,256]{1,0:T(8,128)(2,1)}), bf16[2048,2048]{1,0:T(8,128)(2,1)}) %all-gather.19.cloned.1.call-update) | async-done | bytes 8388624 | tf_op jit(solution)/shard_map/all_gather | solution.py:124
  668.2 21.8 %fusion.17 = (bf16[1,1024,2048]{2,1,0:T(8,128)(2,1)}, bf16[1,1024,2048]{2,1,0:T(8,128)(2,1)}, bf16[1024,2048]{1,0:T(8,128)(2,1)}) fusion(f32[2,1024,2048]{2,1,0:T(8,128)} %convolution_bitcast_fusion, bf16[1024,2048]{1,0:T(8,128)(2,1)} %all-gather.21.cloned.1.call-done, bf16[2048,2048]{1,0:T(8,128)(2,1)} %all-gather.19.cloned.1.call-done), kind=kOutput, calls=%fused_computation.52 | convolution fusion | flops 8627683328 | bytes 41943040 | tf_op jit(solution)/shard_map/dot_general | solution.py:81
  690.0 23.8 %bitcast_convert_fusion = bf16[1024,2048]{1,0:T(8,128)(2,1)} fusion(bf16[2,2048,2048]{2,1,0:T(8,128)(2,1)} %all-gather.17.cloned.1.call-done, bf16[1,1024,2048]{2,1,0:T(8,128)(2,1)} %get-tuple-element.78, bf16[1,1024,2048]{2,1,0:T(8,128)(2,1)} %get-tuple-element.77), kind=kOutput, calls=%fused_computation.29 | convolution fusion | flops 17186160640 | bytes 29360128 | tf_op jit(solution)/shard_map/ktf,kdf->td/dot_general | solution.py:216
  714.1 76.7 %reduce-scatter.13.cloned.1.call-done = bf16[256,2048]{1,0:T(8,128)(2,1)} async-done(((bf16[1024,2048]{1,0:T(8,128)(2,1)}), bf16[256,2048]{1,0:T(8,128)(2,1)}) %reduce-scatter.13.cloned.1.call-update) | async-done | bytes 1048592 | tf_op jit(solution)/shard_map/reduce_scatter | solution.py:219
  810.6 64.9 %all-gather.23.cloned.1.call-done = bf16[1024,2048]{1,0:T(8,128)(2,1)} async-done(((bf16[256,2048]{1,0:T(8,128)(2,1)}), bf16[1024,2048]{1,0:T(8,128)(2,1)}) %all-gather.23.cloned.1.call-update) | async-done | bytes 4194320 | tf_op jit(solution)/shard_map/all_gather | solution.py:224
  882.4 21.9 %multiply_convert_fusion = bf16[2,4,1024,1024]{2,3,1,0:T(8,128)(2,1)} fusion(f32[2,1024,1024,4]{2,1,3,0:T(8,128)} %get-tuple-element.103, bf16[2,4,1024,64]{2,3,1,0:T(8,128)(2,1)S(1)} %bitcast.249, f32[2,4,1024]{2,1,0:T(4,128)S(1)} %get-tuple-element.110, f32[2,4,1024]{2,1,0:T(4,128)S(1)} %log_add_fusion, pred[1024,1024]{0,1:T(8,128)(4,1)S(1)} %copy-done.19, ...), kind=kOutput, calls=%fused_computation.3 | convolution fusion | flops 1124073472 | bytes 52756480 | tf_op jit(solution)/shard_map/gqtd,sgd->gqts/dot_general | solution.py:233
  904.2 16.4 %fusion.46 = bf16[1024,2,64]{0,2,1:T(8,128)(2,1)S(1)} fusion(bf16[2,4,1024,64]{2,3,1,0:T(8,128)(2,1)} %bitcast.250, f32[2,1024,1024,4]{2,1,3,0:T(8,128)} %get-tuple-element.103, f32[2,4,1024]{2,1,0:T(4,128)} %copy-done.47, pred[1024,1024]{0,1:T(8,128)(4,1)S(1)} %copy-done.19), kind=kOutput, calls=%fused_computation.107 | convolution fusion | flops 1107427328 | bytes 35946496 | tf_op jit(solution)/shard_map/gqts,gqtd->sgd/dot_general | solution.py:243
  934.9 21.3 %multiply_convert_fusion.1 = bf16[2,4,1024,1024]{2,3,1,0:T(8,128)(2,1)} fusion(f32[2,1024,1024,4]{2,1,3,0:T(8,128)} %get-tuple-element.105, bf16[2,4,1024,64]{2,3,1,0:T(8,128)(2,1)} %bitcast.251, f32[2,4,1024]{2,1,0:T(4,128)S(1)} %get-tuple-element.110, f32[2,4,1024]{2,1,0:T(4,128)S(1)} %copy-done.48, pred[1024,1024]{0,1:T(8,128)(4,1)S(1)} %copy-done.17, ...), kind=kOutput, calls=%fused_computation.4 | convolution fusion | flops 1124073472 | bytes 52756480 | tf_op jit(solution)/shard_map/gqtd,sgd->gqts/dot_general | solution.py:233
  1094.4 24.7 %convert_bitcast_fusion = bf16[2,2048,2048]{1,2,0:T(8,128)(2,1)} fusion(bf16[1,1024,2048]{2,1,0:T(8,128)(2,1)} %get-tuple-element.78, bf16[1,1024,2048]{2,1,0:T(8,128)(2,1)} %get-tuple-element.77, bf16[1024,2048]{1,0:T(8,128)(2,1)} %all-gather.15.cloned.1.call-done), kind=kOutput, calls=%fused_computation.18 | convolution fusion | flops 17192452096 | bytes 29360128 | tf_op jit(solution)/shard_map/td,ktf->kdf/dot_general | solution.py:213
  1149.1 56.4 %reduce-scatter.15.cloned.1.call-done = bf16[256,2048]{1,0:T(8,128)(2,1)} async-done(((bf16[1024,2048]{1,0:T(8,128)(2,1)}), bf16[256,2048]{1,0:T(8,128)(2,1)}) %reduce-scatter.15.cloned.1.call-update) | async-done | bytes 1048592 | tf_op jit(solution)/shard_map/reduce_scatter | solution.py:262
  1207.5 46.4 %psum.7 = f32[2,2048]{1,0:T(2,128)S(1)} all-reduce(f32[2,2048]{1,0:T(2,128)S(1)} %pad_maximum_fusion.10), channel_id=1, replica_groups=mesh['seq'=8,'tp'=4] {'seq','tp'}, use_global_device_ids=true, to_apply=%region_21.22 | all-reduce | flops 4096 | bytes 32768 | tf_op jit(solution)/shard_map/psum | solution.py:267
  1254.5 31.5 %reduce-scatter.11.cloned.1.call-done = bf16[256,2048]{1,0:T(8,128)(2,1)} async-done(((bf16[1024,2048]{1,0:T(8,128)(2,1)}), bf16[256,2048]{1,0:T(8,128)(2,1)}) %reduce-scatter.11.cloned.1.call-update) | async-done | bytes 1048592 | tf_op jit(solution)/shard_map/reduce_scatter | solution.py:191
  1291.2 115.0 %reduce-scatter.21.cloned.1.call-done = bf16[2,256,2048]{1,2,0:T(8,128)(2,1)} async-done(((bf16[2,2048,2048]{1,2,0:T(8,128)(2,1)}), bf16[2,256,2048]{1,2,0:T(8,128)(2,1)}) %reduce-scatter.21.cloned.1.call-update) | async-done | bytes 2097168 | tf_op jit(solution)/shard_map/reduce_scatter | solution.py:275
  (249 shorter events, 354.2 us)
Async XLA Ops:
  7.2 36.8 %all-gather.11.cloned.1.call-start = ((), (), s32[]{:S(2)}) async-start(), calls=%async_computation.9 | async-start | bytes 3538944 | tf_op jit(solution)/shard_map/all_gather | solution.py:121
  9.3 115.2 %all-gather.9.cloned.1.call-start = ((), (), s32[]{:S(2)}) async-start(), calls=%async_computation.8 | async-start | bytes 5242880 | tf_op jit(solution)/shard_map/all_gather | solution.py:131
  12.2 781.1 %copy-start.32 = (f32[1,2048]{1,0:T(1,128)}, f32[1,2048]{1,0:T(1,128)S(1)}, u32[]{:S(2)}) copy-start(f32[1,2048]{1,0:T(1,128)S(1)} %get-tuple-element.91) | copy-start | bytes 24580
  14.7 252.6 %all-gather.13.cloned.1.call-start = ((), (), s32[]{:S(2)}) async-start(), calls=%async_computation.10 | async-start | bytes 2359296 | tf_op jit(solution)/shard_map/all_gather | solution.py:122
  14.8 6.8 collective-permute-start.2
  18.2 5.0 collective-permute-start
  20.9 331.1 %reduce-scatter.9.cloned.1.call-start = ((), (), s32[]{:S(2)}) async-start(), calls=%async_computation.11 | async-start | bytes 5242880 | tf_op jit(solution)/shard_map/reduce_scatter | solution.py:177
  131.4 19.9 %collective-permute-start.3 = (bf16[1024,2,128]{0,2,1:T(8,128)(2,1)S(1)}, bf16[1024,2,128]{0,2,1:T(8,128)(2,1)S(1)}, u32[]{:S(2)}, u32[]{:S(2)}) collective-permute-start(bf16[1024,2,128]{0,2,1:T(8,128)(2,1)S(1)} %pad_maximum_fusion.7), channel_id=1, source_target_pairs={{0,8},{4,12},{8,16},{12,20},{16,24},{20,28},{1,9},{5,13},{9,17},{1... | collective-permute-start | bytes 1572872 | tf_op jit(solution)/shard_map/ppermute | solution.py:23
  134.7 30.2 %collective-permute-start.1 = (bf16[1024,2,128]{0,2,1:T(8,128)(2,1)S(1)}, bf16[1024,2,128]{0,2,1:T(8,128)(2,1)S(1)}, u32[]{:S(2)}, u32[]{:S(2)}) collective-permute-start(bf16[1024,2,128]{0,2,1:T(8,128)(2,1)S(1)} %pad_maximum_fusion.7), channel_id=1, source_target_pairs={{0,4},{4,8},{8,12},{12,16},{16,20},{20,24},{24,28},{1,5},{5,9},{9,... | collective-permute-start | bytes 1572872 | tf_op jit(solution)/shard_map/ppermute | solution.py:23
  216.7 664.7 %copy-start.47 = (f32[2,4,1024]{2,1,0:T(4,128)}, f32[2,4,1024]{2,1,0:T(4,128)S(1)}, u32[]{:S(2)}) copy-start(f32[2,4,1024]{2,1,0:T(4,128)S(1)} %log_add_fusion) | copy-start | bytes 98308
  274.3 160.9 %all-gather.15.cloned.1.call-start = ((), (), s32[]{:S(2)}) async-start(), calls=%async_computation.12 | async-start | bytes 5242880 | tf_op jit(solution)/shard_map/all_gather | solution.py:185
  356.2 172.3 %all-gather.17.cloned.1.call-start = ((), (), s32[]{:S(2)}) async-start(), calls=%async_computation.13 | async-start | bytes 18874368 | tf_op jit(solution)/shard_map/all_gather | solution.py:123
  360.3 248.3 %all-gather.21.cloned.1.call-start = ((), (), s32[]{:S(2)}) async-start(), calls=%async_computation.16 | async-start | bytes 5242880 | tf_op jit(solution)/shard_map/all_gather | solution.py:205
  361.0 307.1 %all-gather.19.cloned.1.call-start = ((), (), s32[]{:S(2)}) async-start(), calls=%async_computation.14 | async-start | bytes 9437184 | tf_op jit(solution)/shard_map/all_gather | solution.py:124
  362.2 428.6 %reduce-scatter.13.cloned.1.call-start = ((), (), s32[]{:S(2)}) async-start(), calls=%async_computation.17 | async-start | bytes 5242880 | tf_op jit(solution)/shard_map/reduce_scatter | solution.py:219
  713.8 161.6 %all-gather.23.cloned.1.call-start = ((), (), s32[]{:S(2)}) async-start(), calls=%async_computation.18 | async-start | bytes 5242880 | tf_op jit(solution)/shard_map/all_gather | solution.py:224
  796.4 339.2 %reduce-scatter.23.cloned.1.call-start = ((), (), s32[]{:S(2)}) async-start(), calls=%async_computation.23 | async-start | bytes 9437184 | tf_op jit(solution)/shard_map/reduce_scatter | solution.py:278
  810.5 332.0 %reduce-scatter.19.cloned.1.call-start = ((), (), s32[]{:S(2)}) async-start(), calls=%async_computation.21 | async-start | bytes 2359296 | tf_op jit(solution)/shard_map/reduce_scatter | solution.py:272
  932.8 132.6 %collective-permute-start.5 = (bf16[1024,2,128]{0,2,1:T(8,128)(2,1)}, bf16[1024,2,128]{0,2,1:T(8,128)(2,1)}, u32[]{:S(2)}, u32[]{:S(2)}) collective-permute-start(bf16[1024,2,128]{0,2,1:T(8,128)(2,1)} %pad_maximum_fusion.9), channel_id=1, source_target_pairs={{8,0},{12,4},{16,8},{20,12},{24,16},{28,20},{9,1},{13,5},{17,9},{2... | collective-permute-start | bytes 1572872 | tf_op jit(solution)/shard_map/ppermute | solution.py:23
  983.1 82.3 %collective-permute-start.4 = (bf16[1024,2,128]{0,2,1:T(8,128)(2,1)}, bf16[1024,2,128]{0,2,1:T(8,128)(2,1)}, u32[]{:S(2)}, u32[]{:S(2)}) collective-permute-start(bf16[1024,2,128]{0,2,1:T(8,128)(2,1)} %pad_maximum_fusion.8), channel_id=1, source_target_pairs={{4,0},{8,4},{12,8},{16,12},{20,16},{24,20},{28,24},{5,1},{9,5},{13... | collective-permute-start | bytes 1572872 | tf_op jit(solution)/shard_map/ppermute | solution.py:23
  1032.3 113.0 %reduce-scatter.17.cloned.1.call-start = ((), (), s32[]{:S(2)}) async-start(), calls=%async_computation.20 | async-start | bytes 3538944 | tf_op jit(solution)/shard_map/reduce_scatter | solution.py:269
  1073.2 132.4 %reduce-scatter.15.cloned.1.call-start = ((), (), s32[]{:S(2)}) async-start(), calls=%async_computation.19 | async-start | bytes 5242880 | tf_op jit(solution)/shard_map/reduce_scatter | solution.py:262
  1080.4 205.6 %reduce-scatter.11.cloned.1.call-start = ((), (), s32[]{:S(2)}) async-start(), calls=%async_computation.15 | async-start | bytes 5242880 | tf_op jit(solution)/shard_map/reduce_scatter | solution.py:191
  1094.4 311.9 %reduce-scatter.21.cloned.1.call-start = ((), (), s32[]{:S(2)}) async-start(), calls=%async_computation.22 | async-start | bytes 18874368 | tf_op jit(solution)/shard_map/reduce_scatter | solution.py:275
  (63 other events, 4088.6 us)
Sparse Core Ops, SparseCore 0:
  10.5 33.4 all-gather.10
  46.2 78.3 all-gather.8
  127.0 33.7 all-gather.12
  274.4 77.5 reduce-scatter.8
  356.4 78.8 all-gather.14
  437.7 90.8 all-gather.16
  530.2 78.3 all-gather.20
  611.2 56.8 all-gather.18
  714.0 76.7 reduce-scatter.12
  796.5 78.8 all-gather.22
  878.9 82.8 reduce-scatter.22
  1032.4 43.7 reduce-scatter.18
  1079.6 46.2 reduce-scatter.16
  1128.7 76.7 reduce-scatter.14
  1207.7 78.3 reduce-scatter.10
  1289.9 116.3 reduce-scatter.20
where the time goes:
time: 1450 us
  waiting for transfers between devices  806 us (56%)
  matrix products  414 us (29%)
  other arithmetic  99.6 us (7%)
  local copies, waits for them, and re-layouts  48.9 us (3%)
  blocking collectives  46.4 us (3%)
  starting transfers between devices  16.4 us (1%)
  between operations  15.2 us (1%)
    reduce_scatter x1, waiting for transfers between devices, local(): lax.psum_scatter(gate_up_grad.astype(jnp.bfloat16), 'seq', scatter_dimens...  115 us
    all_gather x1, waiting for transfers between devices, local(): lax.all_gather(low_weights[2], 'seq', axis=1, tiled=True)  93.4 us
    all_gather x1, waiting for transfers between devices, local(): rows_one = lax.all_gather(normed_one, 'tp', axis=0, tiled=True)  80.5 us
    reduce_scatter x1, waiting for transfers between devices, local(): lax.psum_scatter(jnp.dot(attn_in, w_out, preferred_element_type=jnp.float...  77.6 us
    reduce_scatter x1, waiting for transfers between devices, local(): lax.psum_scatter(d_normed_two.astype(jnp.bfloat16), 'tp', scatter_dimensi...  76.7 us
    all_gather x1, waiting for transfers between devices, local(): rows_two = lax.all_gather(normed_two, 'tp', axis=0, tiled=True)  73 us
    all_gather x1, waiting for transfers between devices, local(): lax.all_gather(d_mid.astype(jnp.bfloat16), 'tp', axis=0, tiled=True)  64.9 us
    all_gather x1, waiting for transfers between devices, local(): lax.all_gather(low_weights[3], 'seq', axis=1, tiled=True)  59.5 us
  transfers between devices with their start and end apart: 22, of which 14 were waited for; matrix products, arithmetic and copies ran while one was open for 32% of the time, Pallas kernels for 0%

commit v1 on v0

v1 whole, which is shorter than its diff:
```python
import functools

import jax
import jax.numpy as jnp
from jax import lax
from jax.experimental import pallas as pl
from jax.experimental.pallas import tpu as pltpu
from jax.sharding import PartitionSpec as P

HD = 64
QPK = 4
REACH = 2
SEQLEN = 4096

NORM_EPS = 1e-05
ROPE_BASE = 500000.0
BETA = 0.5
RATE = 0.02
DECAY = 0.1
ADAM_EPS = 1e-08
NEG_FILL = -1e30
LOG2E = 1.4426950408889634
EXP_SCALE = HD**-0.5 * LOG2E
VMEM_LIMIT = 48 * 2**20

ROWS_BY_ROWS = (((0,), (0,)), ((), ()))
COLS_BY_COLS = (((1,), (1,)), ((), ()))


def cost(micros):
    return pl.CostEstimate(
        flops=int(micros * 1.15e9), transcendentals=0, bytes_accessed=int(micros * 3.0e6)
    )


def after(block, *others):
    return lax.optimization_barrier((block, *others))[0]


def contract_rows(left, right):
    return lax.dot_general(left, right, ROWS_BY_ROWS, preferred_element_type=jnp.float32)


def contract_cols(left, right):
    return lax.dot_general(left, right, COLS_BY_COLS, preferred_element_type=jnp.float32)


def shifted(block, axis, distance):
    size = lax.axis_size(axis)
    return lax.ppermute(
        block, axis, [(i, i + distance) for i in range(size) if 0 <= i + distance < size]
    )


class LineGather:
    def __init__(self, block, axis):
        self.axis = axis
        self.hops = lax.axis_size(axis) - 1
        self.from_low = [block]
        self.from_high = [block]

    @property
    def step(self):
        return len(self.from_low) - 1

    def hop(self):
        self.from_low.append(shifted(self.from_low[-1], self.axis, 1))
        self.from_high.append(shifted(self.from_high[-1], self.axis, -1))

    @property
    def moving(self):
        return self.from_low[-1], self.from_high[-1]

    @moving.setter
    def moving(self, pair):
        self.from_low[-1], self.from_high[-1] = pair

    @property
    def pieces(self):
        return [*self.from_low, *self.from_high[1:]]


def send_order(size):
    return [sorted(range(size), key=lambda peer: (-abs(peer - me), peer)) for me in range(size)]


def peers_of(axis):
    size = lax.axis_size(axis)
    return jnp.array(send_order(size), jnp.int32)[lax.axis_index(axis)]


class LineScatter:
    def __init__(self, made, axis):
        self.axis = axis
        self.hops = lax.axis_size(axis) - 1
        self.made = list(made)
        self.step = 0
        self.moving = None

    def addend(self, distance):
        order = send_order(self.hops + 1)
        slots = [
            order[me].index(me + distance) if 0 <= me + distance <= self.hops else None
            for me in range(self.hops + 1)
        ]
        choices = sorted(set(slots) - {None})
        table = jnp.array([choices[0] if slot is None else slot for slot in slots], jnp.int32)
        block = self.made[choices[0]]
        for choice in choices[1:]:
            chosen = table[lax.axis_index(self.axis)] == choice
            block = jnp.where(chosen, self.made[choice], block)
        return block

    def hop(self):
        self.step += 1
        size, step = self.hops + 1, self.step
        to_high = self.addend(size - step)
        to_low = self.addend(step - size)
        if step > 1:
            to_high = to_high + self.moving[0]
            to_low = to_low + self.moving[1]
        self.moving = (
            lax.ppermute(to_high, self.axis, [(i, i + 1) for i in range(step)]),
            lax.ppermute(to_low, self.axis, [(i, i - 1) for i in range(size - step, size)]),
        )

    @property
    def parts(self):
        return [self.made[-1], *self.moving]


def swap_gather(block, axis):
    copies = jnp.broadcast_to(block[None], (lax.axis_size(axis), *block.shape))
    return lax.all_to_all(copies, axis, split_axis=0, concat_axis=0, tiled=True)


def swap_scatter_parts(block, axis):
    size = lax.axis_size(axis)
    parts = block.reshape(size, block.shape[0] // size, block.shape[1])
    return lax.all_to_all(parts, axis, split_axis=0, concat_axis=0, tiled=True)


def sum_parts(parts):
    return jnp.sum(parts.astype(jnp.float32), axis=0)


def halving_hop(blocks, axis, hop):
    rank = lax.axis_index(axis)
    pairs = blocks.reshape(blocks.shape[0] // 2, 2, *blocks.shape[1:])
    mine = (rank // hop) % 2
    keep = lax.dynamic_index_in_dim(pairs, mine, axis=1, keepdims=False)
    send = lax.dynamic_index_in_dim(pairs, 1 - mine, axis=1, keepdims=False)
    came = lax.ppermute(send, axis, [(i, i ^ hop) for i in range(lax.axis_size(axis))])
    return (keep.astype(jnp.float32) + came.astype(jnp.float32)).astype(blocks.dtype)


def sum_everywhere(block, axes):
    for axis in axes:
        size = lax.axis_size(axis)
        hop = 1
        while hop < size:
            block = block + lax.ppermute(block, axis, [(i, i ^ hop) for i in range(size)])
            hop *= 2
    return block


def along_sequence(block, distance, tokens):
    shards = SEQLEN // tokens
    route = [
        (i, i + distance)
        for i in range(lax.axis_size("seq"))
        if 0 <= i + distance < lax.axis_size("seq") and i // shards == (i + distance) // shards
    ]
    return lax.ppermute(block, "seq", route)


def turn_halves(block):
    lane = lax.broadcasted_iota(jnp.int32, block.shape, 1)
    return jnp.where(lane % HD < HD // 2, pltpu.roll(block, 96, 1), pltpu.roll(block, 32, 1))


def pick_piece(pieces, below, put):
    size = (len(pieces) + 1) // 2
    for distance in range(1 - size, size):
        piece = pieces[distance if distance >= 0 else size - 1 - distance]
        pl.when(below == distance)(functools.partial(put, piece))


def place_kernel(rank_ref, *refs):
    *pieces, out_ref = refs

    def put(piece):
        out_ref[...] = piece[...]

    pick_piece(pieces, rank_ref[0] - pl.program_id(0), put)


def place_rows(pieces, rank):
    own, width = pieces[0].shape
    size = (len(pieces) + 1) // 2
    return pl.pallas_call(
        place_kernel,
        grid_spec=pltpu.PrefetchScalarGridSpec(
            num_scalar_prefetch=1,
            grid=(size,),
            in_specs=[pl.BlockSpec((own, width), lambda i, r: (0, 0))] * len(pieces),
            out_specs=pl.BlockSpec((own, width), lambda i, r: (i, 0)),
        ),
        out_shape=jax.ShapeDtypeStruct((own * size, width), pieces[0].dtype),
        compiler_params=pltpu.CompilerParams(vmem_limit_bytes=VMEM_LIMIT),
        cost_estimate=cost(4),
        name="place_rows",
    )(jnp.reshape(rank, (1,)).astype(jnp.int32), *pieces)


def qkv_kernel(rank_ref, w_ref, gain_ref, cos_ref, sin_ref, *refs):
    x_ref, normed_ref, q_ref, kv_ref = refs[-4:]

    def put(piece):
        x_ref[...] = piece[...]

    pick_piece(refs[:-4], rank_ref[0] - pl.program_id(0), put)
    x = x_ref[...].astype(jnp.float32)
    inverse = lax.rsqrt(jnp.mean(x * x, axis=1, keepdims=True) + NORM_EPS)
    normed = (x * inverse * gain_ref[...]).astype(jnp.bfloat16)
    normed_ref[...] = normed
    mixed = jnp.dot(normed, w_ref[...], preferred_element_type=jnp.float32)
    cos, sin = cos_ref[...], sin_ref[...]
    key_lane = lax.broadcasted_iota(jnp.int32, cos.shape, 1) < HD
    for group in range(mixed.shape[1] // ((QPK + 2) * HD)):
        base = group * (QPK + 2) * HD
        for pair in range(QPK // 2):
            part = mixed[:, base + pair * 128 : base + (pair + 1) * 128]
            part = part * cos + turn_halves(part) * sin
            q_ref[:, group * QPK * HD + pair * 128 : group * QPK * HD + (pair + 1) * 128] = (
                part.astype(jnp.bfloat16)
            )
        part = mixed[:, base + QPK * HD : base + (QPK + 2) * HD]
        part = jnp.where(key_lane, part * cos + turn_halves(part) * sin, part)
        kv_ref[:, group * 128 : (group + 1) * 128] = part.astype(jnp.bfloat16)


def project_qkv(pieces, rank, weight, gain, cos, sin):
    own, width = pieces[0].shape
    size = (len(pieces) + 1) // 2
    tokens = own * size
    groups = weight.shape[1] // ((QPK + 2) * HD)

    def rows(wide):
        return pl.BlockSpec((own, wide), lambda i, r: (i, 0))

    def whole(shape):
        return pl.BlockSpec(shape, lambda i, r: (0, 0))

    widths = (width, width, groups * QPK * HD, groups * 2 * HD)
    return pl.pallas_call(
        qkv_kernel,
        grid_spec=pltpu.PrefetchScalarGridSpec(
            num_scalar_prefetch=1,
            grid=(size,),
            in_specs=[whole(weight.shape), whole((1, width)), rows(128), rows(128)]
            + [whole((own, width))] * len(pieces),
            out_specs=[rows(wide) for wide in widths],
        ),
        out_shape=[jax.ShapeDtypeStruct((tokens, wide), jnp.bfloat16) for wide in widths],
        compiler_params=pltpu.CompilerParams(vmem_limit_bytes=VMEM_LIMIT),
        cost_estimate=cost(9),
        name="project_qkv",
    )(jnp.reshape(rank, (1,)).astype(jnp.int32), weight, gain[None], cos, sin, *pieces)


def stack_heads(block, low_lanes):
    rows = block.shape[0]
    lane = lax.broadcasted_iota(jnp.int32, (rows, 128), 1)
    keep = (lane < HD) if low_lanes else (lane >= HD)
    stacked = []
    for pair in range(QPK // 2):
        both = block[:, pair * 128 : (pair + 1) * 128].astype(jnp.float32)
        turned = pltpu.roll(both, HD, 1)
        for part in (both, turned) if low_lanes else (turned, both):
            stacked.append(jnp.where(keep, part, 0.0))
    return jnp.concatenate(stacked, axis=0).astype(jnp.bfloat16)


def unstack_heads(stacked, low_lanes):
    rows = stacked.shape[0] // QPK
    lane = lax.broadcasted_iota(jnp.int32, (rows, 128), 1)
    blocks = []
    for pair in range(QPK // 2):
        first = stacked[2 * pair * rows : (2 * pair + 1) * rows]
        second = stacked[(2 * pair + 1) * rows : (2 * pair + 2) * rows]
        if low_lanes:
            second = pltpu.roll(second, HD, 1)
        else:
            first = pltpu.roll(first, HD, 1)
        blocks.append(jnp.where(lane < HD, first, second))
    return blocks


def key_blocks(pos_ref, tile, tq, tk, step, low=0, high=None):
    tokens = pos_ref.shape[0]
    query = tile * tq
    start = REACH * tokens + query
    first = jnp.maximum(start - pos_ref[query], low)
    last_start = start + tq - 1 - pos_ref[query + tq - 1]
    end = (start + tq - 1) // tk + 1
    if high is not None:
        end = jnp.minimum(end, high // tk)

    def body(block, carry):
        key = block * tk
        clear = (key >= last_start) & (key + tk - 1 <= start)

        @pl.when(clear)
        def _():
            step(key, False)

        @pl.when(jnp.logical_not(clear))
        def _():
            step(key, True)

        return carry

    lax.fori_loop(first // tk, end, body, 0)


def allowed_block(key, tile, tokens, tk, tq, back_row):
    key_at = key + lax.broadcasted_iota(jnp.int32, (tk, tq), 0)
    query_at = REACH * tokens + tile * tq + lax.broadcasted_iota(jnp.int32, (tk, tq), 1)
    back = query_at - key_at
    allowed = (back >= 0) & (back <= back_row)
    return jnp.concatenate([allowed] * QPK, axis=1)


def attend_step(key, masked, tile, tk, base, back_ref, kv, vx, qs, acc, top, tokens):
    tq = qs.shape[0] // QPK
    scores = lax.dot_general(
        kv[pl.ds(key - base, tk), :], qs[...], COLS_BY_COLS, preferred_element_type=jnp.float32
    )
    if masked:
        allowed = allowed_block(key, tile, tokens, tk, tq, back_ref[0:1, :])
        scores = jnp.where(allowed, scores, NEG_FILL)
    old = top[0:1, :]
    new = jnp.maximum(old, jnp.max(scores, axis=0, keepdims=True))
    top[0:1, :] = new
    probs = jnp.exp2((scores - new) * EXP_SCALE).astype(jnp.bfloat16)
    fade = jnp.exp2((old - new) * EXP_SCALE)
    acc[...] = acc[...] * fade + lax.dot_general(
        vx[pl.ds(key - base, tk), :], probs, ROWS_BY_ROWS, preferred_element_type=jnp.float32
    )


def load_sources(refs, kv, vx):
    tokens = refs[0].shape[0]
    lane = lax.broadcasted_iota(jnp.int32, (tokens, 2 * HD), 1)
    for i, ref in enumerate(refs):
        kv[pl.ds(i * tokens, tokens), :] = ref[...]
        vx[pl.ds(i * tokens, tokens), :] = jnp.where(lane < HD, jnp.ones_like(ref), ref[...])


def attend_here_kernel(tk, pos_ref, q_ref, back_ref, here, acc_ref, top_ref, vx, qs):
    tokens = here.shape[0]
    tq = q_ref.shape[0]
    tile = pl.program_id(0)
    acc, top = acc_ref.at[0], top_ref.at[0]

    @pl.when(tile == 0)
    def _():
        lane = lax.broadcasted_iota(jnp.int32, (tokens, 2 * HD), 1)
        vx[...] = jnp.where(lane < HD, jnp.ones_like(here), here[...])

    qs[...] = stack_heads(q_ref[...], True)
    acc[...] = jnp.zeros_like(acc)
    top[...] = jnp.full_like(top, NEG_FILL)
    base = REACH * tokens

    def step(key, masked):
        attend_step(key, masked, tile, tk, base, back_ref, here, vx, qs, acc, top, tokens)

    key_blocks(pos_ref, tile, tq, tk, step, low=base)


def attend_far_kernel(
    tk, pos_ref, q_ref, back_ref, far_two, far_one, acc_ref, top_ref,
    out_ref, lse_ref, kv, vx, qs, acc, top
):
    tokens = far_one.shape[0]
    tq = q_ref.shape[0]
    tile = pl.program_id(0)

    @pl.when(tile == 0)
    def _():
        load_sources((far_two, far_one), kv, vx)

    qs[...] = stack_heads(q_ref[...], True)
    acc[...] = acc_ref[0]
    top[...] = top_ref[0]

    def step(key, masked):
        attend_step(key, masked, tile, tk, 0, back_ref, kv, vx, qs, acc, top, tokens)

    key_blocks(pos_ref, tile, tq, tk, step, high=REACH * tokens)
    total = acc[...]
    weight = total[0:1]
    blocks = unstack_heads(jnp.transpose(total / weight), False)
    out_ref[...] = jnp.concatenate(blocks, axis=1).astype(jnp.bfloat16)
    lse = top[0:1, :] * EXP_SCALE + jnp.log2(weight)
    lse_ref[...] = jnp.broadcast_to(lse, (8, lse.shape[1]))[None]


def attend_here(queries, here, positions, back_rows, group, tq, tk):
    tokens = queries.shape[0]
    state = (
        jax.ShapeDtypeStruct((tokens // tq, 2 * HD, QPK * tq), jnp.float32),
        jax.ShapeDtypeStruct((tokens // tq, 8, QPK * tq), jnp.float32),
    )
    return pl.pallas_call(
        functools.partial(attend_here_kernel, tk),
        grid_spec=pltpu.PrefetchScalarGridSpec(
            num_scalar_prefetch=1,
            grid=(tokens // tq,),
            in_specs=[
                pl.BlockSpec((tq, QPK * HD), lambda i, p: (i, group)),
                pl.BlockSpec((8, tq), lambda i, p: (0, i)),
                pl.BlockSpec((tokens, 2 * HD), lambda i, p: (0, group)),
            ],
            out_specs=[pl.BlockSpec((1, *shape.shape[1:]), lambda i, p: (i, 0, 0)) for shape in state],
            scratch_shapes=[
                pltpu.VMEM((tokens, 2 * HD), jnp.bfloat16),
                pltpu.VMEM((QPK * tq, 2 * HD), jnp.bfloat16),
            ],
        ),
        out_shape=state,
        compiler_params=pltpu.CompilerParams(vmem_limit_bytes=VMEM_LIMIT),
        cost_estimate=cost(10),
        name="attend_here",
    )(positions, queries, back_rows, here)


def attend_far(queries, far, state, positions, back_rows, group, tq, tk):
    tokens = queries.shape[0]
    kv_spec = pl.BlockSpec((tokens, 2 * HD), lambda i, p: (0, group))
    return pl.pallas_call(
        functools.partial(attend_far_kernel, tk),
        grid_spec=pltpu.PrefetchScalarGridSpec(
            num_scalar_prefetch=1,
            grid=(tokens // tq,),
            in_specs=[
                pl.BlockSpec((tq, QPK * HD), lambda i, p: (i, group)),
                pl.BlockSpec((8, tq), lambda i, p: (0, i)),
                kv_spec,
                kv_spec,
            ]
            + [pl.BlockSpec((1, *part.shape[1:]), lambda i, p: (i, 0, 0)) for part in state],
            out_specs=[
                pl.BlockSpec((tq, QPK * HD), lambda i, p: (i, 0)),
                pl.BlockSpec((1, 8, QPK * tq), lambda i, p: (i, 0, 0)),
            ],
            scratch_shapes=[
                pltpu.VMEM((REACH * tokens, 2 * HD), jnp.bfloat16),
                pltpu.VMEM((REACH * tokens, 2 * HD), jnp.bfloat16),
                pltpu.VMEM((QPK * tq, 2 * HD), jnp.bfloat16),
                pltpu.VMEM((2 * HD, QPK * tq), jnp.float32),
                pltpu.VMEM((8, QPK * tq), jnp.float32),
            ],
        ),
        out_shape=[
            jax.ShapeDtypeStruct((tokens, QPK * HD), jnp.bfloat16),
            jax.ShapeDtypeStruct((tokens // tq, 8, QPK * tq), jnp.float32),
        ],
        compiler_params=pltpu.CompilerParams(vmem_limit_bytes=VMEM_LIMIT),
        cost_estimate=cost(14),
        name="attend_far",
    )(positions, queries, back_rows, *far, *state)


def attend_back_kernel(
    tk, pos_ref, q_ref, do_ref, o_ref, back_ref, lse_ref, cos_ref, sin_ref, far_two, far_one, here,
    dq_ref, d_far_two, d_far_one, d_here, kv, dkv, qs, dos, dq
):
    tokens = here.shape[0]
    tq = q_ref.shape[0]
    tile = pl.program_id(0)

    @pl.when(tile == 0)
    def _():
        for i, ref in enumerate((far_two, far_one, here)):
            kv[pl.ds(i * tokens, tokens), :] = ref[...]
        dkv[...] = jnp.zeros_like(dkv)

    qs[...] = stack_heads(q_ref[...], True)
    dos[...] = stack_heads(do_ref[...], False)
    dq[...] = jnp.zeros_like(dq)
    product = dos[...].astype(jnp.float32) * stack_heads(o_ref[...], False).astype(jnp.float32)
    delta = jnp.sum(jnp.transpose(product), axis=0, keepdims=True)
    lse = lse_ref[0, 0:1, :]

    def step(key, masked):
        keys = kv[pl.ds(key, tk), :]
        scores = lax.dot_general(keys, qs[...], COLS_BY_COLS, preferred_element_type=jnp.float32)
        probs = jnp.exp2(scores * EXP_SCALE - lse)
        if masked:
            allowed = allowed_block(key, tile, tokens, tk, tq, back_ref[0:1, :])
            probs = jnp.where(allowed, probs, 0.0)
        d_probs = lax.dot_general(keys, dos[...], COLS_BY_COLS, preferred_element_type=jnp.float32)
        d_scores = (probs * (d_probs - delta)).astype(jnp.bfloat16)
        d_keys = jnp.dot(d_scores, qs[...], preferred_element_type=jnp.float32)
        d_values = jnp.dot(probs.astype(jnp.bfloat16), dos[...], preferred_element_type=jnp.float32)
        dkv[pl.ds(key, tk), :] += d_keys * HD**-0.5 + d_values
        dq[...] += lax.dot_general(
            d_scores, keys, ROWS_BY_ROWS, preferred_element_type=jnp.float32
        )

    key_blocks(pos_ref, tile, tq, tk, step)
    cos, sin = cos_ref[...], sin_ref[...]
    blocks = unstack_heads(dq[...] * HD**-0.5, True)
    blocks = [block * cos - turn_halves(block) * sin for block in blocks]
    dq_ref[...] = jnp.concatenate(blocks, axis=1).astype(jnp.bfloat16)

    @pl.when(tile == pl.num_programs(0) - 1)
    def _():
        d_far_two[...] = dkv[pl.ds(0, tokens), :].astype(jnp.bfloat16)
        d_far_one[...] = dkv[pl.ds(tokens, tokens), :].astype(jnp.bfloat16)
        d_here[...] = dkv[pl.ds(2 * tokens, tokens), :]


def attend_back(
    queries, d_attn, attn, lse, sources, positions, back_rows, cos, sin, group, tq, tk
):
    tokens = queries.shape[0]
    kv_spec = pl.BlockSpec((tokens, 2 * HD), lambda i, p: (0, group))
    own_kv = pl.BlockSpec((tokens, 2 * HD), lambda i, p: (0, 0))
    q_spec = pl.BlockSpec((tq, QPK * HD), lambda i, p: (i, group))
    own_q = pl.BlockSpec((tq, QPK * HD), lambda i, p: (i, 0))
    angle_spec = pl.BlockSpec((tq, 128), lambda i, p: (i, 0))
    return pl.pallas_call(
        functools.partial(attend_back_kernel, tk),
        grid_spec=pltpu.PrefetchScalarGridSpec(
            num_scalar_prefetch=1,
            grid=(tokens // tq,),
            in_specs=[
                q_spec,
                q_spec,
                own_q,
                pl.BlockSpec((8, tq), lambda i, p: (0, i)),
                pl.BlockSpec((1, 8, QPK * tq), lambda i, p: (i, 0, 0)),
                angle_spec,
                angle_spec,
                kv_spec,
                kv_spec,
                kv_spec,
            ],
            out_specs=[own_q, own_kv, own_kv, own_kv],
            scratch_shapes=[
                pltpu.VMEM(((REACH + 1) * tokens, 2 * HD), jnp.bfloat16),
                pltpu.VMEM(((REACH + 1) * tokens, 2 * HD), jnp.float32),
                pltpu.VMEM((QPK * tq, 2 * HD), jnp.bfloat16),
                pltpu.VMEM((QPK * tq, 2 * HD), jnp.bfloat16),
                pltpu.VMEM((QPK * tq, 2 * HD), jnp.float32),
            ],
        ),
        out_shape=[
            jax.ShapeDtypeStruct((tokens, QPK * HD), jnp.bfloat16),
            jax.ShapeDtypeStruct((tokens, 2 * HD), jnp.bfloat16),
            jax.ShapeDtypeStruct((tokens, 2 * HD), jnp.bfloat16),
            jax.ShapeDtypeStruct((tokens, 2 * HD), jnp.float32),
        ],
        compiler_params=pltpu.CompilerParams(vmem_limit_bytes=VMEM_LIMIT),
        cost_estimate=cost(28),
        name="attend_back",
    )(positions, queries, d_attn, attn, back_rows, lse, cos, sin, *sources)


def mix_kernel(groups, cos_ref, sin_ref, *refs):
    out_ref = refs[-1]
    cos, sin = cos_ref[...], sin_ref[...]
    key_lane = lax.broadcasted_iota(jnp.int32, cos.shape, 1) < HD
    for group in range(groups):
        dq_ref, here, from_one, from_two = refs[4 * group : 4 * group + 4]
        base = group * (QPK + 2) * HD
        out_ref[:, base : base + QPK * HD] = dq_ref[...]
        total = here[...] + from_one[...].astype(jnp.float32) + from_two[...].astype(jnp.float32)
        turned = total * cos - turn_halves(total) * sin
        out_ref[:, base + QPK * HD : base + (QPK + 2) * HD] = jnp.where(
            key_lane, turned, total
        ).astype(jnp.bfloat16)


def mix_grads(parts, cos, sin, tile):
    tokens = cos.shape[0]
    groups = len(parts)

    def rows(wide):
        return pl.BlockSpec((tile, wide), lambda i: (i, 0))

    flat = [array for part in parts for array in part]
    return pl.pallas_call(
        functools.partial(mix_kernel, groups),
        grid=(tokens // tile,),
        in_specs=[rows(128), rows(128)] + [rows(array.shape[1]) for array in flat],
        out_specs=rows(groups * (QPK + 2) * HD),
        out_shape=jax.ShapeDtypeStruct((tokens, groups * (QPK + 2) * HD), jnp.bfloat16),
        compiler_params=pltpu.CompilerParams(vmem_limit_bytes=VMEM_LIMIT),
        cost_estimate=cost(3),
        name="mix_grads",
    )(cos, sin, *flat)


def out_kernel(rank_ref, x_ref, w_ref, gain_ref, *refs):
    *pieces, mid_ref, normed_ref, own_ref, heads = refs
    size = (len(pieces) + 1) // 2
    columns = pieces[0].shape[1]
    for slot in range(size):

        def put(piece, slot=slot):
            heads[:, slot * columns : (slot + 1) * columns] = piece[...]

        pick_piece(pieces, rank_ref[0] - slot, put)
    mid = x_ref[...].astype(jnp.float32) + jnp.dot(
        heads[...], w_ref[...], preferred_element_type=jnp.float32
    )
    mid_ref[...] = mid
    inverse = lax.rsqrt(jnp.mean(mid * mid, axis=1, keepdims=True) + NORM_EPS)
    normed_ref[...] = (mid * inverse * gain_ref[...]).astype(jnp.bfloat16)

    @pl.when(pl.program_id(0) == rank_ref[0])
    def _():
        own_ref[...] = heads[...]


def project_out(x_rows, pieces, rank, weight, gain, own):
    tokens, width = x_rows.shape
    columns = weight.shape[0]

    def rows(wide):
        return pl.BlockSpec((own, wide), lambda i, r: (i, 0))

    def whole(shape):
        return pl.BlockSpec(shape, lambda i, r: (0, 0))

    return pl.pallas_call(
        out_kernel,
        grid_spec=pltpu.PrefetchScalarGridSpec(
            num_scalar_prefetch=1,
            grid=(tokens // own,),
            in_specs=[rows(width), whole(weight.shape), whole((1, width))]
            + [rows(piece.shape[1]) for piece in pieces],
            out_specs=[rows(width), rows(width), whole((own, columns))],
            scratch_shapes=[pltpu.VMEM((own, columns), jnp.bfloat16)],
        ),
        out_shape=[
            jax.ShapeDtypeStruct((tokens, width), jnp.float32),
            jax.ShapeDtypeStruct((tokens, width), jnp.bfloat16),
            jax.ShapeDtypeStruct((own, columns), jnp.bfloat16),
        ],
        compiler_params=pltpu.CompilerParams(vmem_limit_bytes=VMEM_LIMIT),
        cost_estimate=cost(15),
        name="project_out",
    )(jnp.reshape(rank, (1,)).astype(jnp.int32), x_rows, weight, gain[None], *pieces)


def gate_kernel(n_ref, w_ref, dh_ref, hidden_ref, dgu_ref):
    wide = dh_ref.shape[1]
    both = jnp.dot(n_ref[...], w_ref[...], preferred_element_type=jnp.float32)
    gate, up = both[:, :wide], both[:, wide:]
    sigmoid = jax.nn.sigmoid(gate)
    silu = gate * sigmoid
    d_hidden = dh_ref[...].astype(jnp.float32)
    hidden_ref[...] = (silu * up).astype(jnp.bfloat16)
    d_gate = d_hidden * up * (sigmoid + silu * (1.0 - sigmoid))
    dgu_ref[...] = jnp.concatenate([d_gate, d_hidden * silu], axis=1).astype(jnp.bfloat16)


def gate_and_back(normed, weight, d_hidden, tile, wide):
    tokens, width = normed.shape
    units = d_hidden.shape[1]
    cell = pl.BlockSpec((tile, wide), lambda j, i: (i, j))
    pair_cell = pl.BlockSpec((tile, 2 * wide), lambda j, i: (i, j))
    return pl.pallas_call(
        gate_kernel,
        grid=(units // wide, tokens // tile),
        in_specs=[
            pl.BlockSpec((tile, width), lambda j, i: (i, 0)),
            pl.BlockSpec((width, 2 * wide), lambda j, i: (0, j)),
            cell,
        ],
        out_specs=[cell, pair_cell],
        out_shape=[
            jax.ShapeDtypeStruct((tokens, units), jnp.bfloat16),
            jax.ShapeDtypeStruct((tokens, 2 * units), jnp.bfloat16),
        ],
        compiler_params=pltpu.CompilerParams(vmem_limit_bytes=VMEM_LIMIT),
        cost_estimate=cost(27),
        name="gate_and_back",
    )(normed, weight, d_hidden)


def blocks_kernel(chunks_ref, *refs):
    count = (len(refs) - 1) // 2
    left = jnp.concatenate([ref[...] for ref in refs[:count]], axis=0)
    product = lax.dot_general(
        left, refs[count][...], COLS_BY_COLS, preferred_element_type=jnp.float32
    ).astype(jnp.bfloat16)
    rows = refs[0].shape[0]
    for i, out_ref in enumerate(refs[count + 1 :]):
        out_ref[...] = product[i * rows : (i + 1) * rows]


def blocks_times(left, right, chunks, rows, wide, micros):
    depth = left.shape[1]
    count = chunks.shape[0]

    def block_spec(i):
        return pl.BlockSpec((rows, depth), lambda j, c: (c[i], 0))

    return pl.pallas_call(
        blocks_kernel,
        grid_spec=pltpu.PrefetchScalarGridSpec(
            num_scalar_prefetch=1,
            grid=(right.shape[0] // wide,),
            in_specs=[block_spec(i) for i in range(count)]
            + [pl.BlockSpec((wide, depth), lambda j, c: (j, 0))],
            out_specs=[pl.BlockSpec((rows, wide), lambda j, c: (0, j))] * count,
        ),
        out_shape=[jax.ShapeDtypeStruct((rows, right.shape[0]), jnp.bfloat16)] * count,
        compiler_params=pltpu.CompilerParams(vmem_limit_bytes=VMEM_LIMIT),
        cost_estimate=cost(micros),
        name="blocks_times",
    )(chunks, *[left] * count, right)


def gain_kernel(part_ref, w_ref, out_ref):
    product = part_ref[...].astype(jnp.float32) * w_ref[...].astype(jnp.float32)
    ones = jnp.ones((8, product.shape[1]), jnp.float32)
    out_ref[...] = lax.dot_general(
        ones, product, COLS_BY_COLS, precision=lax.Precision.HIGHEST,
        preferred_element_type=jnp.float32,
    )


def row_products(part, weight, tile):
    rows, columns = part.shape
    cell = pl.BlockSpec((tile, columns), lambda i: (i, 0))
    sums = pl.pallas_call(
        gain_kernel,
        grid=(rows // tile,),
        in_specs=[cell, cell],
        out_specs=pl.BlockSpec((8, tile), lambda i: (0, i)),
        out_shape=jax.ShapeDtypeStruct((8, rows), jnp.float32),
        compiler_params=pltpu.CompilerParams(vmem_limit_bytes=VMEM_LIMIT),
        cost_estimate=cost(4),
        name="row_products",
    )(part, weight)
    return sums[0]


def norm_back_rows(vector, grad_in, gain):
    inverse = lax.rsqrt(jnp.mean(vector * vector, axis=1, keepdims=True) + NORM_EPS)
    scaled = grad_in * gain
    mean = jnp.mean(vector * scaled, axis=1, keepdims=True)
    grad = inverse * scaled - vector * (inverse * inverse * inverse * mean)
    return grad, jnp.sum(grad_in * vector * inverse, axis=0, keepdims=True)


def sum_refs(refs):
    total = refs[0][...].astype(jnp.float32)
    for ref in refs[1:]:
        total = total + ref[...].astype(jnp.float32)
    return total


def mid_kernel(rank_ref, mid_ref, dy_ref, gain_ref, *refs):
    *parts, d_mid_ref, branch_ref, mid_out, gain_grad_ref = refs
    mid = mid_ref[...]
    grad, gain_grad = norm_back_rows(mid, sum_refs(parts), gain_ref[...])
    d_mid = dy_ref[...].astype(jnp.float32) + grad
    d_mid_ref[...] = d_mid
    branch_ref[...] = d_mid.astype(jnp.bfloat16)
    mid_out[...] = mid
    gain_grad = jnp.broadcast_to(gain_grad, gain_grad_ref.shape)

    @pl.when(pl.program_id(0) == 0)
    def _():
        gain_grad_ref[...] = gain_grad

    @pl.when(pl.program_id(0) > 0)
    def _():
        gain_grad_ref[...] += gain_grad


def back_to_mid(parts, mid_rows, rank, output_grad, gain):
    own, width = output_grad.shape
    tile = min(64, own)
    tiles = own // tile

    def rows(index):
        return pl.BlockSpec((tile, width), index)

    own_rows = rows(lambda i, r: (i, 0))
    outs = pl.pallas_call(
        mid_kernel,
        grid_spec=pltpu.PrefetchScalarGridSpec(
            num_scalar_prefetch=1,
            grid=(tiles,),
            in_specs=[
                rows(lambda i, r: (r[0] * tiles + i, 0)),
                own_rows,
                pl.BlockSpec((1, width), lambda i, r: (0, 0)),
            ]
            + [own_rows] * len(parts),
            out_specs=[own_rows, own_rows, own_rows, pl.BlockSpec((8, width), lambda i, r: (0, 0))],
        ),
        out_shape=[
            jax.ShapeDtypeStruct((own, width), jnp.float32),
            jax.ShapeDtypeStruct((own, width), jnp.bfloat16),
            jax.ShapeDtypeStruct((own, width), jnp.float32),
            jax.ShapeDtypeStruct((8, width), jnp.float32),
        ],
        compiler_params=pltpu.CompilerParams(vmem_limit_bytes=VMEM_LIMIT),
        cost_estimate=cost(4),
        name="back_to_mid",
    )(jnp.reshape(rank, (1,)).astype(jnp.int32), mid_rows, output_grad, gain[None], *parts)
    return outs[0], outs[1], outs[2], outs[3][0]


def input_kernel(x_ref, d_mid_ref, gain_ref, *refs):
    *parts, out_ref = refs
    x = x_ref[...].astype(jnp.float32)
    grad, _ = norm_back_rows(x, sum_refs(parts), gain_ref[...])
    out_ref[...] = d_mid_ref[...] + grad


def back_to_input(parts, layer_input, d_mid, gain):
    own, width = layer_input.shape
    tile = min(64, own)
    rows = pl.BlockSpec((tile, width), lambda i: (i, 0))
    return pl.pallas_call(
        input_kernel,
        grid=(own // tile,),
        in_specs=[rows, rows, pl.BlockSpec((1, width), lambda i: (0, 0))] + [rows] * len(parts),
        out_specs=rows,
        out_shape=jax.ShapeDtypeStruct((own, width), jnp.float32),
        compiler_params=pltpu.CompilerParams(vmem_limit_bytes=VMEM_LIMIT),
        cost_estimate=cost(4),
        name="back_to_input",
    )(layer_input, d_mid, gain[None], *parts)


def round_kernel(w_ref, out_ref):
    out_ref[...] = w_ref[0].astype(jnp.bfloat16)


def round_interleaved(weight, wide):
    _, rows, units = weight.shape
    return pl.pallas_call(
        round_kernel,
        grid=(units // wide, 2),
        in_specs=[pl.BlockSpec((1, rows, wide), lambda j, k: (k, 0, j))],
        out_specs=pl.BlockSpec((rows, wide), lambda j, k: (0, 2 * j + k)),
        out_shape=jax.ShapeDtypeStruct((rows, 2 * units), jnp.bfloat16),
        cost_estimate=cost(6),
        name="round_interleaved",
    )(weight)


def adam_kernel(g_ref, w_ref, m_ref, s_ref, grad_ref, w_out, m_out, s_out, copy_out):
    grad = g_ref[...].astype(jnp.float32)
    new, moment, square, _ = adam_step(w_ref[0], grad, m_ref[0], s_ref[0])
    grad_ref[0] = grad
    w_out[0] = new
    m_out[0] = moment
    s_out[0] = square
    copy_out[0] = new.astype(jnp.bfloat16)


def adam_interleaved(grad, weight, moment, square, wide):
    _, rows, units = weight.shape
    cell = pl.BlockSpec((1, rows, wide), lambda j, k: (k, 0, j))
    shape = jax.ShapeDtypeStruct(weight.shape, jnp.float32)
    return pl.pallas_call(
        adam_kernel,
        grid=(units // wide, 2),
        in_specs=[pl.BlockSpec((rows, wide), lambda j, k: (0, 2 * j + k)), cell, cell, cell],
        out_specs=[cell] * 5,
        out_shape=[shape] * 4 + [jax.ShapeDtypeStruct(weight.shape, jnp.bfloat16)],
        compiler_params=pltpu.CompilerParams(vmem_limit_bytes=VMEM_LIMIT),
        cost_estimate=cost(13),
        name="adam_interleaved",
    )(grad, weight, moment, square)


def angle_tables(positions):
    half_size = HD // 2
    freq = ROPE_BASE ** (-(jnp.arange(half_size).astype(jnp.float32) * 2.0 / HD))
    angle = positions.astype(jnp.float32)[:, None] * freq[None, :]
    cos, sin = jnp.cos(angle), jnp.sin(angle)
    return jnp.concatenate([cos] * 4, axis=1), jnp.concatenate([-sin, sin] * 2, axis=1)


def adam_step(weight_old, grad_new, moment_one, moment_two):
    moment_next = BETA * moment_one + (1.0 - BETA) * grad_new
    square_next = BETA * moment_two + (1.0 - BETA) * grad_new * grad_new
    change = -RATE * (moment_next / (jnp.sqrt(square_next) + ADAM_EPS) + DECAY * weight_old)
    return (weight_old + change, moment_next, square_next, change)


def local(
    layer_input,
    output_grad,
    segment_ids,
    positions,
    qkv_weight,
    qkv_moment,
    qkv_square,
    out_weight,
    out_moment,
    out_square,
    gate_up_weight,
    gate_up_moment,
    gate_up_square,
    down_weight,
    down_moment,
    down_square,
    norm_gains,
    gains_moment,
    gains_square,
):
    low = low_type = jnp.bfloat16
    full = jnp.float32
    own, width = layer_input.shape
    tokens = positions.shape[0]
    rank = lax.axis_index("tp")
    units = down_weight.shape[0]
    groups = qkv_weight.shape[1] // ((QPK + 2) * HD)
    head_columns = groups * QPK * HD
    tile = min(256, own)
    gain_one = norm_gains[0]
    gain_two = norm_gains[1]

    wide = min(512, units)

    close = lax.optimization_barrier

    low_qkv = qkv_weight.astype(low)
    low_down = down_weight.astype(low)
    w_qkv = lax.all_gather(low_qkv, "seq", axis=0, tiled=True)
    w_down = lax.all_gather(low_down, "seq", axis=1, tiled=True)
    low_gate_up = round_interleaved(gate_up_weight, wide)
    low_out = out_weight.astype(low)
    cos, sin = angle_tables(positions)
    back_rows = jnp.broadcast_to(positions[None, :], (8, tokens))
    side = (low_gate_up, low_out, cos, sin, back_rows)
    x_line = LineGather(layer_input, "tp")
    for _ in range(x_line.hops):
        x_line.hop()
        x_line.moving, side = close((x_line.moving, side))
    pieces, side, w_qkv, output_grad = close((x_line.pieces, side, w_qkv, output_grad))
    low_gate_up, low_out, cos, sin, back_rows = side

    dy_line = LineGather(output_grad, "tp")
    dy_line.hop()
    made = project_qkv(pieces, rank, w_qkv, gain_one, cos, sin)
    made, dy_line.moving, w_down, low_out = close((made, dy_line.moving, w_down, low_out))
    x_rows, normed_one, queries, kv = made
    out_strip = lax.all_gather(low_out, "tp", axis=0, tiled=True)
    far = [along_sequence(kv, distance, tokens) for distance in (2, 1)]
    if dy_line.hops > 1:
        dy_line.hop()
    states = [
        attend_here(queries, kv, positions, back_rows, group, 256, 512) for group in range(groups)
    ]
    far, states, out_strip, queries, low_gate_up, dy_line.moving = close(
        (far, states, out_strip, queries, low_gate_up, dy_line.moving)
    )
    w_out = lax.all_gather(out_strip, "seq", axis=1, tiled=True)
    w_gate_up = lax.all_gather(low_gate_up, "seq", axis=0, tiled=True)
    for _ in range(2, dy_line.hops):
        dy_line.hop()
    attn, lse = [], []
    for group in range(groups):
        out, log_total = attend_far(
            queries, far, states[group], positions, back_rows, group, 256, 512
        )
        attn.append(out)
        lse.append(log_total)
    attn, lse, dy_pieces, w_down, x_rows = close((attn, lse, dy_line.pieces, w_down, x_rows))

    heads_line = LineGather(jnp.concatenate(attn, axis=1), "tp")
    for index in range(heads_line.hops):
        heads_line.hop()
        if index == 0:
            grad_rows = place_rows(dy_pieces, rank)
            d_hidden = contract_cols(grad_rows, w_down).astype(low)
            side = (grad_rows, d_hidden, x_rows)
            heads_line.moving, side, w_out = close((heads_line.moving, side, w_out))
        else:
            heads_line.moving, side = close((heads_line.moving, side))
    grad_rows, d_hidden, x_rows = side

    mid_rows, normed_two, own_heads = project_out(
        x_rows, heads_line.pieces, rank, w_out, gain_two, own
    )
    mid_rows, normed_two, own_heads, w_gate_up, d_hidden = close(
        (mid_rows, normed_two, own_heads, w_gate_up, d_hidden)
    )
    hidden, d_gate_up = close(gate_and_back(normed_two, w_gate_up, d_hidden, 512, wide))
    peers = peers_of("tp")
    half = peers.shape[0] // 2
    first = blocks_times(d_gate_up, w_gate_up, peers[:half], own, 256, 15)
    first, side = close((first, (hidden, d_gate_up, normed_two, grad_rows)))
    back_line = LineScatter(first, "tp")
    for index in range(back_line.hops):
        back_line.hop()
        hidden, d_gate_up, normed_two, grad_rows = side
        if index == 0:
            second = blocks_times(d_gate_up, w_gate_up, peers[half:], own, 256, 15)
            down_grad = contract_rows(hidden, grad_rows).astype(low)
            back_line.moving, side, second, down_grad = close(
                (back_line.moving, side, second, down_grad)
            )
            back_line.made += second
            down_grad = lax.psum_scatter(down_grad, "seq", scatter_dimension=1, tiled=True)
        elif index == 1:
            gate_up_grad = contract_rows(normed_two, d_gate_up).astype(low)
            back_line.moving, side, gate_up_grad = close((back_line.moving, side, gate_up_grad))
            gate_up_grad = lax.psum_scatter(gate_up_grad, "seq", scatter_dimension=0, tiled=True)
        elif index == 2:
            partial_out = jnp.dot(hidden, w_down, preferred_element_type=full).astype(low)
            back_line.moving, side, partial_out = close((back_line.moving, side, partial_out))
        else:
            back_line.moving, side = close((back_line.moving, side))
    d_mid, d_branch, mid, gain_two_grad = back_to_mid(
        back_line.parts, mid_rows, rank, output_grad, gain_two
    )

    d_attn = contract_cols(d_branch, w_out).astype(low)
    d_attn, d_branch, d_mid, mid, gain_two_grad, own_heads, partial_out = close(
        (d_attn, d_branch, d_mid, mid, gain_two_grad, own_heads, partial_out)
    )
    d_attn = lax.all_to_all(d_attn, "tp", split_axis=1, concat_axis=0, tiled=True)
    out_grad = contract_rows(own_heads, d_branch).astype(low)
    d_attn, out_grad, partial_out, down_grad = close((d_attn, out_grad, partial_out, down_grad))
    out_grad = lax.psum_scatter(out_grad, "seq", scatter_dimension=1, tiled=True)
    made = [
        lax.dynamic_slice_in_dim(partial_out, peers[i] * own, own, axis=0)
        for i in range(peers.shape[0])
    ]
    out_line = LineScatter(made, "tp")
    grads = []
    travelled = []
    for group in range(groups):
        out_line.hop()
        made = attend_back(
            queries, d_attn, attn[group], lse[group], [*far, kv], positions, back_rows,
            cos, sin, group, 256, 512,
        )
        made, d_attn, travelled, out_line.moving = close(
            (made, d_attn, travelled, out_line.moving)
        )
        grads.append(made)
        travelled.append(
            [along_sequence(made[2], -1, tokens), along_sequence(made[1], -2, tokens)]
        )
    down_new = adam_step(down_weight, down_grad.astype(full), down_moment, down_square)
    while out_line.step < out_line.hops:
        out_line.hop()
        down_new, grads, travelled, down_grad, out_line.moving = close(
            (down_new, grads, travelled, down_grad, out_line.moving)
        )
    d_mixed = mix_grads(
        [(made[0], made[3], *moved) for made, moved in zip(grads, travelled, strict=True)],
        cos, sin, tile,
    )
    made = blocks_times(d_mixed, w_qkv, peers, own, 512, 7)
    made, d_mixed, gate_up_grad = close((made, d_mixed, gate_up_grad))
    in_line = LineScatter(made, "tp")
    bits = [1 << bit for bit in range(lax.axis_size("seq").bit_length() - 1)]
    for index in range(in_line.hops):
        in_line.hop()
        if index == 0:
            qkv_grad = contract_rows(normed_one, d_mixed).astype(low)
            gain_one_grad = row_products(qkv_grad, w_qkv, min(512, width)) / gain_one
            qkv_grad = qkv_grad.reshape(lax.axis_size("seq"), -1, qkv_grad.shape[1])
            in_line.moving, qkv_grad, gain_one_grad = close(
                (in_line.moving, qkv_grad, gain_one_grad)
            )
        elif index == 1:
            gate_up_new = adam_interleaved(
                gate_up_grad, gate_up_weight, gate_up_moment, gate_up_square, wide
            )
            for hop in bits[:2]:
                qkv_grad = halving_hop(qkv_grad, "seq", hop)
            gains_grad = sum_everywhere(jnp.stack([gain_one_grad, gain_two_grad]), ("seq",))
            in_line.moving, gate_up_new, gains_grad, qkv_grad = close(
                (in_line.moving, gate_up_new, gains_grad, qkv_grad)
            )
            for hop in bits[2:]:
                qkv_grad = halving_hop(qkv_grad, "seq", hop)
            qkv_grad = qkv_grad[0]
            gains_grad = sum_everywhere(gains_grad, ("tp",))
            outputs = (mid + sum(part.astype(full) for part in out_line.parts)).astype(low)
        elif index == in_line.hops - 1:
            in_line.moving, gains_grad, qkv_grad, outputs, out_grad = close(
                (in_line.moving, gains_grad, qkv_grad, outputs, out_grad)
            )
        else:
            in_line.moving = close(in_line.moving)
    out_parts = swap_scatter_parts(out_grad, "tp")
    input_grad = back_to_input(in_line.parts, layer_input, d_mid, gain_one)
    out_grad = sum_parts(out_parts)
    out_new = adam_step(out_weight, out_grad, out_moment, out_square)

    qkv_grad = qkv_grad.astype(full)
    out_grad = out_grad.astype(full)
    down_grad = down_grad.astype(full)
    qkv_new = adam_step(qkv_weight, qkv_grad, qkv_moment, qkv_square)
    gains_new = adam_step(norm_gains, gains_grad, gains_moment, gains_square)
    return (
        outputs,
        input_grad,
        qkv_grad,
        qkv_new[0],
        qkv_new[1],
        qkv_new[2],
        qkv_new[0].astype(low),
        out_grad,
        out_new[3],
        out_new[1],
        out_new[2],
        *gate_up_new,
        down_grad,
        down_new[0],
        down_new[1],
        down_new[2],
        down_new[0].astype(low),
        gains_grad,
        gains_new[3],
        gains_new[1],
        gains_new[2],
    )


def solution(mesh):
    tokens = P(("seq", "tp"), None)
    rows = P("seq", "tp")
    columns = P("tp", "seq")
    pair = P(None, "seq", "tp")
    return jax.shard_map(
        local,
        mesh=mesh,
        in_specs=(
            (tokens,) * 2 + (P("seq"),) * 2 + (rows,) * 3 + (columns,) * 3 + (pair,) * 3
            + (columns,) * 3 + (P(),) * 3
        ),
        out_specs=(
            (tokens,) * 2 + (rows,) * 5 + (columns,) * 4 + (pair,) * 5 + (columns,) * 5 + (P(),) * 4
        ),
        check_vma=False,
    )
```

time: 1450 us -> 782 us (0.54)
  waiting for transfers between devices: 806 us -> 247 us
  matrix products: 414 us -> 83.1 us
  Pallas kernels: 0 us -> 210 us
  starting transfers between devices: 16.4 us -> 128 us
  other arithmetic: 99.6 us -> 45.5 us
  blocking collectives: 46.4 us -> 0 us
  local copies, waits for them, and re-layouts: 48.9 us -> 32.5 us
    all_gather x8 -> x5, waiting for transfers between devices: 446 us -> 16.7 us  [the longest x1 12.3 us: local(): w_gate_up = lax.all_gather(low_gate_up, 'seq', axis=0, tiled=True)]
    reduce_scatter x8 -> x3, waiting for transfers between devices: 357 us -> 0.02 us  [the longest x1 0.02 us: local(): lax.psum_scatter(out_grad, 'seq', scatter_dimension=1, tiled=True)]
    dot_general x30 -> x7, matrix products: 414 us -> 83.1 us  [the longest x4 50.7 us: contract_rows(): lax.dot_general(left, right, ROWS_BY_ROWS, preferred_element_type=jnp.flo...]
    pallas_call x0 -> x19, Pallas kernels: none -> 210 us  [the longest x2 43.5 us: attend_back(): pl.pallas_call(functools.partial(attend_back_kernel, tk), grid_spec=pltpu...]
    ppermute x6 -> x50, waiting for transfers between devices: 2.12 us -> 209 us  [the longest x18 134 us: shifted(): lax.ppermute(block, axis, [(i, i + distance) for i in range(size) if 0 <=...]
    ppermute x6 -> x50, starting transfers between devices: 15 us -> 119 us  [the longest x18 54.2 us: shifted(): lax.ppermute(block, axis, [(i, i + distance) for i in range(size) if 0 <=...]
    psum x1 -> x0, blocking collectives: 46.4 us -> none  [local(): lax.psum(jnp.stack([gain_one_grad, gain_two_grad]), ('seq', 'tp'))]
    reduce_sum x6 -> x1, other arithmetic: 45.6 us -> 0.14 us  [sum_parts(): return jnp.sum(parts.astype(jnp.float32), axis=0)]
  transfers between devices with their start and end apart: 22 -> 60, of which waited for: 14 -> 33; matrix products, arithmetic and copies ran while one was open for 32% -> 17% of each run, Pallas kernels for 0% -> 22%
where the time goes in v1:
time: 782 us; the launch traced here: 766 us
  waiting for transfers between devices  247 us (32%)
  Pallas kernels  210 us (27%)
  starting transfers between devices  128 us (16%)
  matrix products  83.1 us (11%)
  other arithmetic  45.5 us (6%)
  local copies, waits for them, and re-layouts  32.5 us (4%)
  between operations  20.6 us (3%)
    ppermute x18, waiting for transfers between devices, shifted(): lax.ppermute(block, axis, [(i, i + distance) for i in range(size) if 0 <=...  134 us
    ppermute x18, starting transfers between devices, shifted(): lax.ppermute(block, axis, [(i, i + distance) for i in range(size) if 0 <=...  54.2 us
    dot_general x4, matrix products, contract_rows(): lax.dot_general(left, right, ROWS_BY_ROWS, preferred_element_type=jnp.flo...  50.7 us
    pallas_call x2, Pallas kernels, attend_back(): pl.pallas_call(functools.partial(attend_back_kernel, tk), grid_spec=pltpu...  43.5 us
    pallas_call x3, Pallas kernels, blocks_times(): pl.pallas_call(blocks_kernel, grid_spec=pltpu.PrefetchScalarGridSpec(num_...  38.4 us
    ppermute x9, starting transfers between devices, hop(): lax.ppermute(to_high, self.axis, [(i, i + 1) for i in range(step)])  28.5 us
    pallas_call x1, Pallas kernels, gate_and_back(): pl.pallas_call(gate_kernel, grid=(units // wide, tokens // tile), in_spec...  26.9 us
    unnamed x159, local copies, waits for them, and re-layouts  24.6 us
  transfers between devices with their start and end apart: 60, of which 33 were waited for; matrix products, arithmetic and copies ran while one was open for 17% of the time, Pallas kernels for 22%

profile of v1, /device:TPU:10, one launch (start us, length us, event | category | flops | bytes accessed | tf_op | source)
XLA Modules:
  0.0 766.5 jit_solution(14557370036341376355)
XLA Ops:
  28.1 10.9 %collective-permute-done.1.refs_4_ = bf16[256,2048]{1,0:T(8,128)(2,1)} collective-permute-done((bf16[256,2048]{1,0:T(8,128)(2,1)S(1)}, bf16[256,2048]{1,0:T(8,128)(2,1)}, u32[]{:S(2)}, u32[]{:S(2)}) %collective-permute-start.1) | collective-permute-done | bytes 1048608 | tf_op jit(solution)/shard_map/ppermute | solution.py:50
  47.0 19.9 %collective-permute-done.2.refs_2_ = bf16[256,2048]{1,0:T(8,128)(2,1)S(1)} collective-permute-done((bf16[256,2048]{1,0:T(8,128)(2,1)}, bf16[256,2048]{1,0:T(8,128)(2,1)S(1)}, u32[]{:S(2)}, u32[]{:S(2)}) %collective-permute-start.2) | collective-permute-done | bytes 1048608 | tf_op jit(solution)/shard_map/ppermute | solution.py:50
  77.9 17.9 %collective-permute-done.4.refs_3_ = bf16[256,2048]{1,0:T(8,128)(2,1)S(1)} collective-permute-done((bf16[256,2048]{1,0:T(8,128)(2,1)S(1)}, bf16[256,2048]{1,0:T(8,128)(2,1)S(1)}, u32[]{:S(2)}, u32[]{:S(2)}) %collective-permute-start.4) | collective-permute-done | bytes 1048608 | tf_op jit(solution)/shard_map/ppermute | solution.py:50
  108.3 10.8 %project_qkv.1 = (bf16[1024,2048]{1,0:T(8,128)(2,1)}, bf16[1024,2048]{1,0:T(8,128)(2,1)}, bf16[1024,512]{1,0:T(8,128)(2,1)S(1)}, bf16[1024,256]{1,0:T(8,128)(2,1)S(1)}) custom-call(s32[1]{0:T(128)} %bitcast.1.rank_ref, bf16[2048,768]{1,0:T(8,128)(2,1)} %all-gather.6.cloned.1.call-done.w_ref.refs_4_, f32[1,2048]{1,0:T(1,128)S(1)} %get-tuple-element.485.gain_ref, ...), custom_call_target="tpu_custom_call" | custom-call | flops 10350000128 | bytes 27000000 | tf_op jit(solution)/shard_map/project_qkv/pallas_call | solution.py:256
  154.0 13.4 %collective-permute-done.10.refs_2_ = bf16[256,2048]{1,0:T(8,128)(2,1)S(1)} collective-permute-done((bf16[256,2048]{1,0:T(8,128)(2,1)}, bf16[256,2048]{1,0:T(8,128)(2,1)S(1)}, u32[]{:S(2)}, u32[]{:S(2)}) %collective-permute-start.10) | collective-permute-done | bytes 1048608 | tf_op jit(solution)/shard_map/ppermute | solution.py:50
  213.4 13.9 %convolution_convert_fusion.4.dh_ref = bf16[1024,2048]{1,0:T(8,128)(2,1)} fusion(bf16[1024,2048]{1,0:T(8,128)(2,1)} %place_rows.1, bf16[2048,2048]{1,0:T(8,128)(2,1)} %all-gather.8.cloned.1.call-done), kind=kOutput, calls=%fused_computation.4 | convolution fusion | flops 8592031744 | bytes 16777216 | tf_op jit(solution)/shard_map/dot_general | solution.py:45
  239.4 21.5 %collective-permute-done.16.refs_2_ = bf16[1024,512]{1,0:T(8,128)(2,1)S(1)} collective-permute-done((bf16[1024,512]{1,0:T(8,128)(2,1)}, bf16[1024,512]{1,0:T(8,128)(2,1)S(1)}, u32[]{:S(2)}, u32[]{:S(2)}) %collective-permute-start.16) | collective-permute-done | bytes 1048608 | tf_op jit(solution)/shard_map/ppermute | solution.py:50
  272.9 17.4 %collective-permute-done.18.refs_3_ = bf16[1024,512]{1,0:T(8,128)(2,1)} collective-permute-done((bf16[1024,512]{1,0:T(8,128)(2,1)S(1)}, bf16[1024,512]{1,0:T(8,128)(2,1)}, u32[]{:S(2)}, u32[]{:S(2)}) %collective-permute-start.18) | collective-permute-done | bytes 1048608 | tf_op jit(solution)/shard_map/ppermute | solution.py:50
  295.9 17.5 %project_out.1 = (f32[1024,2048]{1,0:T(8,128)}, bf16[1024,2048]{1,0:T(8,128)(2,1)}, bf16[256,2048]{1,0:T(8,128)(2,1)S(1)}) custom-call(s32[1]{0:T(128)} %bitcast.1.rank_ref, bf16[1024,2048]{1,0:T(8,128)(2,1)} %get-tuple-element.326.x_ref, bf16[2048,2048]{1,0:T(8,128)(2,1)} %all-gather.12.cloned.1.call-done.w_ref, f32[1,2048]{1,0:T(1,128)S(1)} %get-tuple-element.484.gain_ref, ...), custom_call_target="tpu_custom_call" | custom-call | flops 17250000896 | bytes 45000000 | tf_op jit(solution)/shard_map/project_out/pallas_call | solution.py:641
  313.4 12.3 %all-gather.14.cloned.1.call-done.w_ref.refs_2_ = bf16[2048,4096]{1,0:T(8,128)(2,1)} async-done(((bf16[256,4096]{1,0:T(8,128)(2,1)}), bf16[2048,4096]{1,0:T(8,128)(2,1)}) %all-gather.14.cloned.1.call-update) | async-done | bytes 16777232 | tf_op jit(solution)/shard_map/all_gather | solution.py:976
  325.7 26.9 %gate_and_back.1 = (bf16[1024,2048]{1,0:T(8,128)(2,1)S(1)}, bf16[1024,4096]{1,0:T(8,128)(2,1)}) custom-call(bf16[1024,2048]{1,0:T(8,128)(2,1)} %get-tuple-element.358.n_ref, bf16[2048,4096]{1,0:T(8,128)(2,1)} %all-gather.14.cloned.1.call-done.w_ref.refs_2_, bf16[1024,2048]{1,0:T(8,128)(2,1)} %convolution_convert_fusion.4.dh_ref), custom_call_target="tpu_custom_call" | custom-call | flops 31050000384 | bytes 81000000 | tf_op jit(solution)/shard_map/gate_and_back/pallas_call | solution.py:679
  352.7 17.2 %blocks_times.3 = (bf16[256,2048]{1,0:T(8,128)(2,1)}, bf16[256,2048]{1,0:T(8,128)(2,1)S(1)}) custom-call(s32[2]{0:T(128)S(1)} %get-tuple-element.496.chunks_ref, bf16[1024,4096]{1,0:T(8,128)(2,1)} %get-tuple-element.357.refs_0_.refs_1_, bf16[1024,4096]{1,0:T(8,128)(2,1)} %get-tuple-element.357.refs_0_.refs_1_, ...), custom_call_target="tpu_custom_call" | custom-call | flops 17250000896 | bytes 45000000 | tf_op jit(solution)/shard_map/blocks_times/pallas_call | solution.py:716
  372.9 11.4 %convolution_convert_fusion.2 = bf16[2048,2048]{1,0:T(8,128)(2,1)} fusion(bf16[1024,2048]{1,0:T(8,128)(2,1)S(1)} %get-tuple-element.361, bf16[1024,2048]{1,0:T(8,128)(2,1)S(1)} %copy-done.77), kind=kOutput, calls=%fused_computation.2 | convolution fusion | flops 8594128896 | bytes 16777216 | tf_op jit(solution)/shard_map/dot_general | solution.py:41
  384.3 14.9 %blocks_times.4 = (bf16[256,2048]{1,0:T(8,128)(2,1)S(1)}, bf16[256,2048]{1,0:T(8,128)(2,1)S(1)}) custom-call(s32[2]{0:T(128)S(1)} %get-tuple-element.495.chunks_ref, bf16[1024,4096]{1,0:T(8,128)(2,1)} %get-tuple-element.357.refs_0_.refs_1_, bf16[1024,4096]{1,0:T(8,128)(2,1)} %get-tuple-element.357.refs_0_.refs_1_, ...), custom_call_target="tpu_custom_call" | custom-call | flops 17250000896 | bytes 45000000 | tf_op jit(solution)/shard_map/blocks_times/pallas_call | solution.py:716
  413.1 25.2 %convolution_convert_fusion = bf16[2048,4096]{1,0:T(8,128)(2,1)} fusion(bf16[1024,2048]{1,0:T(8,128)(2,1)S(1)} %copy-done.78, bf16[1024,4096]{1,0:T(8,128)(2,1)} %get-tuple-element.357.refs_0_.refs_1_), kind=kOutput, calls=%fused_computation | convolution fusion | flops 17188257792 | bytes 29360128 | tf_op jit(solution)/shard_map/dot_general | solution.py:41
  448.3 12.7 %convolution_convert_fusion.3 = bf16[1024,2048]{1,0:T(8,128)(2,1)} fusion(bf16[1024,2048]{1,0:T(8,128)(2,1)S(1)} %copy-done.44, bf16[2048,2048]{1,0:T(8,128)(2,1)} %all-gather.8.cloned.1.call-done), kind=kOutput, calls=%fused_computation.3 | convolution fusion | flops 8592031744 | bytes 16777216 | tf_op jit(solution)/shard_map/dot_general | solution.py:1028
  498.0 12.4 %all-to-all-done = bf16[256,4,512]{2,0,1:T(8,128)(2,1)S(1)} async-done(((bf16[256,4,512]{2,0,1:T(8,128)(2,1)}), bf16[256,4,512]{2,0,1:T(8,128)(2,1)S(1)}, u32[]{:S(2)}, u32[]{:S(2)}) %all-to-all-start) | async-done | bytes 1048608 | tf_op jit(solution)/shard_map/all_to_all | solution.py:1040
  518.2 21.9 %attend_back.2 = (bf16[1024,256]{1,0:T(8,128)(2,1)S(1)}, bf16[1024,128]{1,0:T(8,128)(2,1)S(1)}, bf16[1024,128]{1,0:T(8,128)(2,1)S(1)}, f32[1024,128]{1,0:T(8,128)S(1)}) custom-call(s32[1024]{0:T(1024)S(1)} %copy-done.13, bf16[1024,512]{1,0:T(8,128)(2,1)S(1)} %copy-done.48, bf16[1024,512]{1,0:T(8,128)(2,1)} %bitcast.60, bf16[1024,256]{1,0:T(8,128)(2,1)S(1)} %copy-done.9, ...), custom_call_target="tpu_custom_call" | custom-call | flops 32199999488 | bytes 84000000 | tf_op jit(solution)/shard_map/attend_back/pallas_call | solution.py:536
  557.2 21.6 %attend_back.3 = (bf16[1024,256]{1,0:T(8,128)(2,1)S(1)}, bf16[1024,128]{1,0:T(8,128)(2,1)S(1)}, bf16[1024,128]{1,0:T(8,128)(2,1)S(1)}, f32[1024,128]{1,0:T(8,128)S(1)}) custom-call(s32[1024]{0:T(1024)S(1)} %copy-done.13, bf16[1024,512]{1,0:T(8,128)(2,1)S(1)} %copy-done.48, bf16[1024,512]{1,0:T(8,128)(2,1)} %bitcast.61, bf16[1024,256]{1,0:T(8,128)(2,1)S(1)} %copy-done.7, ...), custom_call_target="tpu_custom_call" | custom-call | flops 32199999488 | bytes 84000000 | tf_op jit(solution)/shard_map/attend_back/pallas_call | solution.py:536
  638.9 11.7 %collective-permute-done.36 = bf16[256,2048]{1,0:T(8,128)(2,1)S(1)} collective-permute-done((bf16[256,2048]{1,0:T(8,128)(2,1)S(1)}, bf16[256,2048]{1,0:T(8,128)(2,1)S(1)}, u32[]{:S(2)}, u32[]{:S(2)}) %collective-permute-start.36) | collective-permute-done | bytes 1048608 | tf_op jit(solution)/shard_map/ppermute | solution.py:123
  667.3 13.7 %adam_interleaved.1 = (f32[2,256,2048]{2,1,0:T(8,128)}, f32[2,256,2048]{2,1,0:T(8,128)}, f32[2,256,2048]{2,1,0:T(8,128)}, f32[2,256,2048]{2,1,0:T(8,128)}, bf16[2,256,2048]{2,1,0:T(8,128)(2,1)}) custom-call(bf16[256,4096]{1,0:T(8,128)(2,1)S(1)} %copy-done.16, f32[2,256,2048]{2,1,0:T(8,128)} %w_ref.3, f32[2,256,2048]{2,1,0:T(8,128)} %m_ref.1, ...), custom_call_target="tpu_custom_call" | custom-call | flops 14949999616 | bytes 39000000 | tf_op jit(solution)/shard_map/adam_interleaved/pallas_call | solution.py:880
  681.0 14.7 %collective-permute-done.44 = bf16[2,256,768]{2,1,0:T(8,128)(2,1)S(1)} collective-permute-done((bf16[2,256,768]{2,1,0:T(8,128)(2,1)S(1)}, bf16[2,256,768]{2,1,0:T(8,128)(2,1)S(1)}, u32[]{:S(2)}, u32[]{:S(2)}) %collective-permute-start.44) | collective-permute-done | bytes 786464 | tf_op jit(solution)/shard_map/ppermute | solution.py:153
  705.9 19.8 %collective-permute-done.47 = f32[2,2048]{1,0:T(2,128)S(1)} collective-permute-done((f32[2,2048]{1,0:T(2,128)S(1)}, f32[2,2048]{1,0:T(2,128)S(1)}, u32[]{:S(2)}, u32[]{:S(2)}) %collective-permute-start.47) | collective-permute-done | bytes 16416 | tf_op jit(solution)/shard_map/ppermute | solution.py:162
  748.2 7.9 %all-to-all-done.1 = bf16[4,512,256]{2,1,0:T(8,128)(2,1)S(1)} async-done(((bf16[4,512,256]{2,1,0:T(8,128)(2,1)}), bf16[4,512,256]{2,1,0:T(8,128)(2,1)S(1)}, u32[]{:S(2)}, u32[]{:S(2)}) %all-to-all-start.1) | async-done | bytes 1048608 | tf_op jit(solution)/shard_map/all_to_all | solution.py:140
  (335 shorter events, 358.0 us)
Async XLA Ops:
  7.2 92.7 %all-gather.6.cloned.1.call-start = ((), (), s32[]{:S(2)}) async-start(), calls=%async_computation.5 | async-start | bytes 3538944 | tf_op jit(solution)/shard_map/all_gather | solution.py:946
  9.3 116.6 %all-gather.8.cloned.1.call-start = ((), (), s32[]{:S(2)}) async-start(), calls=%async_computation.6 | async-start | bytes 9437184 | tf_op jit(solution)/shard_map/all_gather | solution.py:947
  12.1 158.6 %all-gather.10.cloned.1.call-start = ((), (), s32[]{:S(2)}) async-start(), calls=%async_computation.7 | async-start | bytes 1310720 | tf_op jit(solution)/shard_map/all_gather | solution.py:965
  125.9 28.1 %collective-permute-start.9 = (bf16[1024,256]{1,0:T(8,128)(2,1)S(1)}, bf16[1024,256]{1,0:T(8,128)(2,1)}, u32[]{:S(2)}, u32[]{:S(2)}) collective-permute-start(bf16[1024,256]{1,0:T(8,128)(2,1)S(1)} %get-tuple-element.278.here), channel_id=1, source_target_pairs={{0,4},{4,8},{8,12},{16,20},{20,24},{24,28},{1,5},{5,9},{9,13},{17,... | collective-permute-start | bytes 1572872 | tf_op jit(solution)/shard_map/ppermute | solution.py:174
  129.1 104.4 %all-gather.12.cloned.1.call-start = ((), (), s32[]{:S(2)}) async-start(), calls=%async_computation.8 | async-start | bytes 9437184 | tf_op jit(solution)/shard_map/all_gather | solution.py:975
  129.2 38.3 %collective-permute-start.10 = (bf16[256,2048]{1,0:T(8,128)(2,1)}, bf16[256,2048]{1,0:T(8,128)(2,1)S(1)}, u32[]{:S(2)}, u32[]{:S(2)}) collective-permute-start(bf16[256,2048]{1,0:T(8,128)(2,1)} %collective-permute-done.6.refs_1_), channel_id=1, source_target_pairs={{0,1},{1,2},{2,3},{4,5},{5,6},{6,7},{8,9},{9,10},{10,11},{12,13},{... | collective-permute-start | bytes 3145736 | tf_op jit(solution)/shard_map/ppermute | solution.py:50
  132.2 38.4 %collective-permute-start.11 = (bf16[256,2048]{1,0:T(8,128)(2,1)}, bf16[256,2048]{1,0:T(8,128)(2,1)}, u32[]{:S(2)}, u32[]{:S(2)}) collective-permute-start(bf16[256,2048]{1,0:T(8,128)(2,1)} %collective-permute-done.7.refs_4_), channel_id=1, source_target_pairs={{1,0},{2,1},{3,2},{5,4},{6,5},{7,6},{9,8},{10,9},{11,10},{13,12},{... | collective-permute-start | bytes 3145736 | tf_op jit(solution)/shard_map/ppermute | solution.py:50
  170.7 155.1 %all-gather.14.cloned.1.call-start = ((), (), s32[]{:S(2)}) async-start(), calls=%async_computation.9 | async-start | bytes 18874368 | tf_op jit(solution)/shard_map/all_gather | solution.py:976
  171.3 339.2 %reduce-scatter.4.cloned.1.call-start = ((), (), s32[]{:S(2)}) async-start(), calls=%async_computation.10 | async-start | bytes 9437184 | tf_op jit(solution)/shard_map/reduce_scatter | solution.py:1022
  369.9 30.3 %collective-permute-start.21 = (bf16[256,2048]{1,0:T(8,128)(2,1)}, bf16[256,2048]{1,0:T(8,128)(2,1)}, u32[]{:S(2)}, u32[]{:S(2)}) collective-permute-start(bf16[256,2048]{1,0:T(8,128)(2,1)} %get-tuple-element.344), channel_id=1, source_target_pairs={{3,2},{7,6},{11,10},{15,14},{19,18},{23,22},{27,26},{31,30}} | collective-permute-start | bytes 3145736 | tf_op jit(solution)/shard_map/ppermute | solution.py:124
  371.6 28.6 %collective-permute-start.20 = (bf16[256,2048]{1,0:T(8,128)(2,1)}, bf16[256,2048]{1,0:T(8,128)(2,1)}, u32[]{:S(2)}, u32[]{:S(2)}) collective-permute-start(bf16[256,2048]{1,0:T(8,128)(2,1)} %get-tuple-element.344), channel_id=1, source_target_pairs={{0,1},{4,5},{8,9},{12,13},{16,17},{20,21},{24,25},{28,29}} | collective-permute-start | bytes 3145736 | tf_op jit(solution)/shard_map/ppermute | solution.py:123
  400.2 221.8 %reduce-scatter.6.cloned.1.call-start = ((), (), s32[]{:S(2)}) async-start(), calls=%async_computation.11 | async-start | bytes 18874368 | tf_op jit(solution)/shard_map/reduce_scatter | solution.py:1026
  406.9 31.5 %collective-permute-start.23 = (bf16[256,2048]{1,0:T(8,128)(2,1)}, bf16[256,2048]{1,0:T(8,128)(2,1)}, u32[]{:S(2)}, u32[]{:S(2)}) collective-permute-start(bf16[256,2048]{1,0:T(8,128)(2,1)} %get-tuple-element.478), channel_id=1, source_target_pairs={{2,1},{3,2},{6,5},{7,6},{10,9},{11,10},{14,13},{15,14},{18,17},{19... | collective-permute-start | bytes 3145736 | tf_op jit(solution)/shard_map/ppermute | solution.py:124
  408.2 30.2 %collective-permute-start.22 = (bf16[256,2048]{1,0:T(8,128)(2,1)}, bf16[256,2048]{1,0:T(8,128)(2,1)}, u32[]{:S(2)}, u32[]{:S(2)}) collective-permute-start(bf16[256,2048]{1,0:T(8,128)(2,1)} %get-tuple-element.479), channel_id=1, source_target_pairs={{0,1},{1,2},{4,5},{5,6},{8,9},{9,10},{12,13},{13,14},{16,17},{17,1... | collective-permute-start | bytes 3145736 | tf_op jit(solution)/shard_map/ppermute | solution.py:123
  488.3 243.6 %reduce-scatter.8.cloned.1.call-start = ((), (), s32[]{:S(2)}) async-start(), calls=%async_computation.12 | async-start | bytes 9437184 | tf_op jit(solution)/shard_map/reduce_scatter | solution.py:1043
  542.4 36.5 %collective-permute-start.29 = (bf16[1024,128]{1,0:T(8,128)(2,1)S(1)}, bf16[1024,128]{1,0:T(8,128)(2,1)S(1)}, u32[]{:S(2)}, u32[]{:S(2)}) collective-permute-start(bf16[1024,128]{1,0:T(8,128)(2,1)S(1)} %get-tuple-element.384), channel_id=1, source_target_pairs={{8,0},{12,4},{24,16},{28,20},{9,1},{13,5},{25,17},{29,21},{10,2},{... | collective-permute-start | bytes 786440 | tf_op jit(solution)/shard_map/ppermute | solution.py:174
  545.0 33.9 %collective-permute-start.28 = (bf16[1024,128]{1,0:T(8,128)(2,1)S(1)}, bf16[1024,128]{1,0:T(8,128)(2,1)S(1)}, u32[]{:S(2)}, u32[]{:S(2)}) collective-permute-start(bf16[1024,128]{1,0:T(8,128)(2,1)S(1)} %get-tuple-element.385), channel_id=1, source_target_pairs={{4,0},{8,4},{12,8},{20,16},{24,20},{28,24},{5,1},{9,5},{13,9},{21,... | collective-permute-start | bytes 786440 | tf_op jit(solution)/shard_map/ppermute | solution.py:174
  552.4 29.0 %collective-permute-start.30 = (bf16[256,2048]{1,0:T(8,128)(2,1)S(1)}, bf16[256,2048]{1,0:T(8,128)(2,1)S(1)}, u32[]{:S(2)}, u32[]{:S(2)}) collective-permute-start(bf16[256,2048]{1,0:T(8,128)(2,1)S(1)} %get-tuple-element.473), channel_id=1, source_target_pairs={{0,1},{1,2},{4,5},{5,6},{8,9},{9,10},{12,13},{13,14},{16,17},{17,1... | collective-permute-start | bytes 3145736 | tf_op jit(solution)/shard_map/ppermute | solution.py:123
  583.6 27.9 %collective-permute-start.35 = (bf16[256,2048]{1,0:T(8,128)(2,1)}, bf16[256,2048]{1,0:T(8,128)(2,1)}, u32[]{:S(2)}, u32[]{:S(2)}) collective-permute-start(bf16[256,2048]{1,0:T(8,128)(2,1)} %get-tuple-element.474), channel_id=1, source_target_pairs={{1,0},{2,1},{3,2},{5,4},{6,5},{7,6},{9,8},{10,9},{11,10},{13,12},{... | collective-permute-start | bytes 3145736 | tf_op jit(solution)/shard_map/ppermute | solution.py:124
  657.4 38.5 %collective-permute-start.39 = (bf16[256,2048]{1,0:T(8,128)(2,1)S(1)}, bf16[256,2048]{1,0:T(8,128)(2,1)S(1)}, u32[]{:S(2)}, u32[]{:S(2)}) collective-permute-start(bf16[256,2048]{1,0:T(8,128)(2,1)S(1)} %get-tuple-element.476), channel_id=1, source_target_pairs={{2,1},{3,2},{6,5},{7,6},{10,9},{11,10},{14,13},{15,14},{18,17},{19... | collective-permute-start | bytes 3145736 | tf_op jit(solution)/shard_map/ppermute | solution.py:124
  658.7 37.3 %collective-permute-start.38 = (bf16[256,2048]{1,0:T(8,128)(2,1)S(1)}, bf16[256,2048]{1,0:T(8,128)(2,1)S(1)}, u32[]{:S(2)}, u32[]{:S(2)}) collective-permute-start(bf16[256,2048]{1,0:T(8,128)(2,1)S(1)} %get-tuple-element.477), channel_id=1, source_target_pairs={{0,1},{1,2},{4,5},{5,6},{8,9},{9,10},{12,13},{13,14},{16,17},{17,1... | collective-permute-start | bytes 3145736 | tf_op jit(solution)/shard_map/ppermute | solution.py:123
  665.5 30.2 %collective-permute-start.44 = (bf16[2,256,768]{2,1,0:T(8,128)(2,1)S(1)}, bf16[2,256,768]{2,1,0:T(8,128)(2,1)S(1)}, u32[]{:S(2)}, u32[]{:S(2)}) collective-permute-start(bf16[2,256,768]{2,1,0:T(8,128)(2,1)S(1)} %dynamic-slice_bitcast_fusion.1), channel_id=1, source_target_pairs={{0,8},{4,12},{8,0},{12,4},{16,24},{20,28},{24,16},{28,20},{1,9},{5... | collective-permute-start | bytes 2359304 | tf_op jit(solution)/shard_map/ppermute | solution.py:153
  697.5 34.4 %collective-permute-start.46 = (bf16[256,2048]{1,0:T(8,128)(2,1)}, bf16[256,2048]{1,0:T(8,128)(2,1)S(1)}, u32[]{:S(2)}, u32[]{:S(2)}) collective-permute-start(bf16[256,2048]{1,0:T(8,128)(2,1)} %get-tuple-element.480), channel_id=1, source_target_pairs={{1,0},{2,1},{3,2},{5,4},{6,5},{7,6},{9,8},{10,9},{11,10},{13,12},{... | collective-permute-start | bytes 3145736 | tf_op jit(solution)/shard_map/ppermute | solution.py:124
  699.4 32.5 %collective-permute-start.45 = (bf16[256,2048]{1,0:T(8,128)(2,1)}, bf16[256,2048]{1,0:T(8,128)(2,1)S(1)}, u32[]{:S(2)}, u32[]{:S(2)}) collective-permute-start(bf16[256,2048]{1,0:T(8,128)(2,1)} %get-tuple-element.481), channel_id=1, source_target_pairs={{0,1},{1,2},{2,3},{4,5},{5,6},{6,7},{8,9},{9,10},{10,11},{12,13},{... | collective-permute-start | bytes 3145736 | tf_op jit(solution)/shard_map/ppermute | solution.py:123
  (115 other events, 1897.6 us)
Sparse Core Ops, SparseCore 0:
  10.5 33.4 all-gather.5
  46.5 55.9 all-gather.7
  129.2 40.9 all-gather.9
  172.0 61.4 all-gather.11
  235.8 89.8 all-gather.13
  400.4 73.2 reduce-scatter.3
  477.6 127.0 reduce-scatter.5
  608.6 86.7 reduce-scatter.7

commit v2 on v1

--- a/solution.py
+++ b/solution.py
@@ -45,13 +45,6 @@
     return lax.dot_general(left, right, COLS_BY_COLS, preferred_element_type=jnp.float32)
 
 
-def shifted(block, axis, distance):
-    size = lax.axis_size(axis)
-    return lax.ppermute(
-        block, axis, [(i, i + distance) for i in range(size) if 0 <= i + distance < size]
-    )
-
-
 class LineGather:
     def __init__(self, block, axis):
         self.axis = axis
@@ -64,8 +57,11 @@
         return len(self.from_low) - 1
 
     def hop(self):
-        self.from_low.append(shifted(self.from_low[-1], self.axis, 1))
-        self.from_high.append(shifted(self.from_high[-1], self.axis, -1))
+        size, passed = self.hops + 1, self.step
+        up = [(i, i + 1) for i in range(passed, size - 1)]
+        down = [(i, i - 1) for i in range(1, size - passed)]
+        self.from_low.append(lax.ppermute(self.from_low[-1], self.axis, up))
+        self.from_high.append(lax.ppermute(self.from_high[-1], self.axis, down))
 
     @property
     def moving(self):
@@ -144,24 +140,27 @@
     return jnp.sum(parts.astype(jnp.float32), axis=0)
 
 
-def halving_hop(blocks, axis, hop):
+def sum_by_swaps(block, axis):
+    size = lax.axis_size(axis)
+    hop = 1
+    while hop < size:
+        block = block + lax.ppermute(block, axis, [(i, i ^ hop) for i in range(size)])
+        hop *= 2
+    return block
+
+
+def sum_at_once(block, axis):
+    size = lax.axis_size(axis)
+    came = [block]
+    for distance in range(1, size):
+        route = [(i, (i + distance) % size) for i in range(size)]
+        came.append(lax.ppermute(block, axis, route))
+    came = jnp.stack(came)
     rank = lax.axis_index(axis)
-    pairs = blocks.reshape(blocks.shape[0] // 2, 2, *blocks.shape[1:])
-    mine = (rank // hop) % 2
-    keep = lax.dynamic_index_in_dim(pairs, mine, axis=1, keepdims=False)
-    send = lax.dynamic_index_in_dim(pairs, 1 - mine, axis=1, keepdims=False)
-    came = lax.ppermute(send, axis, [(i, i ^ hop) for i in range(lax.axis_size(axis))])
-    return (keep.astype(jnp.float32) + came.astype(jnp.float32)).astype(blocks.dtype)
-
-
-def sum_everywhere(block, axes):
-    for axis in axes:
-        size = lax.axis_size(axis)
-        hop = 1
-        while hop < size:
-            block = block + lax.ppermute(block, axis, [(i, i ^ hop) for i in range(size)])
-            hop *= 2
-    return block
+    total = lax.dynamic_index_in_dim(came, rank, keepdims=False)
+    for peer in range(1, size):
+        total = total + lax.dynamic_index_in_dim(came, (rank - peer) % size, keepdims=False)
+    return total
 
 
 def along_sequence(block, distance, tokens):
@@ -606,57 +605,92 @@
     )(cos, sin, *flat)
 
 
-def out_kernel(rank_ref, x_ref, w_ref, gain_ref, *refs):
-    *pieces, mid_ref, normed_ref, own_ref, heads = refs
+def out_step_kernel(distances, last, rank_ref, *refs):
+    refs = list(refs)
+    base_ref = refs.pop(0)
+    gain_ref = refs.pop(0) if last else None
+    total = base_ref[...].astype(jnp.float32)
+    for distance, count in distances:
+        piece = refs.pop(0)[...]
+        if count == 2:
+            piece = jnp.where(rank_ref[0] >= distance, piece, refs.pop(0)[...])
+        total = total + jnp.dot(piece, refs.pop(0)[...], preferred_element_type=jnp.float32)
+    refs[0][...] = total
+    if last:
+        inverse = lax.rsqrt(jnp.mean(total * total, axis=1, keepdims=True) + NORM_EPS)
+        refs[1][...] = (total * inverse * gain_ref[...]).astype(jnp.bfloat16)
+
+
+def out_step(base, pieces, rank, weight, gain=None, tile=256):
+    tokens, width = base.shape
+    depth = pieces[0][1][0].shape[1]
+    last = gain is not None
+    slots = weight.shape[0] // depth
+
+    def rows(wide):
+        return pl.BlockSpec((tile, wide), lambda i, r: (i, 0))
+
+    def slot_rows(distance, count):
+        def index(i, r):
+            slot = r[0] - distance
+            if count == 2:
+                slot = jnp.where(r[0] >= distance, slot, r[0] + distance)
+            return jnp.clip(slot, 0, slots - 1), 0
+
+        return pl.BlockSpec((depth, width), index)
+
+    operands, specs = [base], [rows(width)]
+    if last:
+        operands.append(gain[None])
+        specs.append(pl.BlockSpec((1, width), lambda i, r: (0, 0)))
+    for distance, blocks in pieces:
+        operands += [*blocks, weight]
+        specs += [rows(depth)] * len(blocks) + [slot_rows(distance, len(blocks))]
+    outs = [jax.ShapeDtypeStruct((tokens, width), jnp.float32)]
+    if last:
+        outs.append(jax.ShapeDtypeStruct((tokens, width), jnp.bfloat16))
+    distances = tuple((distance, len(blocks)) for distance, blocks in pieces)
+    made = pl.pallas_call(
+        functools.partial(out_step_kernel, distances, last),
+        grid_spec=pltpu.PrefetchScalarGridSpec(
+            num_scalar_prefetch=1,
+            grid=(tokens // tile,),
+            in_specs=specs,
+            out_specs=[rows(width)] * len(outs),
+        ),
+        out_shape=outs,
+        compiler_params=pltpu.CompilerParams(vmem_limit_bytes=VMEM_LIMIT),
+        cost_estimate=cost(7),
+        name="out_step",
+    )(jnp.reshape(rank, (1,)).astype(jnp.int32), *operands)
+    return made if last else made[0]
+
+
+def own_kernel(rank_ref, *refs):
+    *pieces, out_ref = refs
+
+    def put(piece):
+        out_ref[...] = piece[...]
+
+    pick_piece(pieces, rank_ref[0] - pl.program_id(0), put)
+
+
+def own_rows_of_heads(pieces, rank, own):
     size = (len(pieces) + 1) // 2
     columns = pieces[0].shape[1]
-    for slot in range(size):
-
-        def put(piece, slot=slot):
-            heads[:, slot * columns : (slot + 1) * columns] = piece[...]
-
-        pick_piece(pieces, rank_ref[0] - slot, put)
-    mid = x_ref[...].astype(jnp.float32) + jnp.dot(
-        heads[...], w_ref[...], preferred_element_type=jnp.float32
-    )
-    mid_ref[...] = mid
-    inverse = lax.rsqrt(jnp.mean(mid * mid, axis=1, keepdims=True) + NORM_EPS)
-    normed_ref[...] = (mid * inverse * gain_ref[...]).astype(jnp.bfloat16)
-
-    @pl.when(pl.program_id(0) == rank_ref[0])
-    def _():
-        own_ref[...] = heads[...]
-
-
-def project_out(x_rows, pieces, rank, weight, gain, own):
-    tokens, width = x_rows.shape
-    columns = weight.shape[0]
-
-    def rows(wide):
-        return pl.BlockSpec((own, wide), lambda i, r: (i, 0))
-
-    def whole(shape):
-        return pl.BlockSpec(shape, lambda i, r: (0, 0))
-
     return pl.pallas_call(
-        out_kernel,
+        own_kernel,
         grid_spec=pltpu.PrefetchScalarGridSpec(
             num_scalar_prefetch=1,
-            grid=(tokens // own,),
-            in_specs=[rows(width), whole(weight.shape), whole((1, width))]
-            + [rows(piece.shape[1]) for piece in pieces],
-            out_specs=[rows(width), rows(width), whole((own, columns))],
-            scratch_shapes=[pltpu.VMEM((own, columns), jnp.bfloat16)],
+            grid=(size,),
+            in_specs=[pl.BlockSpec((own, columns), lambda i, r: (r[0], 0))] * len(pieces),
+            out_specs=pl.BlockSpec((own, columns), lambda i, r: (0, i)),
         ),
-        out_shape=[
-            jax.ShapeDtypeStruct((tokens, width), jnp.float32),
-            jax.ShapeDtypeStruct((tokens, width), jnp.bfloat16),
-            jax.ShapeDtypeStruct((own, columns), jnp.bfloat16),
-        ],
-        compiler_params=pltpu.CompilerParams(vmem_limit_bytes=VMEM_LIMIT),
-        cost_estimate=cost(15),
-        name="project_out",
-    )(jnp.reshape(rank, (1,)).astype(jnp.int32), x_rows, weight, gain[None], *pieces)
+        out_shape=jax.ShapeDtypeStruct((own, columns * size), pieces[0].dtype),
+        compiler_params=pltpu.CompilerParams(vmem_limit_bytes=VMEM_LIMIT),
+        cost_estimate=cost(2),
+        name="own_rows_of_heads",
+    )(jnp.reshape(rank, (1,)).astype(jnp.int32), *pieces)
 
 
 def gate_kernel(n_ref, w_ref, dh_ref, hidden_ref, dgu_ref):
@@ -944,36 +978,35 @@
     low_qkv = qkv_weight.astype(low)
     low_down = down_weight.astype(low)
     w_qkv = lax.all_gather(low_qkv, "seq", axis=0, tiled=True)
-    w_down = lax.all_gather(low_down, "seq", axis=1, tiled=True)
     low_gate_up = round_interleaved(gate_up_weight, wide)
+    w_gate_up = lax.all_gather(low_gate_up, "seq", axis=0, tiled=True)
     low_out = out_weight.astype(low)
     cos, sin = angle_tables(positions)
     back_rows = jnp.broadcast_to(positions[None, :], (8, tokens))
-    side = (low_gate_up, low_out, cos, sin, back_rows)
+    side = (low_down, low_out, cos, sin, back_rows)
     x_line = LineGather(layer_input, "tp")
     for _ in range(x_line.hops):
         x_line.hop()
         x_line.moving, side = close((x_line.moving, side))
     pieces, side, w_qkv, output_grad = close((x_line.pieces, side, w_qkv, output_grad))
-    low_gate_up, low_out, cos, sin, back_rows = side
+    low_down, low_out, cos, sin, back_rows = side
 
     dy_line = LineGather(output_grad, "tp")
     dy_line.hop()
     made = project_qkv(pieces, rank, w_qkv, gain_one, cos, sin)
-    made, dy_line.moving, w_down, low_out = close((made, dy_line.moving, w_down, low_out))
+    made, dy_line.moving, low_out, low_down = close((made, dy_line.moving, low_out, low_down))
     x_rows, normed_one, queries, kv = made
-    out_strip = lax.all_gather(low_out, "tp", axis=0, tiled=True)
+    w_down = lax.all_gather(low_down, "seq", axis=1, tiled=True)
     far = [along_sequence(kv, distance, tokens) for distance in (2, 1)]
     if dy_line.hops > 1:
         dy_line.hop()
     states = [
         attend_here(queries, kv, positions, back_rows, group, 256, 512) for group in range(groups)
     ]
-    far, states, out_strip, queries, low_gate_up, dy_line.moving = close(
-        (far, states, out_strip, queries, low_gate_up, dy_line.moving)
-    )
-    w_out = lax.all_gather(out_strip, "seq", axis=1, tiled=True)
-    w_gate_up = lax.all_gather(low_gate_up, "seq", axis=0, tiled=True)
+    far, states, queries, low_out, w_gate_up, dy_line.moving = close(
+        (far, states, queries, low_out, w_gate_up, dy_line.moving)
+    )
+    out_strip = swap_gather(low_out, "tp")
     for _ in range(2, dy_line.hops):
         dy_line.hop()
     attn, lse = [], []
@@ -983,43 +1016,54 @@
         )
         attn.append(out)
         lse.append(log_total)
-    attn, lse, dy_pieces, w_down, x_rows = close((attn, lse, dy_line.pieces, w_down, x_rows))
+    attn, lse, dy_pieces, w_down, x_rows, out_strip = close(
+        (attn, lse, dy_line.pieces, w_down, x_rows, out_strip)
+    )
+    w_out = lax.all_gather(out_strip.reshape(-1, low_out.shape[1]), "seq", axis=1, tiled=True)
 
     heads_line = LineGather(jnp.concatenate(attn, axis=1), "tp")
+    arrived = [(0, [heads_line.from_low[0]])]
+    total = x_rows
     for index in range(heads_line.hops):
         heads_line.hop()
         if index == 0:
             grad_rows = place_rows(dy_pieces, rank)
             d_hidden = contract_cols(grad_rows, w_down).astype(low)
-            side = (grad_rows, d_hidden, x_rows)
-            heads_line.moving, side, w_out = close((heads_line.moving, side, w_out))
+            heads_line.moving, grad_rows, d_hidden, total = close(
+                (heads_line.moving, grad_rows, d_hidden, total)
+            )
+        elif index < heads_line.hops - 1:
+            heads_line.moving, w_out = close((heads_line.moving, w_out))
         else:
-            heads_line.moving, side = close((heads_line.moving, side))
-    grad_rows, d_hidden, x_rows = side
-
-    mid_rows, normed_two, own_heads = project_out(
-        x_rows, heads_line.pieces, rank, w_out, gain_two, own
-    )
-    mid_rows, normed_two, own_heads, w_gate_up, d_hidden = close(
-        (mid_rows, normed_two, own_heads, w_gate_up, d_hidden)
-    )
+            total = out_step(total, arrived, rank, w_out)
+            heads_line.moving, total = close((heads_line.moving, total))
+            arrived = []
+        below, above = heads_line.moving
+        step = heads_line.step
+        if 2 * step > heads_line.hops:
+            arrived.append((step, [below, above]))
+        else:
+            arrived += [(step, [below]), (-step, [above])]
+
+    mid_rows, normed_two = out_step(total, arrived, rank, w_out, gain_two)
+    mid_rows, normed_two, w_gate_up, d_hidden = close((mid_rows, normed_two, w_gate_up, d_hidden))
     hidden, d_gate_up = close(gate_and_back(normed_two, w_gate_up, d_hidden, 512, wide))
+    down_grad = contract_rows(hidden, grad_rows).astype(low)
+    down_grad, hidden, d_gate_up, normed_two, grad_rows = close(
+        (down_grad, hidden, d_gate_up, normed_two, grad_rows)
+    )
+    down_grad = lax.psum_scatter(down_grad, "seq", scatter_dimension=1, tiled=True)
     peers = peers_of("tp")
-    half = peers.shape[0] // 2
-    first = blocks_times(d_gate_up, w_gate_up, peers[:half], own, 256, 15)
+    first = blocks_times(d_gate_up, w_gate_up, peers[:1], own, 512, 9)
     first, side = close((first, (hidden, d_gate_up, normed_two, grad_rows)))
     back_line = LineScatter(first, "tp")
     for index in range(back_line.hops):
         back_line.hop()
         hidden, d_gate_up, normed_two, grad_rows = side
         if index == 0:
-            second = blocks_times(d_gate_up, w_gate_up, peers[half:], own, 256, 15)
-            down_grad = contract_rows(hidden, grad_rows).astype(low)
-            back_line.moving, side, second, down_grad = close(
-                (back_line.moving, side, second, down_grad)
-            )
+            second = blocks_times(d_gate_up, w_gate_up, peers[1:], own, 256, 22)
+            back_line.moving, side, second = close((back_line.moving, side, second))
             back_line.made += second
-            down_grad = lax.psum_scatter(down_grad, "seq", scatter_dimension=1, tiled=True)
         elif index == 1:
             gate_up_grad = contract_rows(normed_two, d_gate_up).astype(low)
             back_line.moving, side, gate_up_grad = close((back_line.moving, side, gate_up_grad))
@@ -1034,39 +1078,31 @@
     )
 
     d_attn = contract_cols(d_branch, w_out).astype(low)
-    d_attn, d_branch, d_mid, mid, gain_two_grad, own_heads, partial_out = close(
-        (d_attn, d_branch, d_mid, mid, gain_two_grad, own_heads, partial_out)
+    d_attn, d_branch, d_mid, mid, gain_two_grad, partial_out = close(
+        (d_attn, d_branch, d_mid, mid, gain_two_grad, partial_out)
     )
     d_attn = lax.all_to_all(d_attn, "tp", split_axis=1, concat_axis=0, tiled=True)
+    own_heads = own_rows_of_heads(heads_line.pieces, rank, own)
     out_grad = contract_rows(own_heads, d_branch).astype(low)
     d_attn, out_grad, partial_out, down_grad = close((d_attn, out_grad, partial_out, down_grad))
     out_grad = lax.psum_scatter(out_grad, "seq", scatter_dimension=1, tiled=True)
-    made = [
-        lax.dynamic_slice_in_dim(partial_out, peers[i] * own, own, axis=0)
-        for i in range(peers.shape[0])
-    ]
-    out_line = LineScatter(made, "tp")
+    result = swap_scatter_parts(partial_out, "tp")
     grads = []
     travelled = []
     for group in range(groups):
-        out_line.hop()
         made = attend_back(
             queries, d_attn, attn[group], lse[group], [*far, kv], positions, back_rows,
             cos, sin, group, 256, 512,
         )
-        made, d_attn, travelled, out_line.moving = close(
-            (made, d_attn, travelled, out_line.moving)
-        )
+        made, d_attn, travelled = close((made, d_attn, travelled))
         grads.append(made)
         travelled.append(
             [along_sequence(made[2], -1, tokens), along_sequence(made[1], -2, tokens)]
         )
     down_new = adam_step(down_weight, down_grad.astype(full), down_moment, down_square)
-    while out_line.step < out_line.hops:
-        out_line.hop()
-        down_new, grads, travelled, down_grad, out_line.moving = close(
-            (down_new, grads, travelled, down_grad, out_line.moving)
-        )
+    down_new, grads, travelled, down_grad, result = close(
+        (down_new, grads, travelled, down_grad, result)
+    )
     d_mixed = mix_grads(
         [(made[0], made[3], *moved) for made, moved in zip(grads, travelled, strict=True)],
         cos, sin, tile,
@@ -1074,38 +1110,31 @@
     made = blocks_times(d_mixed, w_qkv, peers, own, 512, 7)
     made, d_mixed, gate_up_grad = close((made, d_mixed, gate_up_grad))
     in_line = LineScatter(made, "tp")
-    bits = [1 << bit for bit in range(lax.axis_size("seq").bit_length() - 1)]
     for index in range(in_line.hops):
         in_line.hop()
         if index == 0:
             qkv_grad = contract_rows(normed_one, d_mixed).astype(low)
             gain_one_grad = row_products(qkv_grad, w_qkv, min(512, width)) / gain_one
-            qkv_grad = qkv_grad.reshape(lax.axis_size("seq"), -1, qkv_grad.shape[1])
-            in_line.moving, qkv_grad, gain_one_grad = close(
-                (in_line.moving, qkv_grad, gain_one_grad)
-            )
+            gains_grad = jnp.stack([gain_one_grad, gain_two_grad])
+            in_line.moving, qkv_grad, gains_grad = close((in_line.moving, qkv_grad, gains_grad))
+            qkv_grad = lax.psum_scatter(qkv_grad, "seq", scatter_dimension=0, tiled=True)
         elif index == 1:
             gate_up_new = adam_interleaved(
                 gate_up_grad, gate_up_weight, gate_up_moment, gate_up_square, wide
             )
-            for hop in bits[:2]:
-                qkv_grad = halving_hop(qkv_grad, "seq", hop)
-            gains_grad = sum_everywhere(jnp.stack([gain_one_grad, gain_two_grad]), ("seq",))
-            in_line.moving, gate_up_new, gains_grad, qkv_grad = close(
-                (in_line.moving, gate_up_new, gains_grad, qkv_grad)
+            gains_grad = sum_by_swaps(gains_grad, "seq")
+            in_line.moving, gate_up_new, gains_grad, out_grad = close(
+                (in_line.moving, gate_up_new, gains_grad, out_grad)
             )
-            for hop in bits[2:]:
-                qkv_grad = halving_hop(qkv_grad, "seq", hop)
-            qkv_grad = qkv_grad[0]
-            gains_grad = sum_everywhere(gains_grad, ("tp",))
-            outputs = (mid + sum(part.astype(full) for part in out_line.parts)).astype(low)
-        elif index == in_line.hops - 1:
-            in_line.moving, gains_grad, qkv_grad, outputs, out_grad = close(
-                (in_line.moving, gains_grad, qkv_grad, outputs, out_grad)
+            out_parts = swap_scatter_parts(out_grad, "tp")
+        elif index == 2:
+            gains_grad = sum_at_once(gains_grad, "tp")
+            outputs = (mid + sum_parts(result)).astype(low)
+            in_line.moving, gains_grad, out_parts, outputs = close(
+                (in_line.moving, gains_grad, out_parts, outputs)
             )
         else:
             in_line.moving = close(in_line.moving)
-    out_parts = swap_scatter_parts(out_grad, "tp")
     input_grad = back_to_input(in_line.parts, layer_input, d_mid, gain_one)
     out_grad = sum_parts(out_parts)
     out_new = adam_step(out_weight, out_grad, out_moment, out_square)

time: 782 us -> 740 us (0.946)
  waiting for transfers between devices: 247 us -> 207 us
  local copies, waits for them, and re-layouts: 32.5 us -> 45.1 us
  other arithmetic: 45.5 us -> 35 us
    ppermute x26 -> x24, waiting for transfers between devices: 171 us -> 130 us  [the longest x9 52.2 us: hop(): self.from_high.append(lax.ppermute(self.from_high[-1], self.axis, down))]
    unnamed x159 -> x177, local copies, waits for them, and re-layouts: 24.6 us -> 40.4 us
    all_gather x1, waiting for transfers between devices: 0.01 us -> 13 us  [local(): w_down = lax.all_gather(low_down, 'seq', axis=1, tiled=True)]
    all_gather x1, waiting for transfers between devices: 12.3 us -> 0.01 us  [local(): w_gate_up = lax.all_gather(low_gate_up, 'seq', axis=0, tiled=True)]
    all_to_all x1 -> x2, waiting for transfers between devices: 7.9 us -> 18.5 us  [swap_scatter_parts(): return lax.all_to_all(parts, axis, split_axis=0, concat_axis=0, tiled=True)]
    ppermute x26 -> x24, starting transfers between devices: 59.8 us -> 49.6 us  [the longest x9 25 us: hop(): self.from_high.append(lax.ppermute(self.from_high[-1], self.axis, down))]
    pallas_call x1 -> x3, Pallas kernels: 17.5 us -> 26.5 us  [the longest x2 24.9 us: out_step(): pl.pallas_call(functools.partial(out_step_kernel, distances, last), grid_...]
    all_to_all x1 -> x2, starting transfers between devices: 4.38 us -> 13.3 us  [swap_scatter_parts(): return lax.all_to_all(parts, axis, split_axis=0, concat_axis=0, tiled=True)]
  transfers between devices with their start and end apart: 60 -> 54, of which waited for: 33 -> 25; matrix products, arithmetic and copies ran while one was open for 17% -> 15% of each run, Pallas kernels for 22% -> 24%
where the time goes in v2:
time: 740 us; the launch traced here: 725 us
  Pallas kernels  214 us (29%)
  waiting for transfers between devices  207 us (28%)
  starting transfers between devices  123 us (17%)
  matrix products  82.8 us (11%)
  local copies, waits for them, and re-layouts  45.1 us (6%)
  other arithmetic  35 us (5%)
  between operations  17.9 us (2%)
    ppermute x9, waiting for transfers between devices, hop(): self.from_high.append(lax.ppermute(self.from_high[-1], self.axis, down))  52.2 us
    dot_general x4, matrix products, contract_rows(): lax.dot_general(left, right, ROWS_BY_ROWS, preferred_element_type=jnp.flo...  48.8 us
    ppermute x9, waiting for transfers between devices, hop(): self.from_low.append(lax.ppermute(self.from_low[-1], self.axis, up))  47.2 us
    pallas_call x2, Pallas kernels, attend_back(): pl.pallas_call(functools.partial(attend_back_kernel, tk), grid_spec=pltpu...  42.9 us
    unnamed x177, local copies, waits for them, and re-layouts  40.4 us
    pallas_call x3, Pallas kernels, blocks_times(): pl.pallas_call(blocks_kernel, grid_spec=pltpu.PrefetchScalarGridSpec(num_...  36.3 us
    ppermute x3, waiting for transfers between devices, sum_at_once(): came.append(lax.ppermute(block, axis, route))  29.3 us
    pallas_call x1, Pallas kernels, gate_and_back(): pl.pallas_call(gate_kernel, grid=(units // wide, tokens // tile), in_spec...  27.1 us
  transfers between devices with their start and end apart: 54, of which 25 were waited for; matrix products, arithmetic and copies ran while one was open for 15% of the time, Pallas kernels for 24%

profile of v2, /device:TPU:10, one launch (start us, length us, event | category | flops | bytes accessed | tf_op | source)
XLA Modules:
  0.0 725.1 jit_solution(7190267776939267023)
XLA Ops:
  27.2 15.5 %collective-permute-done.1.refs_4_ = bf16[256,2048]{1,0:T(8,128)(2,1)} collective-permute-done((bf16[256,2048]{1,0:T(8,128)(2,1)S(1)}, bf16[256,2048]{1,0:T(8,128)(2,1)}, u32[]{:S(2)}, u32[]{:S(2)}) %collective-permute-start.1) | collective-permute-done | bytes 1048608 | tf_op jit(solution)/shard_map/ppermute | solution.py:64
  50.2 19.5 %collective-permute-done.2.refs_2_ = bf16[256,2048]{1,0:T(8,128)(2,1)S(1)} collective-permute-done((bf16[256,2048]{1,0:T(8,128)(2,1)}, bf16[256,2048]{1,0:T(8,128)(2,1)S(1)}, u32[]{:S(2)}, u32[]{:S(2)}) %collective-permute-start.2) | collective-permute-done | bytes 1048608 | tf_op jit(solution)/shard_map/ppermute | solution.py:63
  79.7 18.4 %collective-permute-done.5.refs_6_ = bf16[256,2048]{1,0:T(8,128)(2,1)} collective-permute-done((bf16[256,2048]{1,0:T(8,128)(2,1)S(1)}, bf16[256,2048]{1,0:T(8,128)(2,1)}, u32[]{:S(2)}, u32[]{:S(2)}) %collective-permute-start.5) | collective-permute-done | bytes 1048608 | tf_op jit(solution)/shard_map/ppermute | solution.py:64
  107.0 10.8 %project_qkv.1 = (bf16[1024,2048]{1,0:T(8,128)(2,1)}, bf16[1024,2048]{1,0:T(8,128)(2,1)}, bf16[1024,512]{1,0:T(8,128)(2,1)S(1)}, bf16[1024,256]{1,0:T(8,128)(2,1)S(1)}) custom-call(s32[1]{0:T(128)} %bitcast.1.rank_ref, bf16[2048,768]{1,0:T(8,128)(2,1)} %all-gather.5.cloned.1.call-done.w_ref.refs_4_, f32[1,2048]{1,0:T(1,128)S(1)} %get-tuple-element.457.gain_ref, ...), custom_call_target="tpu_custom_call" | custom-call | flops 10350000128 | bytes 27000000 | tf_op jit(solution)/shard_map/project_qkv/pallas_call | solution.py:255
  184.6 13.0 %all-gather.9.cloned.1.call-done = bf16[2048,2048]{1,0:T(8,128)(2,1)} async-done(((bf16[2048,256]{1,0:T(8,128)(2,1)}), bf16[2048,2048]{1,0:T(8,128)(2,1)}) %all-gather.9.cloned.1.call-update) | async-done | bytes 8388624 | tf_op jit(solution)/shard_map/all_gather | solution.py:999
  211.0 14.6 %convolution_convert_fusion.4.dh_ref = bf16[1024,2048]{1,0:T(8,128)(2,1)} fusion(bf16[1024,2048]{1,0:T(8,128)(2,1)} %place_rows.1, bf16[2048,2048]{1,0:T(8,128)(2,1)} %all-gather.9.cloned.1.call-done), kind=kOutput, calls=%fused_computation.5 | convolution fusion | flops 8592031744 | bytes 16777216 | tf_op jit(solution)/shard_map/dot_general | solution.py:45
  232.5 19.8 %collective-permute-done.16.refs_7_.refs_2_ = bf16[1024,512]{1,0:T(8,128)(2,1)S(1)} collective-permute-done((bf16[1024,512]{1,0:T(8,128)(2,1)S(1)}, bf16[1024,512]{1,0:T(8,128)(2,1)S(1)}, u32[]{:S(2)}, u32[]{:S(2)}) %collective-permute-start.16) | collective-permute-done | bytes 1048608 | tf_op jit(solution)/shard_map/ppermute | solution.py:63
  266.1 14.7 %out_step.2.refs_0_ = f32[1024,2048]{1,0:T(8,128)} custom-call(s32[1]{0:T(128)} %bitcast.1.rank_ref, bf16[1024,2048]{1,0:T(8,128)(2,1)} %get-tuple-element.309.refs_0_, bf16[1024,512]{1,0:T(8,128)(2,1)S(1)} %constant_dynamic-update-slice_fusion.refs_1_.refs_0_, bf16[2048,2048]{1,0:T(8,128)(2,1)} %all-gather.11.cloned.1.call-done.refs_2_.refs_4_.refs_6_.refs_9_, ...), custom_call_target="tpu_custom_call" | custom-call | flops 8049999872 | bytes 21000000 | tf_op jit(solution)/shard_map/out_step/pallas_call | solution.py:653
  287.8 10.2 %out_step.3 = (f32[1024,2048]{1,0:T(8,128)}, bf16[1024,2048]{1,0:T(8,128)(2,1)}) custom-call(s32[1]{0:T(128)} %bitcast.1.rank_ref, f32[1024,2048]{1,0:T(8,128)} %out_step.2.refs_0_, f32[1,2048]{1,0:T(1,128)S(1)} %get-tuple-element.456.refs_1_.gain_ref, bf16[1024,512]{1,0:T(8,128)(2,1)S(1)} %collective-permute-done.18.refs_2_.refs_3_, ...), custom_call_target="tpu_custom_call" | custom-call | flops 8049999872 | bytes 21000000 | tf_op jit(solution)/shard_map/out_step/pallas_call | solution.py:653
  298.0 27.1 %gate_and_back.1 = (bf16[1024,2048]{1,0:T(8,128)(2,1)S(1)}, bf16[1024,4096]{1,0:T(8,128)(2,1)}) custom-call(bf16[1024,2048]{1,0:T(8,128)(2,1)} %get-tuple-element.342.n_ref, bf16[2048,4096]{1,0:T(8,128)(2,1)} %all-gather.7.cloned.1.call-done.w_ref.refs_1_.refs_3_, bf16[1024,2048]{1,0:T(8,128)(2,1)} %convolution_convert_fusion.4.dh_ref), custom_call_target="tpu_custom_call" | custom-call | flops 31050000384 | bytes 81000000 | tf_op jit(solution)/shard_map/gate_and_back/pallas_call | solution.py:713
  327.1 11.2 %convolution_convert_fusion.2 = bf16[2048,2048]{1,0:T(8,128)(2,1)} fusion(bf16[1024,2048]{1,0:T(8,128)(2,1)S(1)} %get-tuple-element.345, bf16[1024,2048]{1,0:T(8,128)(2,1)S(1)} %copy-done.86), kind=kOutput, calls=%fused_computation.3 | convolution fusion | flops 8594128896 | bytes 16777216 | tf_op jit(solution)/shard_map/dot_general | solution.py:41
  342.2 10.5 %blocks_times.3 = bf16[256,2048]{1,0:T(8,128)(2,1)S(1)} custom-call(s32[1]{0:T(128)S(1)} %bitcast.42, bf16[1024,4096]{1,0:T(8,128)(2,1)} %get-tuple-element.341.refs_0_.refs_1_.refs_2_, bf16[2048,4096]{1,0:T(8,128)(2,1)} %all-gather.7.cloned.1.call-done.w_ref.refs_1_.refs_3_), custom_call_target="tpu_custom_call" | custom-call | flops 10350000128 | bytes 27000000 | tf_op jit(solution)/shard_map/blocks_times/pallas_call | solution.py:750
  354.7 19.7 %blocks_times.4 = (bf16[256,2048]{1,0:T(8,128)(2,1)S(1)}, bf16[256,2048]{1,0:T(8,128)(2,1)S(1)}, bf16[256,2048]{1,0:T(8,128)(2,1)S(1)}) custom-call(s32[3]{0:T(128)S(1)} %slice_bitcast_fusion.chunks_ref, bf16[1024,4096]{1,0:T(8,128)(2,1)} %get-tuple-element.341.refs_0_.refs_1_.refs_2_, bf16[1024,4096]{1,0:T(8,128)(2,1)} %get-tuple-element.341.refs_0_.refs_1_.refs_2_, ...), custom_call_target="tpu_custom_call" | custom-call | flops 25300000768 | bytes 66000000 | tf_op jit(solution)/shard_map/blocks_times/pallas_call | solution.py:750
  388.2 23.8 %convolution_convert_fusion = bf16[2048,4096]{1,0:T(8,128)(2,1)} fusion(bf16[1024,2048]{1,0:T(8,128)(2,1)S(1)} %copy-done.87, bf16[1024,4096]{1,0:T(8,128)(2,1)} %get-tuple-element.341.refs_0_.refs_1_.refs_2_), kind=kOutput, calls=%fused_computation | convolution fusion | flops 17188257792 | bytes 29360128 | tf_op jit(solution)/shard_map/dot_general | solution.py:41
  422.0 13.4 %convolution_convert_fusion.3 = bf16[1024,2048]{1,0:T(8,128)(2,1)} fusion(bf16[1024,2048]{1,0:T(8,128)(2,1)S(1)} %copy-done.58, bf16[2048,2048]{1,0:T(8,128)(2,1)} %all-gather.9.cloned.1.call-done), kind=kOutput, calls=%fused_computation.4 | convolution fusion | flops 8592031744 | bytes 16777216 | tf_op jit(solution)/shard_map/dot_general | solution.py:1072
  470.2 9.8 %all-to-all-done.1 = bf16[256,4,512]{2,0,1:T(8,128)(2,1)} async-done(((bf16[256,4,512]{2,0,1:T(8,128)(2,1)}), bf16[256,4,512]{2,0,1:T(8,128)(2,1)}, u32[]{:S(2)}, u32[]{:S(2)}) %all-to-all-start.1) | async-done | bytes 1048608 | tf_op jit(solution)/shard_map/all_to_all | solution.py:1084
  480.1 8.2 %all-to-all-start.2 = ((bf16[4,256,2048]{2,1,0:T(8,128)(2,1)}), bf16[4,256,2048]{2,1,0:T(8,128)(2,1)}, u32[]{:S(2)}, u32[]{:S(2)}) async-start(bf16[4,256,2048]{2,1,0:T(8,128)(2,1)} %bitcast.43), calls=%async_computation.3 | async-start | bytes 8388608 | tf_op jit(solution)/shard_map/all_to_all | solution.py:136
  491.9 21.4 %attend_back.2 = (bf16[1024,256]{1,0:T(8,128)(2,1)S(1)}, bf16[1024,128]{1,0:T(8,128)(2,1)S(1)}, bf16[1024,128]{1,0:T(8,128)(2,1)S(1)}, f32[1024,128]{1,0:T(8,128)S(1)}) custom-call(s32[1024]{0:T(1024)S(1)} %copy-done.18, bf16[1024,512]{1,0:T(8,128)(2,1)S(1)} %copy-done.62, bf16[1024,512]{1,0:T(8,128)(2,1)} %bitcast.10.do_ref, ...), custom_call_target="tpu_custom_call" | custom-call | flops 32199999488 | bytes 84000000 | tf_op jit(solution)/shard_map/attend_back/pallas_call | solution.py:535
  523.4 21.4 %attend_back.3 = (bf16[1024,256]{1,0:T(8,128)(2,1)S(1)}, bf16[1024,128]{1,0:T(8,128)(2,1)S(1)}, bf16[1024,128]{1,0:T(8,128)(2,1)S(1)}, f32[1024,128]{1,0:T(8,128)S(1)}) custom-call(s32[1024]{0:T(1024)S(1)} %copy-done.18, bf16[1024,512]{1,0:T(8,128)(2,1)S(1)} %copy-done.62, bf16[1024,512]{1,0:T(8,128)(2,1)} %bitcast.10.do_ref, ...), custom_call_target="tpu_custom_call" | custom-call | flops 32199999488 | bytes 84000000 | tf_op jit(solution)/shard_map/attend_back/pallas_call | solution.py:535
  546.4 8.2 %collective-permute-start.28 = (bf16[1024,128]{1,0:T(8,128)(2,1)S(1)}, bf16[1024,128]{1,0:T(8,128)(2,1)S(1)}, u32[]{:S(2)}, u32[]{:S(2)}) collective-permute-start(bf16[1024,128]{1,0:T(8,128)(2,1)S(1)} %get-tuple-element.376), channel_id=1, source_target_pairs={{4,0},{8,4},{12,8},{20,16},{24,20},{28,24},{5,1},{9,5},{13,9},{21,... | collective-permute-start | bytes 786440 | tf_op jit(solution)/shard_map/ppermute | solution.py:173
  559.2 18.5 %all-to-all-done.2 = bf16[4,256,2048]{2,1,0:T(8,128)(2,1)} async-done(((bf16[4,256,2048]{2,1,0:T(8,128)(2,1)}), bf16[4,256,2048]{2,1,0:T(8,128)(2,1)}, u32[]{:S(2)}, u32[]{:S(2)}) %all-to-all-start.2) | async-done | bytes 4194336 | tf_op jit(solution)/shard_map/all_to_all | solution.py:136
  609.6 9.3 %collective-permute-done.30 = bf16[256,2048]{1,0:T(8,128)(2,1)} collective-permute-done((bf16[256,2048]{1,0:T(8,128)(2,1)S(1)}, bf16[256,2048]{1,0:T(8,128)(2,1)}, u32[]{:S(2)}, u32[]{:S(2)}) %collective-permute-start.30) | collective-permute-done | bytes 1048608 | tf_op jit(solution)/shard_map/ppermute | solution.py:119
  631.3 13.9 %adam_interleaved.1 = (f32[2,256,2048]{2,1,0:T(8,128)}, f32[2,256,2048]{2,1,0:T(8,128)}, f32[2,256,2048]{2,1,0:T(8,128)}, f32[2,256,2048]{2,1,0:T(8,128)}, bf16[2,256,2048]{2,1,0:T(8,128)(2,1)}) custom-call(bf16[256,4096]{1,0:T(8,128)(2,1)S(1)} %copy-done.21, f32[2,256,2048]{2,1,0:T(8,128)} %w_ref.3, f32[2,256,2048]{2,1,0:T(8,128)} %m_ref.1, ...), custom_call_target="tpu_custom_call" | custom-call | flops 14949999616 | bytes 39000000 | tf_op jit(solution)/shard_map/adam_interleaved/pallas_call | solution.py:914
  675.5 29.2 %collective-permute-done.41 = f32[2,2048]{1,0:T(2,128)S(1)} collective-permute-done((f32[2,2048]{1,0:T(2,128)S(1)}, f32[2,2048]{1,0:T(2,128)S(1)}, u32[]{:S(2)}, u32[]{:S(2)}) %collective-permute-start.41) | collective-permute-done | bytes 16416 | tf_op jit(solution)/shard_map/ppermute | solution.py:157
  (335 shorter events, 325.0 us)
Async XLA Ops:
  7.2 90.9 %all-gather.5.cloned.1.call-start = ((), (), s32[]{:S(2)}) async-start(), calls=%async_computation.8 | async-start | bytes 3538944 | tf_op jit(solution)/shard_map/all_gather | solution.py:980
  9.2 144.9 %all-gather.7.cloned.1.call-start = ((), (), s32[]{:S(2)}) async-start(), calls=%async_computation.9 | async-start | bytes 18874368 | tf_op jit(solution)/shard_map/all_gather | solution.py:982
  15.5 182.0 %all-gather.9.cloned.1.call-start = ((), (), s32[]{:S(2)}) async-start(), calls=%async_computation.10 | async-start | bytes 9437184 | tf_op jit(solution)/shard_map/all_gather | solution.py:999
  155.2 42.4 %all-to-all-start = ((bf16[4,512,256]{2,1,0:T(8,128)(2,1)}), bf16[4,512,256]{2,1,0:T(8,128)(2,1)}, u32[]{:S(2)}, u32[]{:S(2)}) async-start(bf16[4,512,256]{2,1,0:T(8,128)(2,1)} %broadcast_in_dim.5), calls=%async_computation | async-start | bytes 2097152 | tf_op jit(solution)/shard_map/all_to_all | solution.py:130
  160.4 101.1 %all-gather.11.cloned.1.call-start = ((), (), s32[]{:S(2)}) async-start(), calls=%async_computation.11 | async-start | bytes 9437184 | tf_op jit(solution)/shard_map/all_gather | solution.py:1022
  160.4 37.2 %collective-permute-start.12 = (bf16[256,2048]{1,0:T(8,128)(2,1)S(1)}, bf16[256,2048]{1,0:T(8,128)(2,1)}, u32[]{:S(2)}, u32[]{:S(2)}) collective-permute-start(bf16[256,2048]{1,0:T(8,128)(2,1)S(1)} %collective-permute-done.10.refs_2_), channel_id=1, source_target_pairs={{2,3},{6,7},{10,11},{14,15},{18,19},{22,23},{26,27},{30,31}} | collective-permute-start | bytes 3145736 | tf_op jit(solution)/shard_map/ppermute | solution.py:63
  162.0 35.5 %collective-permute-start.13 = (bf16[256,2048]{1,0:T(8,128)(2,1)}, bf16[256,2048]{1,0:T(8,128)(2,1)}, u32[]{:S(2)}, u32[]{:S(2)}) collective-permute-start(bf16[256,2048]{1,0:T(8,128)(2,1)} %collective-permute-done.11.refs_5_), channel_id=1, source_target_pairs={{1,0},{5,4},{9,8},{13,12},{17,16},{21,20},{25,24},{29,28}} | collective-permute-start | bytes 3145736 | tf_op jit(solution)/shard_map/ppermute | solution.py:64
  197.6 282.4 %reduce-scatter.5.cloned.1.call-start = ((), (), s32[]{:S(2)}) async-start(), calls=%async_computation.12 | async-start | bytes 9437184 | tf_op jit(solution)/shard_map/reduce_scatter | solution.py:1055
  197.8 27.9 %collective-permute-start.15 = (bf16[1024,512]{1,0:T(8,128)(2,1)S(1)}, bf16[1024,512]{1,0:T(8,128)(2,1)S(1)}, u32[]{:S(2)}, u32[]{:S(2)}) collective-permute-start(bf16[1024,512]{1,0:T(8,128)(2,1)S(1)} %constant_dynamic-update-slice_fusion.refs_1_.refs_0_), channel_id=1, source_target_pairs={{1,0},{2,1},{3,2},{5,4},{6,5},{7,6},{9,8},{10,9},{11,10},{13,12},{... | collective-permute-start | bytes 3145736 | tf_op jit(solution)/shard_map/ppermute | solution.py:64
  338.3 251.8 %reduce-scatter.7.cloned.1.call-start = ((), (), s32[]{:S(2)}) async-start(), calls=%async_computation.13 | async-start | bytes 18874368 | tf_op jit(solution)/shard_map/reduce_scatter | solution.py:1070
  382.1 29.9 %collective-permute-start.23 = (bf16[256,2048]{1,0:T(8,128)(2,1)}, bf16[256,2048]{1,0:T(8,128)(2,1)}, u32[]{:S(2)}, u32[]{:S(2)}) collective-permute-start(bf16[256,2048]{1,0:T(8,128)(2,1)} %get-tuple-element.450), channel_id=1, source_target_pairs={{2,1},{3,2},{6,5},{7,6},{10,9},{11,10},{14,13},{15,14},{18,17},{19... | collective-permute-start | bytes 3145736 | tf_op jit(solution)/shard_map/ppermute | solution.py:120
  383.4 28.6 %collective-permute-start.22 = (bf16[256,2048]{1,0:T(8,128)(2,1)}, bf16[256,2048]{1,0:T(8,128)(2,1)}, u32[]{:S(2)}, u32[]{:S(2)}) collective-permute-start(bf16[256,2048]{1,0:T(8,128)(2,1)} %get-tuple-element.451), channel_id=1, source_target_pairs={{0,1},{1,2},{4,5},{5,6},{8,9},{9,10},{12,13},{13,14},{16,17},{17,1... | collective-permute-start | bytes 3145736 | tf_op jit(solution)/shard_map/ppermute | solution.py:119
  459.9 185.3 %reduce-scatter.9.cloned.1.call-start = ((), (), s32[]{:S(2)}) async-start(), calls=%async_computation.14 | async-start | bytes 9437184 | tf_op jit(solution)/shard_map/reduce_scatter | solution.py:1088
  480.1 97.6 %all-to-all-start.2 = ((bf16[4,256,2048]{2,1,0:T(8,128)(2,1)}), bf16[4,256,2048]{2,1,0:T(8,128)(2,1)}, u32[]{:S(2)}, u32[]{:S(2)}) async-start(bf16[4,256,2048]{2,1,0:T(8,128)(2,1)} %bitcast.43), calls=%async_computation.3 | async-start | bytes 8388608 | tf_op jit(solution)/shard_map/all_to_all | solution.py:136
  488.4 226.0 %reduce-scatter.11.cloned.1.call-start = ((), (), s32[]{:S(2)}) async-start(), calls=%async_computation.15 | async-start | bytes 3538944 | tf_op jit(solution)/shard_map/reduce_scatter | solution.py:1120
  514.9 30.0 %collective-permute-start.27 = (bf16[1024,128]{1,0:T(8,128)(2,1)S(1)}, bf16[1024,128]{1,0:T(8,128)(2,1)S(1)}, u32[]{:S(2)}, u32[]{:S(2)}) collective-permute-start(bf16[1024,128]{1,0:T(8,128)(2,1)S(1)} %get-tuple-element.365), channel_id=1, source_target_pairs={{8,0},{12,4},{24,16},{28,20},{9,1},{13,5},{25,17},{29,21},{10,2},{... | collective-permute-start | bytes 786440 | tf_op jit(solution)/shard_map/ppermute | solution.py:173
  516.5 28.4 %collective-permute-start.26 = (bf16[1024,128]{1,0:T(8,128)(2,1)S(1)}, bf16[1024,128]{1,0:T(8,128)(2,1)S(1)}, u32[]{:S(2)}, u32[]{:S(2)}) collective-permute-start(bf16[1024,128]{1,0:T(8,128)(2,1)S(1)} %get-tuple-element.366), channel_id=1, source_target_pairs={{4,0},{8,4},{12,8},{20,16},{24,20},{28,24},{5,1},{9,5},{13,9},{21,... | collective-permute-start | bytes 786440 | tf_op jit(solution)/shard_map/ppermute | solution.py:173
  625.0 27.2 %collective-permute-start.32 = (bf16[256,2048]{1,0:T(8,128)(2,1)}, bf16[256,2048]{1,0:T(8,128)(2,1)}, u32[]{:S(2)}, u32[]{:S(2)}) collective-permute-start(bf16[256,2048]{1,0:T(8,128)(2,1)} %get-tuple-element.449), channel_id=1, source_target_pairs={{0,1},{1,2},{4,5},{5,6},{8,9},{9,10},{12,13},{13,14},{16,17},{17,1... | collective-permute-start | bytes 3145736 | tf_op jit(solution)/shard_map/ppermute | solution.py:119
  652.2 52.7 %all-to-all-start.3 = ((bf16[4,512,256]{2,1,0:T(8,128)(2,1)}), bf16[4,512,256]{2,1,0:T(8,128)(2,1)}, u32[]{:S(2)}, u32[]{:S(2)}) async-start(bf16[4,512,256]{2,1,0:T(8,128)(2,1)} %bitcast.45), calls=%async_computation.6 | async-start | bytes 2097152 | tf_op jit(solution)/shard_map/all_to_all | solution.py:136
  658.7 46.1 %collective-permute-start.38 = (bf16[256,2048]{1,0:T(8,128)(2,1)S(1)}, bf16[256,2048]{1,0:T(8,128)(2,1)S(1)}, u32[]{:S(2)}, u32[]{:S(2)}) collective-permute-start(bf16[256,2048]{1,0:T(8,128)(2,1)S(1)} %get-tuple-element.452), channel_id=1, source_target_pairs={{1,0},{2,1},{3,2},{5,4},{6,5},{7,6},{9,8},{10,9},{11,10},{13,12},{... | collective-permute-start | bytes 3145736 | tf_op jit(solution)/shard_map/ppermute | solution.py:120
  660.8 44.0 %collective-permute-start.37 = (bf16[256,2048]{1,0:T(8,128)(2,1)S(1)}, bf16[256,2048]{1,0:T(8,128)(2,1)S(1)}, u32[]{:S(2)}, u32[]{:S(2)}) collective-permute-start(bf16[256,2048]{1,0:T(8,128)(2,1)S(1)} %get-tuple-element.453), channel_id=1, source_target_pairs={{0,1},{1,2},{2,3},{4,5},{5,6},{6,7},{8,9},{9,10},{10,11},{12,13},{... | collective-permute-start | bytes 3145736 | tf_op jit(solution)/shard_map/ppermute | solution.py:119
  668.1 36.6 %collective-permute-start.41 = (f32[2,2048]{1,0:T(2,128)S(1)}, f32[2,2048]{1,0:T(2,128)S(1)}, u32[]{:S(2)}, u32[]{:S(2)}) collective-permute-start(f32[2,2048]{1,0:T(2,128)S(1)} %add.172), channel_id=1, source_target_pairs={{0,3},{1,0},{2,1},{3,2},{4,7},{5,4},{6,5},{7,6},{8,11},{9,8},{10,9... | collective-permute-start | bytes 49160 | tf_op jit(solution)/shard_map/ppermute | solution.py:157
  668.3 36.5 %collective-permute-start.40 = (f32[2,2048]{1,0:T(2,128)S(1)}, f32[2,2048]{1,0:T(2,128)S(1)}, u32[]{:S(2)}, u32[]{:S(2)}) collective-permute-start(f32[2,2048]{1,0:T(2,128)S(1)} %add.172), channel_id=1, source_target_pairs={{0,2},{1,3},{2,0},{3,1},{4,6},{5,7},{6,4},{7,5},{8,10},{9,11},{10,... | collective-permute-start | bytes 49160 | tf_op jit(solution)/shard_map/ppermute | solution.py:157
  671.3 33.5 %collective-permute-start.39 = (f32[2,2048]{1,0:T(2,128)S(1)}, f32[2,2048]{1,0:T(2,128)S(1)}, u32[]{:S(2)}, u32[]{:S(2)}) collective-permute-start(f32[2,2048]{1,0:T(2,128)S(1)} %add.172), channel_id=1, source_target_pairs={{0,1},{1,2},{2,3},{3,0},{4,5},{5,6},{6,7},{7,4},{8,9},{9,10},{10,1... | collective-permute-start | bytes 49160 | tf_op jit(solution)/shard_map/ppermute | solution.py:157
  (118 other events, 2052.2 us)
Sparse Core Ops, SparseCore 0:
  10.5 33.4 all-gather.4
  46.4 89.8 all-gather.6
  138.8 58.7 all-gather.8
  199.3 62.1 all-gather.10
  338.4 72.6 reduce-scatter.4
  415.0 120.6 reduce-scatter.6
  539.5 74.8 reduce-scatter.8
  629.7 44.3 reduce-scatter.10

commit v3 on v2

--- a/solution.py
+++ b/solution.py
@@ -615,13 +615,19 @@
         if count == 2:
             piece = jnp.where(rank_ref[0] >= distance, piece, refs.pop(0)[...])
         total = total + jnp.dot(piece, refs.pop(0)[...], preferred_element_type=jnp.float32)
-    refs[0][...] = total
-    if last:
+    if not last:
+        refs[0][...] = total
+    else:
+
+        @pl.when(pl.program_id(0) == rank_ref[0])
+        def _():
+            refs[0][...] = total
+
         inverse = lax.rsqrt(jnp.mean(total * total, axis=1, keepdims=True) + NORM_EPS)
         refs[1][...] = (total * inverse * gain_ref[...]).astype(jnp.bfloat16)
 
 
-def out_step(base, pieces, rank, weight, gain=None, tile=256):
+def out_step(base, pieces, rank, weight, tile, gain=None):
     tokens, width = base.shape
     depth = pieces[0][1][0].shape[1]
     last = gain is not None
@@ -646,9 +652,11 @@
     for distance, blocks in pieces:
         operands += [*blocks, weight]
         specs += [rows(depth)] * len(blocks) + [slot_rows(distance, len(blocks))]
-    outs = [jax.ShapeDtypeStruct((tokens, width), jnp.float32)]
+    outs = [jax.ShapeDtypeStruct((tile if last else tokens, width), jnp.float32)]
+    out_specs = [pl.BlockSpec((tile, width), lambda i, r: (0, 0)) if last else rows(width)]
     if last:
         outs.append(jax.ShapeDtypeStruct((tokens, width), jnp.bfloat16))
+        out_specs.append(rows(width))
     distances = tuple((distance, len(blocks)) for distance, blocks in pieces)
     made = pl.pallas_call(
         functools.partial(out_step_kernel, distances, last),
@@ -656,7 +664,7 @@
             num_scalar_prefetch=1,
             grid=(tokens // tile,),
             in_specs=specs,
-            out_specs=[rows(width)] * len(outs),
+            out_specs=out_specs,
         ),
         out_shape=outs,
         compiler_params=pltpu.CompilerParams(vmem_limit_bytes=VMEM_LIMIT),
@@ -803,14 +811,12 @@
     return total
 
 
-def mid_kernel(rank_ref, mid_ref, dy_ref, gain_ref, *refs):
-    *parts, d_mid_ref, branch_ref, mid_out, gain_grad_ref = refs
-    mid = mid_ref[...]
-    grad, gain_grad = norm_back_rows(mid, sum_refs(parts), gain_ref[...])
+def mid_kernel(mid_ref, dy_ref, gain_ref, *refs):
+    *parts, d_mid_ref, branch_ref, gain_grad_ref = refs
+    grad, gain_grad = norm_back_rows(mid_ref[...], sum_refs(parts), gain_ref[...])
     d_mid = dy_ref[...].astype(jnp.float32) + grad
     d_mid_ref[...] = d_mid
     branch_ref[...] = d_mid.astype(jnp.bfloat16)
-    mid_out[...] = mid
     gain_grad = jnp.broadcast_to(gain_grad, gain_grad_ref.shape)
 
     @pl.when(pl.program_id(0) == 0)
@@ -822,39 +828,25 @@
         gain_grad_ref[...] += gain_grad
 
 
-def back_to_mid(parts, mid_rows, rank, output_grad, gain):
+def back_to_mid(parts, mid, output_grad, gain):
     own, width = output_grad.shape
     tile = min(64, own)
-    tiles = own // tile
-
-    def rows(index):
-        return pl.BlockSpec((tile, width), index)
-
-    own_rows = rows(lambda i, r: (i, 0))
+    rows = pl.BlockSpec((tile, width), lambda i: (i, 0))
     outs = pl.pallas_call(
         mid_kernel,
-        grid_spec=pltpu.PrefetchScalarGridSpec(
-            num_scalar_prefetch=1,
-            grid=(tiles,),
-            in_specs=[
-                rows(lambda i, r: (r[0] * tiles + i, 0)),
-                own_rows,
-                pl.BlockSpec((1, width), lambda i, r: (0, 0)),
-            ]
-            + [own_rows] * len(parts),
-            out_specs=[own_rows, own_rows, own_rows, pl.BlockSpec((8, width), lambda i, r: (0, 0))],
-        ),
+        grid=(own // tile,),
+        in_specs=[rows, rows, pl.BlockSpec((1, width), lambda i: (0, 0))] + [rows] * len(parts),
+        out_specs=[rows, rows, pl.BlockSpec((8, width), lambda i: (0, 0))],
         out_shape=[
             jax.ShapeDtypeStruct((own, width), jnp.float32),
             jax.ShapeDtypeStruct((own, width), jnp.bfloat16),
-            jax.ShapeDtypeStruct((own, width), jnp.float32),
             jax.ShapeDtypeStruct((8, width), jnp.float32),
         ],
         compiler_params=pltpu.CompilerParams(vmem_limit_bytes=VMEM_LIMIT),
         cost_estimate=cost(4),
         name="back_to_mid",
-    )(jnp.reshape(rank, (1,)).astype(jnp.int32), mid_rows, output_grad, gain[None], *parts)
-    return outs[0], outs[1], outs[2], outs[3][0]
+    )(mid, output_grad, gain[None], *parts)
+    return outs[0], outs[1], outs[2][0]
 
 
 def input_kernel(x_ref, d_mid_ref, gain_ref, *refs):
@@ -975,18 +967,19 @@
 
     close = lax.optimization_barrier
 
-    low_qkv = qkv_weight.astype(low)
-    low_down = down_weight.astype(low)
-    w_qkv = lax.all_gather(low_qkv, "seq", axis=0, tiled=True)
-    low_gate_up = round_interleaved(gate_up_weight, wide)
-    w_gate_up = lax.all_gather(low_gate_up, "seq", axis=0, tiled=True)
-    low_out = out_weight.astype(low)
-    cos, sin = angle_tables(positions)
-    back_rows = jnp.broadcast_to(positions[None, :], (8, tokens))
-    side = (low_down, low_out, cos, sin, back_rows)
+    w_qkv = lax.all_gather(qkv_weight.astype(low), "seq", axis=0, tiled=True)
+    side = (gate_up_weight, down_weight, out_weight, positions)
     x_line = LineGather(layer_input, "tp")
-    for _ in range(x_line.hops):
+    for index in range(x_line.hops):
         x_line.hop()
+        if index == 1:
+            held_gate_up, held_down, held_out, held_positions = side
+            w_gate_up = lax.all_gather(
+                round_interleaved(held_gate_up, wide), "seq", axis=0, tiled=True
+            )
+            cos, sin = angle_tables(held_positions)
+            back_rows = jnp.broadcast_to(held_positions[None, :], (8, tokens))
+            side = (held_down.astype(low), held_out.astype(low), cos, sin, back_rows)
         x_line.moving, side = close((x_line.moving, side))
     pieces, side, w_qkv, output_grad = close((x_line.pieces, side, w_qkv, output_grad))
     low_down, low_out, cos, sin, back_rows = side
@@ -997,16 +990,16 @@
     made, dy_line.moving, low_out, low_down = close((made, dy_line.moving, low_out, low_down))
     x_rows, normed_one, queries, kv = made
     w_down = lax.all_gather(low_down, "seq", axis=1, tiled=True)
+    out_strip = swap_gather(low_out, "tp")
     far = [along_sequence(kv, distance, tokens) for distance in (2, 1)]
     if dy_line.hops > 1:
         dy_line.hop()
     states = [
         attend_here(queries, kv, positions, back_rows, group, 256, 512) for group in range(groups)
     ]
-    far, states, queries, low_out, w_gate_up, dy_line.moving = close(
-        (far, states, queries, low_out, w_gate_up, dy_line.moving)
+    far, states, queries, w_gate_up, dy_line.moving = close(
+        (far, states, queries, w_gate_up, dy_line.moving)
     )
-    out_strip = swap_gather(low_out, "tp")
     for _ in range(2, dy_line.hops):
         dy_line.hop()
     attn, lse = [], []
@@ -1035,7 +1028,7 @@
         elif index < heads_line.hops - 1:
             heads_line.moving, w_out = close((heads_line.moving, w_out))
         else:
-            total = out_step(total, arrived, rank, w_out)
+            total = out_step(total, arrived, rank, w_out, own)
             heads_line.moving, total = close((heads_line.moving, total))
             arrived = []
         below, above = heads_line.moving
@@ -1045,9 +1038,9 @@
         else:
             arrived += [(step, [below]), (-step, [above])]
 
-    mid_rows, normed_two = out_step(total, arrived, rank, w_out, gain_two)
-    mid_rows, normed_two, w_gate_up, d_hidden = close((mid_rows, normed_two, w_gate_up, d_hidden))
-    hidden, d_gate_up = close(gate_and_back(normed_two, w_gate_up, d_hidden, 512, wide))
+    mid, normed_two = out_step(total, arrived, rank, w_out, own, gain_two)
+    mid, normed_two, w_gate_up, d_hidden = close((mid, normed_two, w_gate_up, d_hidden))
+    hidden, d_gate_up = close(gate_and_back(normed_two, w_gate_up, d_hidden, 1024, wide))
     down_grad = contract_rows(hidden, grad_rows).astype(low)
     down_grad, hidden, d_gate_up, normed_two, grad_rows = close(
         (down_grad, hidden, d_gate_up, normed_two, grad_rows)
@@ -1073,9 +1066,7 @@
             back_line.moving, side, partial_out = close((back_line.moving, side, partial_out))
         else:
             back_line.moving, side = close((back_line.moving, side))
-    d_mid, d_branch, mid, gain_two_grad = back_to_mid(
-        back_line.parts, mid_rows, rank, output_grad, gain_two
-    )
+    d_mid, d_branch, gain_two_grad = back_to_mid(back_line.parts, mid, output_grad, gain_two)
 
     d_attn = contract_cols(d_branch, w_out).astype(low)
     d_attn, d_branch, d_mid, mid, gain_two_grad, partial_out = close(
@@ -1099,24 +1090,27 @@
         travelled.append(
             [along_sequence(made[2], -1, tokens), along_sequence(made[1], -2, tokens)]
         )
-    down_new = adam_step(down_weight, down_grad.astype(full), down_moment, down_square)
-    down_new, grads, travelled, down_grad, result = close(
-        (down_new, grads, travelled, down_grad, result)
-    )
+    down_grad = down_grad.astype(full)
+    down_new = adam_step(down_weight, down_grad, down_moment, down_square)
+    down_new, grads, travelled, down_grad = close((down_new, grads, travelled, down_grad))
     d_mixed = mix_grads(
         [(made[0], made[3], *moved) for made, moved in zip(grads, travelled, strict=True)],
         cos, sin, tile,
     )
-    made = blocks_times(d_mixed, w_qkv, peers, own, 512, 7)
+    made = blocks_times(d_mixed, w_qkv, peers[:1], own, 512, 2)
     made, d_mixed, gate_up_grad = close((made, d_mixed, gate_up_grad))
     in_line = LineScatter(made, "tp")
     for index in range(in_line.hops):
         in_line.hop()
         if index == 0:
+            made = blocks_times(d_mixed, w_qkv, peers[1:], own, 512, 5)
             qkv_grad = contract_rows(normed_one, d_mixed).astype(low)
             gain_one_grad = row_products(qkv_grad, w_qkv, min(512, width)) / gain_one
             gains_grad = jnp.stack([gain_one_grad, gain_two_grad])
-            in_line.moving, qkv_grad, gains_grad = close((in_line.moving, qkv_grad, gains_grad))
+            in_line.moving, qkv_grad, gains_grad, result, made = close(
+                (in_line.moving, qkv_grad, gains_grad, result, made)
+            )
+            in_line.made += made
             qkv_grad = lax.psum_scatter(qkv_grad, "seq", scatter_dimension=0, tiled=True)
         elif index == 1:
             gate_up_new = adam_interleaved(
@@ -1130,8 +1124,10 @@
         elif index == 2:
             gains_grad = sum_at_once(gains_grad, "tp")
             outputs = (mid + sum_parts(result)).astype(low)
-            in_line.moving, gains_grad, out_parts, outputs = close(
-                (in_line.moving, gains_grad, out_parts, outputs)
+            qkv_grad = qkv_grad.astype(full)
+            qkv_new = adam_step(qkv_weight, qkv_grad, qkv_moment, qkv_square)
+            in_line.moving, gains_grad, out_parts, outputs, qkv_grad, qkv_new = close(
+                (in_line.moving, gains_grad, out_parts, outputs, qkv_grad, qkv_new)
             )
         else:
             in_line.moving = close(in_line.moving)
@@ -1139,10 +1135,7 @@
     out_grad = sum_parts(out_parts)
     out_new = adam_step(out_weight, out_grad, out_moment, out_square)
 
-    qkv_grad = qkv_grad.astype(full)
     out_grad = out_grad.astype(full)
-    down_grad = down_grad.astype(full)
-    qkv_new = adam_step(qkv_weight, qkv_grad, qkv_moment, qkv_square)
     gains_new = adam_step(norm_gains, gains_grad, gains_moment, gains_square)
     return (
         outputs,

time: 740 us -> 705 us (0.953)
  waiting for transfers between devices: 207 us -> 179 us
  local copies, waits for them, and re-layouts: 45.1 us -> 36.8 us
    ppermute x3, waiting for transfers between devices: 29.3 us -> 0.01 us  [sum_at_once(): came.append(lax.ppermute(block, axis, route))]
    all_to_all x2, waiting for transfers between devices: 18.5 us -> 0.01 us  [swap_scatter_parts(): return lax.all_to_all(parts, axis, split_axis=0, concat_axis=0, tiled=True)]
    reduce_scatter x1, waiting for transfers between devices: 0.01 us -> 17.4 us  [local(): lax.psum_scatter(qkv_grad, 'seq', scatter_dimension=0, tiled=True)]
    ppermute x6, waiting for transfers between devices: 11.3 us -> 21.3 us  [hop(): lax.ppermute(to_low, self.axis, [(i, i - 1) for i in range(size - step, s...]
    unnamed x177 -> x185, local copies, waits for them, and re-layouts: 40.4 us -> 32.2 us
    ppermute x9, waiting for transfers between devices: 52.2 us -> 59.9 us  [hop(): self.from_high.append(lax.ppermute(self.from_high[-1], self.axis, down))]
    pallas_call x3 -> x4, Pallas kernels: 36.3 us -> 38.1 us  [blocks_times(): pl.pallas_call(blocks_kernel, grid_spec=pltpu.PrefetchScalarGridSpec(num_...]
  transfers between devices with their start and end apart: 54 -> 54, of which waited for: 25 -> 22; matrix products, arithmetic and copies ran while one was open for 15% -> 15% of each run, Pallas kernels for 24% -> 25%
where the time goes in v3:
time: 705 us; the launch traced here: 694 us
  Pallas kernels  212 us (30%)
  waiting for transfers between devices  179 us (25%)
  starting transfers between devices  126 us (18%)
  matrix products  80.3 us (11%)
  other arithmetic  40.7 us (6%)
  local copies, waits for them, and re-layouts  36.8 us (5%)
  between operations  18.3 us (3%)
    ppermute x9, waiting for transfers between devices, hop(): self.from_high.append(lax.ppermute(self.from_high[-1], self.axis, down))  59.9 us
    dot_general x4, matrix products, contract_rows(): lax.dot_general(left, right, ROWS_BY_ROWS, preferred_element_type=jnp.flo...  47 us
    pallas_call x2, Pallas kernels, attend_back(): pl.pallas_call(functools.partial(attend_back_kernel, tk), grid_spec=pltpu...  42.9 us
    ppermute x9, waiting for transfers between devices, hop(): self.from_low.append(lax.ppermute(self.from_low[-1], self.axis, up))  40.6 us
    pallas_call x4, Pallas kernels, blocks_times(): pl.pallas_call(blocks_kernel, grid_spec=pltpu.PrefetchScalarGridSpec(num_...  38.1 us
    unnamed x185, local copies, waits for them, and re-layouts  32.2 us
    pallas_call x1, Pallas kernels, gate_and_back(): pl.pallas_call(gate_kernel, grid=(units // wide, tokens // tile), in_spec...  24.6 us
    ppermute x9, starting transfers between devices, hop(): self.from_high.append(lax.ppermute(self.from_high[-1], self.axis, down))  24 us
  transfers between devices with their start and end apart: 54, of which 22 were waited for; matrix products, arithmetic and copies ran while one was open for 15% of the time, Pallas kernels for 25%

profile of v3, /device:TPU:10, one launch (start us, length us, event | category | flops | bytes accessed | tf_op | source)
XLA Modules:
  0.0 694.1 jit_solution(612456412050419905)
XLA Ops:
  15.3 21.1 %collective-permute-done.1.refs_4_ = bf16[256,2048]{1,0:T(8,128)(2,1)S(1)} collective-permute-done((bf16[256,2048]{1,0:T(8,128)(2,1)}, bf16[256,2048]{1,0:T(8,128)(2,1)S(1)}, u32[]{:S(2)}, u32[]{:S(2)}) %collective-permute-start.1) | collective-permute-done | bytes 1048608 | tf_op jit(solution)/shard_map/ppermute | solution.py:64
  57.2 12.8 %collective-permute-done.2.refs_2_ = bf16[256,2048]{1,0:T(8,128)(2,1)} collective-permute-done((bf16[256,2048]{1,0:T(8,128)(2,1)S(1)}, bf16[256,2048]{1,0:T(8,128)(2,1)}, u32[]{:S(2)}, u32[]{:S(2)}) %collective-permute-start.2) | collective-permute-done | bytes 1048608 | tf_op jit(solution)/shard_map/ppermute | solution.py:63
  79.3 19.8 %collective-permute-done.5.refs_6_ = bf16[256,2048]{1,0:T(8,128)(2,1)} collective-permute-done((bf16[256,2048]{1,0:T(8,128)(2,1)}, bf16[256,2048]{1,0:T(8,128)(2,1)}, u32[]{:S(2)}, u32[]{:S(2)}) %collective-permute-start.5) | collective-permute-done | bytes 1048608 | tf_op jit(solution)/shard_map/ppermute | solution.py:64
  107.9 10.8 %project_qkv.1 = (bf16[1024,2048]{1,0:T(8,128)(2,1)}, bf16[1024,2048]{1,0:T(8,128)(2,1)}, bf16[1024,512]{1,0:T(8,128)(2,1)S(1)}, bf16[1024,256]{1,0:T(8,128)(2,1)S(1)}) custom-call(s32[1]{0:T(128)} %bitcast.1.rank_ref, bf16[2048,768]{1,0:T(8,128)(2,1)} %all-gather.5.cloned.1.call-done.w_ref.refs_1_.refs_3_, f32[1,2048]{1,0:T(1,128)S(1)} %get-tuple-element.456.gain_ref, ...), custom_call_target="tpu_custom_call" | custom-call | flops 10350000128 | bytes 27000000 | tf_op jit(solution)/shard_map/project_qkv/pallas_call | solution.py:255
  185.0 12.3 %all-gather.9.cloned.1.call-done = bf16[2048,2048]{1,0:T(8,128)(2,1)} async-done(((bf16[2048,256]{1,0:T(8,128)(2,1)}), bf16[2048,2048]{1,0:T(8,128)(2,1)}) %all-gather.9.cloned.1.call-update) | async-done | bytes 8388624 | tf_op jit(solution)/shard_map/all_gather | solution.py:992
  210.7 14.2 %convolution_convert_fusion.4.dh_ref = bf16[1024,2048]{1,0:T(8,128)(2,1)} fusion(bf16[1024,2048]{1,0:T(8,128)(2,1)} %place_rows.1, bf16[2048,2048]{1,0:T(8,128)(2,1)} %all-gather.9.cloned.1.call-done), kind=kOutput, calls=%fused_computation.5 | convolution fusion | flops 8592031744 | bytes 16777216 | tf_op jit(solution)/shard_map/dot_general | solution.py:45
  232.3 19.7 %collective-permute-done.16.refs_7_.refs_2_ = bf16[1024,512]{1,0:T(8,128)(2,1)S(1)} collective-permute-done((bf16[1024,512]{1,0:T(8,128)(2,1)S(1)}, bf16[1024,512]{1,0:T(8,128)(2,1)S(1)}, u32[]{:S(2)}, u32[]{:S(2)}) %collective-permute-start.16) | collective-permute-done | bytes 1048608 | tf_op jit(solution)/shard_map/ppermute | solution.py:63
  263.4 14.7 %out_step.2.refs_0_ = f32[1024,2048]{1,0:T(8,128)} custom-call(s32[1]{0:T(128)} %bitcast.1.rank_ref, bf16[1024,2048]{1,0:T(8,128)(2,1)} %get-tuple-element.307.refs_0_, bf16[1024,512]{1,0:T(8,128)(2,1)S(1)} %constant_dynamic-update-slice_fusion.refs_1_.refs_0_, bf16[2048,2048]{1,0:T(8,128)(2,1)} %all-gather.11.cloned.1.call-done.refs_2_.refs_4_.refs_6_.refs_9_, ...), custom_call_target="tpu_custom_call" | custom-call | flops 8049999872 | bytes 21000000 | tf_op jit(solution)/shard_map/out_step/pallas_call | solution.py:661
  285.1 9.0 %out_step.3 = (f32[256,2048]{1,0:T(8,128)S(1)}, bf16[1024,2048]{1,0:T(8,128)(2,1)}) custom-call(s32[1]{0:T(128)} %bitcast.1.rank_ref, f32[1024,2048]{1,0:T(8,128)} %out_step.2.refs_0_, f32[1,2048]{1,0:T(1,128)S(1)} %get-tuple-element.455.refs_1_.gain_ref, bf16[1024,512]{1,0:T(8,128)(2,1)S(1)} %collective-permute-done.18.refs_2_.refs_3_, ...), custom_call_target="tpu_custom_call" | custom-call | flops 8049999872 | bytes 21000000 | tf_op jit(solution)/shard_map/out_step/pallas_call | solution.py:661
  295.4 24.6 %gate_and_back.1 = (bf16[1024,2048]{1,0:T(8,128)(2,1)S(1)}, bf16[1024,4096]{1,0:T(8,128)(2,1)}) custom-call(bf16[1024,2048]{1,0:T(8,128)(2,1)} %get-tuple-element.340.n_ref, bf16[2048,4096]{1,0:T(8,128)(2,1)} %all-gather.7.cloned.1.call-done.w_ref.refs_1_.refs_3_, bf16[1024,2048]{1,0:T(8,128)(2,1)} %convolution_convert_fusion.4.dh_ref), custom_call_target="tpu_custom_call" | custom-call | flops 31050000384 | bytes 81000000 | tf_op jit(solution)/shard_map/gate_and_back/pallas_call | solution.py:721
  322.1 11.1 %convolution_convert_fusion.2 = bf16[2048,2048]{1,0:T(8,128)(2,1)} fusion(bf16[1024,2048]{1,0:T(8,128)(2,1)S(1)} %get-tuple-element.343, bf16[1024,2048]{1,0:T(8,128)(2,1)S(1)} %copy-done.90), kind=kOutput, calls=%fused_computation.3 | convolution fusion | flops 8594128896 | bytes 16777216 | tf_op jit(solution)/shard_map/dot_general | solution.py:41
  337.1 10.5 %blocks_times.4 = bf16[256,2048]{1,0:T(8,128)(2,1)S(1)} custom-call(s32[1]{0:T(128)S(1)} %bitcast.40, bf16[1024,4096]{1,0:T(8,128)(2,1)} %get-tuple-element.339.refs_0_.refs_1_.refs_2_, bf16[2048,4096]{1,0:T(8,128)(2,1)} %all-gather.7.cloned.1.call-done.w_ref.refs_1_.refs_3_), custom_call_target="tpu_custom_call" | custom-call | flops 10350000128 | bytes 27000000 | tf_op jit(solution)/shard_map/blocks_times/pallas_call | solution.py:758
  350.1 19.4 %blocks_times.5 = (bf16[256,2048]{1,0:T(8,128)(2,1)S(1)}, bf16[256,2048]{1,0:T(8,128)(2,1)S(1)}, bf16[256,2048]{1,0:T(8,128)(2,1)S(1)}) custom-call(s32[3]{0:T(128)S(1)} %slice_bitcast_fusion.chunks_ref, bf16[1024,4096]{1,0:T(8,128)(2,1)} %get-tuple-element.339.refs_0_.refs_1_.refs_2_, bf16[1024,4096]{1,0:T(8,128)(2,1)} %get-tuple-element.339.refs_0_.refs_1_.refs_2_, ...), custom_call_target="tpu_custom_call" | custom-call | flops 25300000768 | bytes 66000000 | tf_op jit(solution)/shard_map/blocks_times/pallas_call | solution.py:758
  382.9 23.8 %convolution_convert_fusion = bf16[2048,4096]{1,0:T(8,128)(2,1)} fusion(bf16[1024,2048]{1,0:T(8,128)(2,1)S(1)} %copy-done.91, bf16[1024,4096]{1,0:T(8,128)(2,1)} %get-tuple-element.339.refs_0_.refs_1_.refs_2_), kind=kOutput, calls=%fused_computation | convolution fusion | flops 17188257792 | bytes 29360128 | tf_op jit(solution)/shard_map/dot_general | solution.py:41
  416.9 13.3 %convolution_convert_fusion.3 = bf16[1024,2048]{1,0:T(8,128)(2,1)} fusion(bf16[1024,2048]{1,0:T(8,128)(2,1)S(1)} %copy-done.58, bf16[2048,2048]{1,0:T(8,128)(2,1)} %all-gather.9.cloned.1.call-done), kind=kOutput, calls=%fused_computation.4 | convolution fusion | flops 8592031744 | bytes 16777216 | tf_op jit(solution)/shard_map/dot_general | solution.py:1065
  463.7 10.7 %all-to-all-done.1 = bf16[256,4,512]{2,0,1:T(8,128)(2,1)} async-done(((bf16[256,4,512]{2,0,1:T(8,128)(2,1)}), bf16[256,4,512]{2,0,1:T(8,128)(2,1)}, u32[]{:S(2)}, u32[]{:S(2)}) %all-to-all-start.1) | async-done | bytes 1048608 | tf_op jit(solution)/shard_map/all_to_all | solution.py:1075
  474.5 8.1 %all-to-all-start.2 = ((bf16[4,256,2048]{2,1,0:T(8,128)(2,1)}), bf16[4,256,2048]{2,1,0:T(8,128)(2,1)}, u32[]{:S(2)}, u32[]{:S(2)}) async-start(bf16[4,256,2048]{2,1,0:T(8,128)(2,1)} %bitcast.42), calls=%async_computation.4 | async-start | bytes 8388608 | tf_op jit(solution)/shard_map/all_to_all | solution.py:136
  485.3 21.4 %attend_back.2 = (bf16[1024,256]{1,0:T(8,128)(2,1)S(1)}, bf16[1024,128]{1,0:T(8,128)(2,1)S(1)}, bf16[1024,128]{1,0:T(8,128)(2,1)S(1)}, f32[1024,128]{1,0:T(8,128)S(1)}) custom-call(s32[1024]{0:T(1024)S(1)} %copy-done.21, bf16[1024,512]{1,0:T(8,128)(2,1)S(1)} %copy-done.62, bf16[1024,512]{1,0:T(8,128)(2,1)} %bitcast.9.do_ref, ...), custom_call_target="tpu_custom_call" | custom-call | flops 32199999488 | bytes 84000000 | tf_op jit(solution)/shard_map/attend_back/pallas_call | solution.py:535
  508.3 7.7 %collective-permute-start.26 = (bf16[1024,128]{1,0:T(8,128)(2,1)S(1)}, bf16[1024,128]{1,0:T(8,128)(2,1)S(1)}, u32[]{:S(2)}, u32[]{:S(2)}) collective-permute-start(bf16[1024,128]{1,0:T(8,128)(2,1)S(1)} %get-tuple-element.363), channel_id=1, source_target_pairs={{4,0},{8,4},{12,8},{20,16},{24,20},{28,24},{5,1},{9,5},{13,9},{21,... | collective-permute-start | bytes 786440 | tf_op jit(solution)/shard_map/ppermute | solution.py:173
  516.1 21.4 %attend_back.3 = (bf16[1024,256]{1,0:T(8,128)(2,1)S(1)}, bf16[1024,128]{1,0:T(8,128)(2,1)S(1)}, bf16[1024,128]{1,0:T(8,128)(2,1)S(1)}, f32[1024,128]{1,0:T(8,128)S(1)}) custom-call(s32[1024]{0:T(1024)S(1)} %copy-done.21, bf16[1024,512]{1,0:T(8,128)(2,1)S(1)} %copy-done.62, bf16[1024,512]{1,0:T(8,128)(2,1)} %bitcast.9.do_ref, ...), custom_call_target="tpu_custom_call" | custom-call | flops 32199999488 | bytes 84000000 | tf_op jit(solution)/shard_map/attend_back/pallas_call | solution.py:535
  538.8 8.0 %collective-permute-start.28 = (bf16[1024,128]{1,0:T(8,128)(2,1)S(1)}, bf16[1024,128]{1,0:T(8,128)(2,1)S(1)}, u32[]{:S(2)}, u32[]{:S(2)}) collective-permute-start(bf16[1024,128]{1,0:T(8,128)(2,1)S(1)} %get-tuple-element.373), channel_id=1, source_target_pairs={{4,0},{8,4},{12,8},{20,16},{24,20},{28,24},{5,1},{9,5},{13,9},{21,... | collective-permute-start | bytes 786440 | tf_op jit(solution)/shard_map/ppermute | solution.py:173
  597.4 13.6 %adam_interleaved.1 = (f32[2,256,2048]{2,1,0:T(8,128)}, f32[2,256,2048]{2,1,0:T(8,128)}, f32[2,256,2048]{2,1,0:T(8,128)}, f32[2,256,2048]{2,1,0:T(8,128)}, bf16[2,256,2048]{2,1,0:T(8,128)(2,1)}) custom-call(bf16[256,4096]{1,0:T(8,128)(2,1)S(1)} %copy-done.25, f32[2,256,2048]{2,1,0:T(8,128)} %w_ref.2, f32[2,256,2048]{2,1,0:T(8,128)} %m_ref.1, ...), custom_call_target="tpu_custom_call" | custom-call | flops 14949999616 | bytes 39000000 | tf_op jit(solution)/shard_map/adam_interleaved/pallas_call | solution.py:906
  641.7 17.4 %reduce-scatter.11.cloned.1.call-done = bf16[256,768]{1,0:T(8,128)(2,1)} async-done(((bf16[2048,768]{1,0:T(8,128)(2,1)}), bf16[256,768]{1,0:T(8,128)(2,1)}) %reduce-scatter.11.cloned.1.call-update) | async-done | bytes 393232 | tf_op jit(solution)/shard_map/reduce_scatter | solution.py:1114
  664.3 12.3 %collective-permute-done.38.refs_2_ = bf16[256,2048]{1,0:T(8,128)(2,1)} collective-permute-done((bf16[256,2048]{1,0:T(8,128)(2,1)}, bf16[256,2048]{1,0:T(8,128)(2,1)}, u32[]{:S(2)}, u32[]{:S(2)}) %collective-permute-start.38) | collective-permute-done | bytes 1048608 | tf_op jit(solution)/shard_map/ppermute | solution.py:120
  (346 shorter events, 317.8 us)
Async XLA Ops:
  7.2 91.9 %all-gather.5.cloned.1.call-start = ((), (), s32[]{:S(2)}) async-start(), calls=%async_computation.8 | async-start | bytes 3538944 | tf_op jit(solution)/shard_map/all_gather | solution.py:970
  9.2 152.0 %all-gather.7.cloned.1.call-start = ((), (), s32[]{:S(2)}) async-start(), calls=%async_computation.9 | async-start | bytes 18874368 | tf_op jit(solution)/shard_map/all_gather | solution.py:977
  45.0 152.3 %all-gather.9.cloned.1.call-start = ((), (), s32[]{:S(2)}) async-start(), calls=%async_computation.10 | async-start | bytes 9437184 | tf_op jit(solution)/shard_map/all_gather | solution.py:992
  127.2 33.1 %collective-permute-start.9 = (bf16[1024,256]{1,0:T(8,128)(2,1)S(1)}, bf16[1024,256]{1,0:T(8,128)(2,1)S(1)}, u32[]{:S(2)}, u32[]{:S(2)}) collective-permute-start(bf16[1024,256]{1,0:T(8,128)(2,1)S(1)} %get-tuple-element.265.here), channel_id=1, source_target_pairs={{0,4},{4,8},{8,12},{16,20},{20,24},{24,28},{1,5},{5,9},{9,13},{17,... | collective-permute-start | bytes 1572872 | tf_op jit(solution)/shard_map/ppermute | solution.py:173
  129.2 31.2 %collective-permute-start.8 = (bf16[1024,256]{1,0:T(8,128)(2,1)S(1)}, bf16[1024,256]{1,0:T(8,128)(2,1)S(1)}, u32[]{:S(2)}, u32[]{:S(2)}) collective-permute-start(bf16[1024,256]{1,0:T(8,128)(2,1)S(1)} %get-tuple-element.265.here), channel_id=1, source_target_pairs={{0,8},{4,12},{16,24},{20,28},{1,9},{5,13},{17,25},{21,29},{2,10},{... | collective-permute-start | bytes 1572872 | tf_op jit(solution)/shard_map/ppermute | solution.py:173
  130.5 30.7 %collective-permute-start.10 = (bf16[256,2048]{1,0:T(8,128)(2,1)}, bf16[256,2048]{1,0:T(8,128)(2,1)S(1)}, u32[]{:S(2)}, u32[]{:S(2)}) collective-permute-start(bf16[256,2048]{1,0:T(8,128)(2,1)} %collective-permute-done.6.refs_1_), channel_id=1, source_target_pairs={{1,2},{2,3},{5,6},{6,7},{9,10},{10,11},{13,14},{14,15},{17,18},{18... | collective-permute-start | bytes 3145736 | tf_op jit(solution)/shard_map/ppermute | solution.py:63
  132.7 28.4 %collective-permute-start.11 = (bf16[256,2048]{1,0:T(8,128)(2,1)}, bf16[256,2048]{1,0:T(8,128)(2,1)}, u32[]{:S(2)}, u32[]{:S(2)}) collective-permute-start(bf16[256,2048]{1,0:T(8,128)(2,1)} %collective-permute-done.7.refs_4_), channel_id=1, source_target_pairs={{1,0},{2,1},{5,4},{6,5},{9,8},{10,9},{13,12},{14,13},{17,16},{18,1... | collective-permute-start | bytes 3145736 | tf_op jit(solution)/shard_map/ppermute | solution.py:64
  154.6 30.3 %all-to-all-start = ((bf16[4,512,256]{2,1,0:T(8,128)(2,1)}), bf16[4,512,256]{2,1,0:T(8,128)(2,1)}, u32[]{:S(2)}, u32[]{:S(2)}) async-start(bf16[4,512,256]{2,1,0:T(8,128)(2,1)} %broadcast_in_dim.5), calls=%async_computation | async-start | bytes 2097152 | tf_op jit(solution)/shard_map/all_to_all | solution.py:130
  160.4 98.4 %all-gather.11.cloned.1.call-start = ((), (), s32[]{:S(2)}) async-start(), calls=%async_computation.11 | async-start | bytes 9437184 | tf_op jit(solution)/shard_map/all_gather | solution.py:1015
  161.2 36.1 %collective-permute-start.12 = (bf16[256,2048]{1,0:T(8,128)(2,1)S(1)}, bf16[256,2048]{1,0:T(8,128)(2,1)}, u32[]{:S(2)}, u32[]{:S(2)}) collective-permute-start(bf16[256,2048]{1,0:T(8,128)(2,1)S(1)} %collective-permute-done.10.refs_2_), channel_id=1, source_target_pairs={{2,3},{6,7},{10,11},{14,15},{18,19},{22,23},{26,27},{30,31}} | collective-permute-start | bytes 3145736 | tf_op jit(solution)/shard_map/ppermute | solution.py:63
  162.9 34.4 %collective-permute-start.13 = (bf16[256,2048]{1,0:T(8,128)(2,1)}, bf16[256,2048]{1,0:T(8,128)(2,1)}, u32[]{:S(2)}, u32[]{:S(2)}) collective-permute-start(bf16[256,2048]{1,0:T(8,128)(2,1)} %collective-permute-done.11.refs_5_), channel_id=1, source_target_pairs={{1,0},{5,4},{9,8},{13,12},{17,16},{21,20},{25,24},{29,28}} | collective-permute-start | bytes 3145736 | tf_op jit(solution)/shard_map/ppermute | solution.py:64
  197.3 277.1 %reduce-scatter.5.cloned.1.call-start = ((), (), s32[]{:S(2)}) async-start(), calls=%async_computation.12 | async-start | bytes 9437184 | tf_op jit(solution)/shard_map/reduce_scatter | solution.py:1048
  333.3 224.4 %reduce-scatter.7.cloned.1.call-start = ((), (), s32[]{:S(2)}) async-start(), calls=%async_computation.13 | async-start | bytes 18874368 | tf_op jit(solution)/shard_map/reduce_scatter | solution.py:1063
  377.1 29.7 %collective-permute-start.23 = (bf16[256,2048]{1,0:T(8,128)(2,1)}, bf16[256,2048]{1,0:T(8,128)(2,1)}, u32[]{:S(2)}, u32[]{:S(2)}) collective-permute-start(bf16[256,2048]{1,0:T(8,128)(2,1)} %get-tuple-element.449), channel_id=1, source_target_pairs={{2,1},{3,2},{6,5},{7,6},{10,9},{11,10},{14,13},{15,14},{18,17},{19... | collective-permute-start | bytes 3145736 | tf_op jit(solution)/shard_map/ppermute | solution.py:120
  378.3 28.4 %collective-permute-start.22 = (bf16[256,2048]{1,0:T(8,128)(2,1)}, bf16[256,2048]{1,0:T(8,128)(2,1)}, u32[]{:S(2)}, u32[]{:S(2)}) collective-permute-start(bf16[256,2048]{1,0:T(8,128)(2,1)} %get-tuple-element.450), channel_id=1, source_target_pairs={{0,1},{1,2},{4,5},{5,6},{8,9},{9,10},{12,13},{13,14},{16,17},{17,1... | collective-permute-start | bytes 3145736 | tf_op jit(solution)/shard_map/ppermute | solution.py:119
  453.9 161.7 %reduce-scatter.9.cloned.1.call-start = ((), (), s32[]{:S(2)}) async-start(), calls=%async_computation.14 | async-start | bytes 9437184 | tf_op jit(solution)/shard_map/reduce_scatter | solution.py:1079
  474.5 107.7 %all-to-all-start.2 = ((bf16[4,256,2048]{2,1,0:T(8,128)(2,1)}), bf16[4,256,2048]{2,1,0:T(8,128)(2,1)}, u32[]{:S(2)}, u32[]{:S(2)}) async-start(bf16[4,256,2048]{2,1,0:T(8,128)(2,1)} %bitcast.42), calls=%async_computation.4 | async-start | bytes 8388608 | tf_op jit(solution)/shard_map/all_to_all | solution.py:136
  482.6 176.5 %reduce-scatter.11.cloned.1.call-start = ((), (), s32[]{:S(2)}) async-start(), calls=%async_computation.15 | async-start | bytes 3538944 | tf_op jit(solution)/shard_map/reduce_scatter | solution.py:1114
  506.8 30.7 %collective-permute-start.27 = (bf16[1024,128]{1,0:T(8,128)(2,1)S(1)}, bf16[1024,128]{1,0:T(8,128)(2,1)S(1)}, u32[]{:S(2)}, u32[]{:S(2)}) collective-permute-start(bf16[1024,128]{1,0:T(8,128)(2,1)S(1)} %get-tuple-element.362), channel_id=1, source_target_pairs={{8,0},{12,4},{24,16},{28,20},{9,1},{13,5},{25,17},{29,21},{10,2},{... | collective-permute-start | bytes 786440 | tf_op jit(solution)/shard_map/ppermute | solution.py:173
  508.3 29.2 %collective-permute-start.26 = (bf16[1024,128]{1,0:T(8,128)(2,1)S(1)}, bf16[1024,128]{1,0:T(8,128)(2,1)S(1)}, u32[]{:S(2)}, u32[]{:S(2)}) collective-permute-start(bf16[1024,128]{1,0:T(8,128)(2,1)S(1)} %get-tuple-element.363), channel_id=1, source_target_pairs={{4,0},{8,4},{12,8},{20,16},{24,20},{28,24},{5,1},{9,5},{13,9},{21,... | collective-permute-start | bytes 786440 | tf_op jit(solution)/shard_map/ppermute | solution.py:173
  592.7 27.8 %collective-permute-start.32 = (bf16[256,2048]{1,0:T(8,128)(2,1)}, bf16[256,2048]{1,0:T(8,128)(2,1)S(1)}, u32[]{:S(2)}, u32[]{:S(2)}) collective-permute-start(bf16[256,2048]{1,0:T(8,128)(2,1)} %get-tuple-element.448), channel_id=1, source_target_pairs={{0,1},{1,2},{4,5},{5,6},{8,9},{9,10},{12,13},{13,14},{16,17},{17,1... | collective-permute-start | bytes 3145736 | tf_op jit(solution)/shard_map/ppermute | solution.py:119
  624.4 52.2 %all-to-all-start.3 = ((bf16[4,512,256]{2,1,0:T(8,128)(2,1)}), bf16[4,512,256]{2,1,0:T(8,128)(2,1)}, u32[]{:S(2)}, u32[]{:S(2)}) async-start(bf16[4,512,256]{2,1,0:T(8,128)(2,1)} %bitcast.44), calls=%async_computation.6 | async-start | bytes 2097152 | tf_op jit(solution)/shard_map/all_to_all | solution.py:136
  634.3 42.3 %collective-permute-start.38 = (bf16[256,2048]{1,0:T(8,128)(2,1)}, bf16[256,2048]{1,0:T(8,128)(2,1)}, u32[]{:S(2)}, u32[]{:S(2)}) collective-permute-start(bf16[256,2048]{1,0:T(8,128)(2,1)} %get-tuple-element.451), channel_id=1, source_target_pairs={{1,0},{2,1},{3,2},{5,4},{6,5},{7,6},{9,8},{10,9},{11,10},{13,12},{... | collective-permute-start | bytes 3145736 | tf_op jit(solution)/shard_map/ppermute | solution.py:120
  636.4 40.2 %collective-permute-start.37 = (bf16[256,2048]{1,0:T(8,128)(2,1)}, bf16[256,2048]{1,0:T(8,128)(2,1)}, u32[]{:S(2)}, u32[]{:S(2)}) collective-permute-start(bf16[256,2048]{1,0:T(8,128)(2,1)} %get-tuple-element.452), channel_id=1, source_target_pairs={{0,1},{1,2},{2,3},{4,5},{5,6},{6,7},{8,9},{9,10},{10,11},{12,13},{... | collective-permute-start | bytes 3145736 | tf_op jit(solution)/shard_map/ppermute | solution.py:119
  (122 other events, 2061.5 us)
Sparse Core Ops, SparseCore 0:
  10.5 33.4 all-gather.4
  46.4 89.8 all-gather.6
  138.8 58.4 all-gather.8
  199.0 59.6 all-gather.10
  333.4 72.6 reduce-scatter.4
  409.9 121.1 reduce-scatter.6
  535.0 74.3 reduce-scatter.8
  612.8 46.2 reduce-scatter.10

commit v4 on v3

--- a/solution.py
+++ b/solution.py
@@ -360,8 +360,8 @@
 def attend_here_kernel(tk, pos_ref, q_ref, back_ref, here, acc_ref, top_ref, vx, qs):
     tokens = here.shape[0]
     tq = q_ref.shape[0]
-    tile = pl.program_id(0)
-    acc, top = acc_ref.at[0], top_ref.at[0]
+    tile = pl.program_id(1)
+    acc, top = acc_ref.at[0, 0], top_ref.at[0, 0]
 
     @pl.when(tile == 0)
     def _():
@@ -385,15 +385,15 @@
 ):
     tokens = far_one.shape[0]
     tq = q_ref.shape[0]
-    tile = pl.program_id(0)
+    tile = pl.program_id(1)
 
     @pl.when(tile == 0)
     def _():
         load_sources((far_two, far_one), kv, vx)
 
     qs[...] = stack_heads(q_ref[...], True)
-    acc[...] = acc_ref[0]
-    top[...] = top_ref[0]
+    acc[...] = acc_ref[0, 0]
+    top[...] = top_ref[0, 0]
 
     def step(key, masked):
         attend_step(key, masked, tile, tk, 0, back_ref, kv, vx, qs, acc, top, tokens)
@@ -404,26 +404,29 @@
     blocks = unstack_heads(jnp.transpose(total / weight), False)
     out_ref[...] = jnp.concatenate(blocks, axis=1).astype(jnp.bfloat16)
     lse = top[0:1, :] * EXP_SCALE + jnp.log2(weight)
-    lse_ref[...] = jnp.broadcast_to(lse, (8, lse.shape[1]))[None]
-
-
-def attend_here(queries, here, positions, back_rows, group, tq, tk):
+    lse_ref[...] = jnp.broadcast_to(lse, (8, lse.shape[1]))[None, None]
+
+
+def attend_here(queries, here, positions, back_rows, tq, tk):
     tokens = queries.shape[0]
+    groups = queries.shape[1] // (QPK * HD)
     state = (
-        jax.ShapeDtypeStruct((tokens // tq, 2 * HD, QPK * tq), jnp.float32),
-        jax.ShapeDtypeStruct((tokens // tq, 8, QPK * tq), jnp.float32),
+        jax.ShapeDtypeStruct((groups, tokens // tq, 2 * HD, QPK * tq), jnp.float32),
+        jax.ShapeDtypeStruct((groups, tokens // tq, 8, QPK * tq), jnp.float32),
     )
     return pl.pallas_call(
         functools.partial(attend_here_kernel, tk),
         grid_spec=pltpu.PrefetchScalarGridSpec(
             num_scalar_prefetch=1,
-            grid=(tokens // tq,),
+            grid=(groups, tokens // tq),
             in_specs=[
-                pl.BlockSpec((tq, QPK * HD), lambda i, p: (i, group)),
-                pl.BlockSpec((8, tq), lambda i, p: (0, i)),
-                pl.BlockSpec((tokens, 2 * HD), lambda i, p: (0, group)),
+                pl.BlockSpec((tq, QPK * HD), lambda g, i, p: (i, g)),
+                pl.BlockSpec((8, tq), lambda g, i, p: (0, i)),
+                pl.BlockSpec((tokens, 2 * HD), lambda g, i, p: (0, g)),
             ],
-            out_specs=[pl.BlockSpec((1, *shape.shape[1:]), lambda i, p: (i, 0, 0)) for shape in state],
+            out_specs=[
+                pl.BlockSpec((1, 1, *shape.shape[2:]), lambda g, i, p: (g, i, 0, 0)) for shape in state
+            ],
             scratch_shapes=[
                 pltpu.VMEM((tokens, 2 * HD), jnp.bfloat16),
                 pltpu.VMEM((QPK * tq, 2 * HD), jnp.bfloat16),
@@ -431,29 +434,32 @@
         ),
         out_shape=state,
         compiler_params=pltpu.CompilerParams(vmem_limit_bytes=VMEM_LIMIT),
-        cost_estimate=cost(10),
+        cost_estimate=cost(15),
         name="attend_here",
     )(positions, queries, back_rows, here)
 
 
-def attend_far(queries, far, state, positions, back_rows, group, tq, tk):
+def attend_far(queries, far, state, positions, back_rows, tq, tk):
     tokens = queries.shape[0]
-    kv_spec = pl.BlockSpec((tokens, 2 * HD), lambda i, p: (0, group))
+    groups = queries.shape[1] // (QPK * HD)
+    kv_spec = pl.BlockSpec((tokens, 2 * HD), lambda g, i, p: (0, g))
     return pl.pallas_call(
         functools.partial(attend_far_kernel, tk),
         grid_spec=pltpu.PrefetchScalarGridSpec(
             num_scalar_prefetch=1,
-            grid=(tokens // tq,),
+            grid=(groups, tokens // tq),
             in_specs=[
-                pl.BlockSpec((tq, QPK * HD), lambda i, p: (i, group)),
-                pl.BlockSpec((8, tq), lambda i, p: (0, i)),
+                pl.BlockSpec((tq, QPK * HD), lambda g, i, p: (i, g)),
+                pl.BlockSpec((8, tq), lambda g, i, p: (0, i)),
                 kv_spec,
                 kv_spec,
             ]
-            + [pl.BlockSpec((1, *part.shape[1:]), lambda i, p: (i, 0, 0)) for part in state],
+            + [
+                pl.BlockSpec((1, 1, *part.shape[2:]), lambda g, i, p: (g, i, 0, 0)) for part in state
+            ],
             out_specs=[
-                pl.BlockSpec((tq, QPK * HD), lambda i, p: (i, 0)),
-                pl.BlockSpec((1, 8, QPK * tq), lambda i, p: (i, 0, 0)),
+                pl.BlockSpec((tq, QPK * HD), lambda g, i, p: (i, g)),
+                pl.BlockSpec((1, 1, 8, QPK * tq), lambda g, i, p: (g, i, 0, 0)),
             ],
             scratch_shapes=[
                 pltpu.VMEM((REACH * tokens, 2 * HD), jnp.bfloat16),
@@ -464,11 +470,11 @@
             ],
         ),
         out_shape=[
-            jax.ShapeDtypeStruct((tokens, QPK * HD), jnp.bfloat16),
-            jax.ShapeDtypeStruct((tokens // tq, 8, QPK * tq), jnp.float32),
+            jax.ShapeDtypeStruct((tokens, groups * QPK * HD), jnp.bfloat16),
+            jax.ShapeDtypeStruct((groups, tokens // tq, 8, QPK * tq), jnp.float32),
         ],
         compiler_params=pltpu.CompilerParams(vmem_limit_bytes=VMEM_LIMIT),
-        cost_estimate=cost(14),
+        cost_estimate=cost(21),
         name="attend_far",
     )(positions, queries, back_rows, *far, *state)
 
@@ -492,7 +498,7 @@
     dq[...] = jnp.zeros_like(dq)
     product = dos[...].astype(jnp.float32) * stack_heads(o_ref[...], False).astype(jnp.float32)
     delta = jnp.sum(jnp.transpose(product), axis=0, keepdims=True)
-    lse = lse_ref[0, 0:1, :]
+    lse = lse_ref[0, 0, 0:1, :]
 
     def step(key, masked):
         keys = kv[pl.ds(key, tk), :]
@@ -540,9 +546,9 @@
             in_specs=[
                 q_spec,
                 q_spec,
-                own_q,
+                q_spec,
                 pl.BlockSpec((8, tq), lambda i, p: (0, i)),
-                pl.BlockSpec((1, 8, QPK * tq), lambda i, p: (i, 0, 0)),
+                pl.BlockSpec((1, 1, 8, QPK * tq), lambda i, p: (group, i, 0, 0)),
                 angle_spec,
                 angle_spec,
                 kv_spec,
@@ -794,6 +800,106 @@
         name="row_products",
     )(part, weight)
     return sums[0]
+
+
+def norm_back_rows(vector, grad_in, gain):
+    inverse = lax.rsqrt(jnp.mean(vector * vector, axis=1, keepdims=True) + NORM_EPS)
+    scaled = grad_in * gain
+    mean = jnp.mean(vector * scaled, axis=1, keepdims=True)
+    grad = inverse * scaled - vector * (inverse * inverse * inverse * mean)
+    return grad, jnp.sum(grad_in * vector * inverse, axis=0, keepdims=True)
+
+
+def sum_refs(refs):
+    total = refs[0][...].astype(jnp.float32)
+    for ref in refs[1:]:
+        total = total + ref[...].astype(jnp.float32)
+    return total
+
+
+def mid_kernel(mid_ref, dy_ref, gain_ref, *refs):
+    *parts, d_mid_ref, branch_ref, gain_grad_ref = refs
+    grad, gain_grad = norm_back_rows(mid_ref[...], sum_refs(parts), gain_ref[...])
+    d_mid = dy_ref[...].astype(jnp.float32) + grad
+    d_mid_ref[...] = d_mid
+    branch_ref[...] = d_mid.astype(jnp.bfloat16)
+    gain_grad = jnp.broadcast_to(gain_grad, gain_grad_ref.shape)
+
+    @pl.when(pl.program_id(0) == 0)
+    def _():
+        gain_grad_ref[...] = gain_grad
+
+    @pl.when(pl.program_id(0) > 0)
+    def _():
+        gain_grad_ref[...] += gain_grad
+
+
+def back_to_mid(parts, mid, output_grad, gain):
+    own, width = output_grad.shape
+    tile = min(64, own)
+    rows = pl.BlockSpec((tile, width), lambda i: (i, 0))
+    outs = pl.pallas_call(
+        mid_kernel,
+        grid=(own // tile,),
+        in_specs=[rows, rows, pl.BlockSpec((1, width), lambda i: (0, 0))] + [rows] * len(parts),
+        out_specs=[rows, rows, pl.BlockSpec((8, width), lambda i: (0, 0))],
+        out_shape=[
+            jax.ShapeDtypeStruct((own, width), jnp.float32),
+            jax.ShapeDtypeStruct((own, width), jnp.bfloat16),
+            jax.ShapeDtypeStruct((8, width), jnp.float32),
+        ],
+        compiler_params=pltpu.CompilerParams(vmem_limit_bytes=VMEM_LIMIT),
+        cost_estimate=cost(4),
+        name="back_to_mid",
+    )(mid, output_grad, gain[None], *parts)
+    return outs[0], outs[1], outs[2][0]
+
+
+def input_kernel(x_ref, d_mid_ref, gain_ref, *refs):
+    *parts, out_ref = refs
+    x = x_ref[...].astype(jnp.float32)
+    grad, _ = norm_back_rows(x, sum_refs(parts), gain_ref[...])
+    out_ref[...] = d_mid_ref[...] + grad
+
+
+def back_to_input(parts, layer_input, d_mid, gain):
+    own, width = layer_input.shape
+    tile = min(64, own)
+    rows = pl.BlockSpec((tile, width), lambda i: (i, 0))
+    return pl.pallas_call(
+        input_kernel,
+        grid=(own // tile,),
+        in_specs=[rows, rows, pl.BlockSpec((1, width), lambda i: (0, 0))] + [rows] * len(parts),
+        out_specs=rows,
+        out_shape=jax.ShapeDtypeStruct((own, width), jnp.float32),
+        compiler_params=pltpu.CompilerParams(vmem_limit_bytes=VMEM_LIMIT),
+        cost_estimate=cost(4),
+        name="back_to_input",
+    )(layer_input, d_mid, gain[None], *parts)
+
+
+def round_kernel(wide, w_ref, out_ref):
+    for block in range(w_ref.shape[2] // wide):
+        for half in range(2):
+            column = (2 * block + half) * wide
+            out_ref[:, column : column + wide] = w_ref[
+                half, :, block * wide : (block + 1) * wide
+            ].astype(jnp.bfloat16)
+
+
+def round_interleaved(weight, wide):
+    _, rows, units = weight.shape
+    tile = min(64, rows)
+    return pl.pallas_call(
+        functools.partial(round_kernel, wide),
+        grid=(rows // tile,),
+        in_specs=[pl.BlockSpec((2, tile, units), lambda i: (0, i, 0))],
+        out_specs=pl.BlockSpec((tile, 2 * units), lambda i: (i, 0)),
+        out_shape=jax.ShapeDtypeStruct((rows, 2 * units), jnp.bfloat16),
+        compiler_params=pltpu.CompilerParams(vmem_limit_bytes=VMEM_LIMIT),
+        cost_estimate=cost(3),
+        name="round_interleaved",
+    )(weight)
 
 
 def norm_back_rows(vector, grad_in, gain):
@@ -990,31 +1096,23 @@
     made, dy_line.moving, low_out, low_down = close((made, dy_line.moving, low_out, low_down))
     x_rows, normed_one, queries, kv = made
     w_down = lax.all_gather(low_down, "seq", axis=1, tiled=True)
-    out_strip = swap_gather(low_out, "tp")
     far = [along_sequence(kv, distance, tokens) for distance in (2, 1)]
     if dy_line.hops > 1:
         dy_line.hop()
-    states = [
-        attend_here(queries, kv, positions, back_rows, group, 256, 512) for group in range(groups)
-    ]
+    states = attend_here(queries, kv, positions, back_rows, 256, 512)
+    out_strip = swap_gather(after(low_out, states[1]), "tp")
     far, states, queries, w_gate_up, dy_line.moving = close(
         (far, states, queries, w_gate_up, dy_line.moving)
     )
     for _ in range(2, dy_line.hops):
         dy_line.hop()
-    attn, lse = [], []
-    for group in range(groups):
-        out, log_total = attend_far(
-            queries, far, states[group], positions, back_rows, group, 256, 512
-        )
-        attn.append(out)
-        lse.append(log_total)
-    attn, lse, dy_pieces, w_down, x_rows, out_strip = close(
-        (attn, lse, dy_line.pieces, w_down, x_rows, out_strip)
+    attn, lse = attend_far(queries, far, states, positions, back_rows, 256, 512)
+    attn, lse, dy_pieces, x_rows, out_strip = close(
+        (attn, lse, dy_line.pieces, x_rows, out_strip)
     )
     w_out = lax.all_gather(out_strip.reshape(-1, low_out.shape[1]), "seq", axis=1, tiled=True)
 
-    heads_line = LineGather(jnp.concatenate(attn, axis=1), "tp")
+    heads_line = LineGather(attn, "tp")
     arrived = [(0, [heads_line.from_low[0]])]
     total = x_rows
     for index in range(heads_line.hops):
@@ -1082,7 +1180,7 @@
     travelled = []
     for group in range(groups):
         made = attend_back(
-            queries, d_attn, attn[group], lse[group], [*far, kv], positions, back_rows,
+            queries, d_attn, attn, lse, [*far, kv], positions, back_rows,
             cos, sin, group, 256, 512,
         )
         made, d_attn, travelled = close((made, d_attn, travelled))
@@ -1113,21 +1211,19 @@
             in_line.made += made
             qkv_grad = lax.psum_scatter(qkv_grad, "seq", scatter_dimension=0, tiled=True)
         elif index == 1:
+            outputs = (mid + sum_parts(result)).astype(low)
+            gains_grad = sum_by_swaps(gains_grad, "seq")
+            in_line.moving, outputs, gains_grad, out_grad, gate_up_grad = close(
+                (in_line.moving, outputs, gains_grad, out_grad, gate_up_grad)
+            )
+            out_parts = swap_scatter_parts(out_grad, "tp")
+        elif index == 2:
             gate_up_new = adam_interleaved(
                 gate_up_grad, gate_up_weight, gate_up_moment, gate_up_square, wide
             )
-            gains_grad = sum_by_swaps(gains_grad, "seq")
-            in_line.moving, gate_up_new, gains_grad, out_grad = close(
-                (in_line.moving, gate_up_new, gains_grad, out_grad)
-            )
-            out_parts = swap_scatter_parts(out_grad, "tp")
-        elif index == 2:
-            gains_grad = sum_at_once(gains_grad, "tp")
-            outputs = (mid + sum_parts(result)).astype(low)
-            qkv_grad = qkv_grad.astype(full)
-            qkv_new = adam_step(qkv_weight, qkv_grad, qkv_moment, qkv_square)
-            in_line.moving, gains_grad, out_parts, outputs, qkv_grad, qkv_new = close(
-                (in_line.moving, gains_grad, out_parts, outputs, qkv_grad, qkv_new)
+            gains_grad = sum_at_once(after(gains_grad, gate_up_new[4]), "tp")
+            in_line.moving, gains_grad, out_parts, gate_up_new = close(
+                (in_line.moving, gains_grad, out_parts, gate_up_new)
             )
         else:
             in_line.moving = close(in_line.moving)
@@ -1136,6 +1232,8 @@
     out_new = adam_step(out_weight, out_grad, out_moment, out_square)
 
     out_grad = out_grad.astype(full)
+    qkv_grad = qkv_grad.astype(full)
+    qkv_new = adam_step(qkv_weight, qkv_grad, qkv_moment, qkv_square)
     gains_new = adam_step(norm_gains, gains_grad, gains_moment, gains_square)
     return (
         outputs,

time: 705 us -> 697 us (0.989)
    reduce_scatter x1, waiting for transfers between devices: 17.4 us -> 0.01 us  [local(): lax.psum_scatter(qkv_grad, 'seq', scatter_dimension=0, tiled=True)]
    ppermute x3, waiting for transfers between devices: 0.01 us -> 16.4 us  [sum_at_once(): came.append(lax.ppermute(block, axis, route))]
    all_gather x1, waiting for transfers between devices: 12.3 us -> 0.01 us  [local(): w_down = lax.all_gather(low_down, 'seq', axis=1, tiled=True)]
    ppermute x6, waiting for transfers between devices: 21.3 us -> 9 us  [hop(): lax.ppermute(to_low, self.axis, [(i, i - 1) for i in range(size - step, s...]
    all_gather x1, waiting for transfers between devices: 2.5 us -> 13.9 us  [local(): lax.all_gather(out_strip.reshape(-1, low_out.shape[1]), 'seq', axis=1, ti...]
    pallas_call x2 -> x1, Pallas kernels: 15 us -> 14.5 us  [attend_here(): pl.pallas_call(functools.partial(attend_here_kernel, tk), grid_spec=pltpu...]
    unnamed x185 -> x166, local copies, waits for them, and re-layouts: 32.2 us -> 32.1 us
  transfers between devices with their start and end apart: 54 -> 54, of which waited for: 22 -> 24; matrix products, arithmetic and copies ran while one was open for 15% -> 15% of each run, Pallas kernels for 25% -> 26%
where the time goes in v4:
time: 697 us; the launch traced here: 686 us
  Pallas kernels  213 us (31%)
  waiting for transfers between devices  177 us (25%)
  starting transfers between devices  125 us (18%)
  matrix products  76.7 us (11%)
  other arithmetic  39.3 us (6%)
  local copies, waits for them, and re-layouts  36.7 us (5%)
  between operations  18 us (3%)
    ppermute x9, waiting for transfers between devices, hop(): self.from_high.append(lax.ppermute(self.from_high[-1], self.axis, down))  66.2 us
    dot_general x4, matrix products, contract_rows(): lax.dot_general(left, right, ROWS_BY_ROWS, preferred_element_type=jnp.flo...  47 us
    pallas_call x2, Pallas kernels, attend_back(): pl.pallas_call(functools.partial(attend_back_kernel, tk), grid_spec=pltpu...  43 us
    pallas_call x4, Pallas kernels, blocks_times(): pl.pallas_call(blocks_kernel, grid_spec=pltpu.PrefetchScalarGridSpec(num_...  38.3 us
    ppermute x9, waiting for transfers between devices, hop(): self.from_low.append(lax.ppermute(self.from_low[-1], self.axis, up))  34.8 us
    unnamed x166, local copies, waits for them, and re-layouts  32.1 us
    ppermute x9, starting transfers between devices, hop(): self.from_high.append(lax.ppermute(self.from_high[-1], self.axis, down))  26.8 us
    pallas_call x1, Pallas kernels, gate_and_back(): pl.pallas_call(gate_kernel, grid=(units // wide, tokens // tile), in_spec...  24.7 us
  transfers between devices with their start and end apart: 54, of which 24 were waited for; matrix products, arithmetic and copies ran while one was open for 15% of the time, Pallas kernels for 26%

profile of v4, /device:TPU:10, one launch (start us, length us, event | category | flops | bytes accessed | tf_op | source)
XLA Modules:
  0.0 686.4 jit_solution(5293918079431161748)
XLA Ops:
  15.3 21.1 %collective-permute-done.1.refs_4_ = bf16[256,2048]{1,0:T(8,128)(2,1)S(1)} collective-permute-done((bf16[256,2048]{1,0:T(8,128)(2,1)}, bf16[256,2048]{1,0:T(8,128)(2,1)S(1)}, u32[]{:S(2)}, u32[]{:S(2)}) %collective-permute-start.1) | collective-permute-done | bytes 1048608 | tf_op jit(solution)/shard_map/ppermute | solution.py:64
  56.1 13.8 %collective-permute-done.2.refs_2_ = bf16[256,2048]{1,0:T(8,128)(2,1)S(1)} collective-permute-done((bf16[256,2048]{1,0:T(8,128)(2,1)S(1)}, bf16[256,2048]{1,0:T(8,128)(2,1)S(1)}, u32[]{:S(2)}, u32[]{:S(2)}) %collective-permute-start.2) | collective-permute-done | bytes 1048608 | tf_op jit(solution)/shard_map/ppermute | solution.py:63
  80.2 18.8 %collective-permute-done.5.refs_6_ = bf16[256,2048]{1,0:T(8,128)(2,1)} collective-permute-done((bf16[256,2048]{1,0:T(8,128)(2,1)}, bf16[256,2048]{1,0:T(8,128)(2,1)}, u32[]{:S(2)}, u32[]{:S(2)}) %collective-permute-start.5) | collective-permute-done | bytes 1048608 | tf_op jit(solution)/shard_map/ppermute | solution.py:64
  109.1 10.5 %project_qkv.1 = (bf16[1024,2048]{1,0:T(8,128)(2,1)}, bf16[1024,2048]{1,0:T(8,128)(2,1)}, bf16[1024,512]{1,0:T(8,128)(2,1)S(1)}, bf16[1024,256]{1,0:T(8,128)(2,1)S(1)}) custom-call(s32[1]{0:T(128)} %bitcast.2.rank_ref, bf16[2048,768]{1,0:T(8,128)(2,1)} %all-gather.5.cloned.1.call-done.w_ref.refs_1_.refs_3_, f32[1,2048]{1,0:T(1,128)S(1)} %get-tuple-element.437.gain_ref, ...), custom_call_target="tpu_custom_call" | custom-call | flops 10350000128 | bytes 27000000 | tf_op jit(solution)/shard_map/project_qkv/pallas_call | solution.py:255
  136.0 14.5 %attend_here.1 = (f32[2,4,128,1024]{3,2,1,0:T(8,128)S(1)}, f32[2,4,8,1024]{3,2,1,0:T(8,128)S(1)}) custom-call(s32[1024]{0:T(1024)S(1)} %copy-done.16, bf16[1024,512]{1,0:T(8,128)(2,1)S(1)} %copy-done.54, s32[8,1024]{1,0:T(8,128)S(1)} %broadcast_in_dim.4.back_ref, bf16[1024,256]{1,0:T(8,128)(2,1)S(1)} %get-tuple-element.255.here), custom_call_target="tpu_custom_call" | custom-call | flops 17250000896 | bytes 45000000 | tf_op jit(solution)/shard_map/attend_here/pallas_call | solution.py:417
  168.9 13.8 %attend_far.1 = (bf16[1024,512]{1,0:T(8,128)(2,1)S(1)}, f32[2,4,8,1024]{3,2,1,0:T(8,128)S(1)}) custom-call(s32[1024]{0:T(1024)S(1)} %copy-done.16, bf16[1024,512]{1,0:T(8,128)(2,1)S(1)} %copy-done.55, s32[8,1024]{1,0:T(8,128)S(1)} %broadcast_in_dim.4.back_ref, bf16[1024,256]{1,0:T(8,128)(2,1)S(1)} %copy-done.39, bf16[1024,256]{1,0:T(8,128)(2,1)S(1)} %copy-done.36, ...), custom_call_target="tpu_custom_call" | custom-call | flops 24149999616 | bytes 63000000 | tf_op jit(solution)/shard_map/attend_far/pallas_call | solution.py:446
  183.4 9.0 %collective-permute-done.13.refs_6_ = bf16[256,2048]{1,0:T(8,128)(2,1)} collective-permute-done((bf16[256,2048]{1,0:T(8,128)(2,1)}, bf16[256,2048]{1,0:T(8,128)(2,1)}, u32[]{:S(2)}, u32[]{:S(2)}) %collective-permute-start.13) | collective-permute-done | bytes 1048608 | tf_op jit(solution)/shard_map/ppermute | solution.py:64
  205.3 14.0 %convolution_convert_fusion.4.dh_ref = bf16[1024,2048]{1,0:T(8,128)(2,1)} fusion(bf16[1024,2048]{1,0:T(8,128)(2,1)} %place_rows.1, bf16[2048,2048]{1,0:T(8,128)(2,1)} %all-gather.9.cloned.1.call-done), kind=kOutput, calls=%fused_computation.5 | convolution fusion | flops 8592031744 | bytes 16777216 | tf_op jit(solution)/shard_map/dot_general | solution.py:45
  224.6 14.8 %collective-permute-done.16.refs_7_.refs_2_ = bf16[1024,512]{1,0:T(8,128)(2,1)S(1)} collective-permute-done((bf16[1024,512]{1,0:T(8,128)(2,1)S(1)}, bf16[1024,512]{1,0:T(8,128)(2,1)S(1)}, u32[]{:S(2)}, u32[]{:S(2)}) %collective-permute-start.16) | collective-permute-done | bytes 1048608 | tf_op jit(solution)/shard_map/ppermute | solution.py:63
  243.7 13.9 %all-gather.11.cloned.1.call-done.refs_2_.refs_4_.refs_6_.refs_9_ = bf16[2048,2048]{1,0:T(8,128)(2,1)} async-done(((bf16[2048,256]{1,0:T(8,128)(2,1)}), bf16[2048,2048]{1,0:T(8,128)(2,1)}) %all-gather.11.cloned.1.call-update) | async-done | bytes 8388624 | tf_op jit(solution)/shard_map/all_gather | solution.py:1113
  262.3 14.7 %out_step.2.refs_0_ = f32[1024,2048]{1,0:T(8,128)} custom-call(s32[1]{0:T(128)} %bitcast.2.rank_ref, bf16[1024,2048]{1,0:T(8,128)(2,1)} %get-tuple-element.290.refs_0_, bf16[1024,512]{1,0:T(8,128)(2,1)S(1)} %get-tuple-element.275.refs_1_.refs_0_.o_ref, bf16[2048,2048]{1,0:T(8,128)(2,1)} %all-gather.11.cloned.1.call-done.refs_2_.refs_4_.refs_6_.refs_9_, ...), custom_call_target="tpu_custom_call" | custom-call | flops 8049999872 | bytes 21000000 | tf_op jit(solution)/shard_map/out_step/pallas_call | solution.py:667
  283.9 9.0 %out_step.3 = (f32[256,2048]{1,0:T(8,128)S(1)}, bf16[1024,2048]{1,0:T(8,128)(2,1)}) custom-call(s32[1]{0:T(128)} %bitcast.2.rank_ref, f32[1024,2048]{1,0:T(8,128)} %out_step.2.refs_0_, f32[1,2048]{1,0:T(1,128)S(1)} %get-tuple-element.436.refs_1_.gain_ref, bf16[1024,512]{1,0:T(8,128)(2,1)S(1)} %collective-permute-done.18.refs_2_.refs_3_, ...), custom_call_target="tpu_custom_call" | custom-call | flops 8049999872 | bytes 21000000 | tf_op jit(solution)/shard_map/out_step/pallas_call | solution.py:667
  294.3 24.7 %gate_and_back.1 = (bf16[1024,2048]{1,0:T(8,128)(2,1)S(1)}, bf16[1024,4096]{1,0:T(8,128)(2,1)}) custom-call(bf16[1024,2048]{1,0:T(8,128)(2,1)} %get-tuple-element.323.n_ref, bf16[2048,4096]{1,0:T(8,128)(2,1)} %all-gather.7.cloned.1.call-done.w_ref.refs_1_.refs_3_, bf16[1024,2048]{1,0:T(8,128)(2,1)} %convolution_convert_fusion.4.dh_ref), custom_call_target="tpu_custom_call" | custom-call | flops 31050000384 | bytes 81000000 | tf_op jit(solution)/shard_map/gate_and_back/pallas_call | solution.py:727
  320.9 11.2 %convolution_convert_fusion.2 = bf16[2048,2048]{1,0:T(8,128)(2,1)} fusion(bf16[1024,2048]{1,0:T(8,128)(2,1)S(1)} %get-tuple-element.326, bf16[1024,2048]{1,0:T(8,128)(2,1)S(1)} %copy-done.79), kind=kOutput, calls=%fused_computation.3 | convolution fusion | flops 8594128896 | bytes 16777216 | tf_op jit(solution)/shard_map/dot_general | solution.py:41
  336.0 10.5 %blocks_times.4 = bf16[256,2048]{1,0:T(8,128)(2,1)S(1)} custom-call(s32[1]{0:T(128)S(1)} %bitcast.40, bf16[1024,4096]{1,0:T(8,128)(2,1)} %get-tuple-element.322.refs_0_.refs_1_.refs_2_, bf16[2048,4096]{1,0:T(8,128)(2,1)} %all-gather.7.cloned.1.call-done.w_ref.refs_1_.refs_3_), custom_call_target="tpu_custom_call" | custom-call | flops 10350000128 | bytes 27000000 | tf_op jit(solution)/shard_map/blocks_times/pallas_call | solution.py:764
  348.8 19.5 %blocks_times.5 = (bf16[256,2048]{1,0:T(8,128)(2,1)S(1)}, bf16[256,2048]{1,0:T(8,128)(2,1)S(1)}, bf16[256,2048]{1,0:T(8,128)(2,1)S(1)}) custom-call(s32[3]{0:T(128)S(1)} %slice_bitcast_fusion.chunks_ref, bf16[1024,4096]{1,0:T(8,128)(2,1)} %get-tuple-element.322.refs_0_.refs_1_.refs_2_, bf16[1024,4096]{1,0:T(8,128)(2,1)} %get-tuple-element.322.refs_0_.refs_1_.refs_2_, ...), custom_call_target="tpu_custom_call" | custom-call | flops 25300000768 | bytes 66000000 | tf_op jit(solution)/shard_map/blocks_times/pallas_call | solution.py:764
  381.8 23.8 %convolution_convert_fusion = bf16[2048,4096]{1,0:T(8,128)(2,1)} fusion(bf16[1024,2048]{1,0:T(8,128)(2,1)S(1)} %copy-done.80, bf16[1024,4096]{1,0:T(8,128)(2,1)} %get-tuple-element.322.refs_0_.refs_1_.refs_2_), kind=kOutput, calls=%fused_computation | convolution fusion | flops 17188257792 | bytes 29360128 | tf_op jit(solution)/shard_map/dot_general | solution.py:41
  416.5 13.4 %convolution_convert_fusion.3 = bf16[1024,2048]{1,0:T(8,128)(2,1)} fusion(bf16[1024,2048]{1,0:T(8,128)(2,1)S(1)} %copy-done.52, bf16[2048,2048]{1,0:T(8,128)(2,1)} %all-gather.9.cloned.1.call-done), kind=kOutput, calls=%fused_computation.4 | convolution fusion | flops 8592031744 | bytes 16777216 | tf_op jit(solution)/shard_map/dot_general | solution.py:1163
  459.8 10.9 %all-to-all-done.1 = bf16[256,4,512]{2,0,1:T(8,128)(2,1)} async-done(((bf16[256,4,512]{2,0,1:T(8,128)(2,1)}), bf16[256,4,512]{2,0,1:T(8,128)(2,1)}, u32[]{:S(2)}, u32[]{:S(2)}) %all-to-all-start.1) | async-done | bytes 1048608 | tf_op jit(solution)/shard_map/all_to_all | solution.py:1173
  470.9 8.1 %all-to-all-start.2 = ((bf16[4,256,2048]{2,1,0:T(8,128)(2,1)}), bf16[4,256,2048]{2,1,0:T(8,128)(2,1)}, u32[]{:S(2)}, u32[]{:S(2)}) async-start(bf16[4,256,2048]{2,1,0:T(8,128)(2,1)} %bitcast.44), calls=%async_computation.4 | async-start | bytes 8388608 | tf_op jit(solution)/shard_map/all_to_all | solution.py:136
  480.6 21.5 %attend_back.2 = (bf16[1024,256]{1,0:T(8,128)(2,1)S(1)}, bf16[1024,128]{1,0:T(8,128)(2,1)S(1)}, bf16[1024,128]{1,0:T(8,128)(2,1)S(1)}, f32[1024,128]{1,0:T(8,128)S(1)}) custom-call(s32[1024]{0:T(1024)S(1)} %copy-done.17, bf16[1024,512]{1,0:T(8,128)(2,1)S(1)} %copy-done.56, bf16[1024,512]{1,0:T(8,128)(2,1)} %bitcast.9.do_ref, bf16[1024,512]{1,0:T(8,128)(2,1)} %copy-done.4, ...), custom_call_target="tpu_custom_call" | custom-call | flops 32199999488 | bytes 84000000 | tf_op jit(solution)/shard_map/attend_back/pallas_call | solution.py:541
  511.5 21.5 %attend_back.3 = (bf16[1024,256]{1,0:T(8,128)(2,1)S(1)}, bf16[1024,128]{1,0:T(8,128)(2,1)S(1)}, bf16[1024,128]{1,0:T(8,128)(2,1)S(1)}, f32[1024,128]{1,0:T(8,128)S(1)}) custom-call(s32[1024]{0:T(1024)S(1)} %copy-done.17, bf16[1024,512]{1,0:T(8,128)(2,1)S(1)} %copy-done.57, bf16[1024,512]{1,0:T(8,128)(2,1)} %bitcast.9.do_ref, bf16[1024,512]{1,0:T(8,128)(2,1)} %copy-done.4, ...), custom_call_target="tpu_custom_call" | custom-call | flops 32199999488 | bytes 84000000 | tf_op jit(solution)/shard_map/attend_back/pallas_call | solution.py:541
  628.8 13.6 %adam_interleaved.1 = (f32[2,256,2048]{2,1,0:T(8,128)}, f32[2,256,2048]{2,1,0:T(8,128)}, f32[2,256,2048]{2,1,0:T(8,128)}, f32[2,256,2048]{2,1,0:T(8,128)}, bf16[2,256,2048]{2,1,0:T(8,128)(2,1)}) custom-call(bf16[256,4096]{1,0:T(8,128)(2,1)S(1)} %copy-done.21, f32[2,256,2048]{2,1,0:T(8,128)} %w_ref.2, f32[2,256,2048]{2,1,0:T(8,128)} %m_ref.1, ...), custom_call_target="tpu_custom_call" | custom-call | flops 14949999616 | bytes 39000000 | tf_op jit(solution)/shard_map/adam_interleaved/pallas_call | solution.py:1012
  649.6 16.4 %collective-permute-done.41 = f32[2,2048]{1,0:T(2,128)S(1)} collective-permute-done((f32[2,2048]{1,0:T(2,128)S(1)}, f32[2,2048]{1,0:T(2,128)S(1)}, u32[]{:S(2)}, u32[]{:S(2)}) %collective-permute-start.41) | collective-permute-done | bytes 16416 | tf_op jit(solution)/shard_map/ppermute | solution.py:157
  (323 shorter events, 305.6 us)
Async XLA Ops:
  7.2 91.8 %all-gather.5.cloned.1.call-start = ((), (), s32[]{:S(2)}) async-start(), calls=%async_computation.8 | async-start | bytes 3538944 | tf_op jit(solution)/shard_map/all_gather | solution.py:1076
  9.2 151.7 %all-gather.7.cloned.1.call-start = ((), (), s32[]{:S(2)}) async-start(), calls=%async_computation.9 | async-start | bytes 18874368 | tf_op jit(solution)/shard_map/all_gather | solution.py:1083
  9.3 27.1 %collective-permute-start.1 = (bf16[256,2048]{1,0:T(8,128)(2,1)}, bf16[256,2048]{1,0:T(8,128)(2,1)S(1)}, u32[]{:S(2)}, u32[]{:S(2)}) collective-permute-start(bf16[256,2048]{1,0:T(8,128)(2,1)} %x_ref.1), channel_id=1, source_target_pairs={{1,0},{2,1},{3,2},{5,4},{6,5},{7,6},{9,8},{10,9},{11,10},{13,12},{... | collective-permute-start | bytes 3145736 | tf_op jit(solution)/shard_map/ppermute | solution.py:64
  45.0 160.3 %all-gather.9.cloned.1.call-start = ((), (), s32[]{:S(2)}) async-start(), calls=%async_computation.10 | async-start | bytes 9437184 | tf_op jit(solution)/shard_map/all_gather | solution.py:1098
  127.3 32.0 %collective-permute-start.9 = (bf16[1024,256]{1,0:T(8,128)(2,1)S(1)}, bf16[1024,256]{1,0:T(8,128)(2,1)S(1)}, u32[]{:S(2)}, u32[]{:S(2)}) collective-permute-start(bf16[1024,256]{1,0:T(8,128)(2,1)S(1)} %get-tuple-element.255.here), channel_id=1, source_target_pairs={{0,4},{4,8},{8,12},{16,20},{20,24},{24,28},{1,5},{5,9},{9,13},{17,... | collective-permute-start | bytes 1572872 | tf_op jit(solution)/shard_map/ppermute | solution.py:173
  129.3 30.8 %collective-permute-start.8 = (bf16[1024,256]{1,0:T(8,128)(2,1)S(1)}, bf16[1024,256]{1,0:T(8,128)(2,1)S(1)}, u32[]{:S(2)}, u32[]{:S(2)}) collective-permute-start(bf16[1024,256]{1,0:T(8,128)(2,1)S(1)} %get-tuple-element.255.here), channel_id=1, source_target_pairs={{0,8},{4,12},{16,24},{20,28},{1,9},{5,13},{17,25},{21,29},{2,10},{... | collective-permute-start | bytes 1572872 | tf_op jit(solution)/shard_map/ppermute | solution.py:173
  130.6 30.3 %collective-permute-start.10 = (bf16[256,2048]{1,0:T(8,128)(2,1)}, bf16[256,2048]{1,0:T(8,128)(2,1)S(1)}, u32[]{:S(2)}, u32[]{:S(2)}) collective-permute-start(bf16[256,2048]{1,0:T(8,128)(2,1)} %collective-permute-done.6.refs_1_), channel_id=1, source_target_pairs={{1,2},{2,3},{5,6},{6,7},{9,10},{10,11},{13,14},{14,15},{17,18},{18... | collective-permute-start | bytes 3145736 | tf_op jit(solution)/shard_map/ppermute | solution.py:63
  132.8 28.1 %collective-permute-start.11 = (bf16[256,2048]{1,0:T(8,128)(2,1)}, bf16[256,2048]{1,0:T(8,128)(2,1)}, u32[]{:S(2)}, u32[]{:S(2)}) collective-permute-start(bf16[256,2048]{1,0:T(8,128)(2,1)} %collective-permute-done.7.refs_4_), channel_id=1, source_target_pairs={{1,0},{2,1},{5,4},{6,5},{9,8},{10,9},{13,12},{14,13},{17,16},{18,1... | collective-permute-start | bytes 3145736 | tf_op jit(solution)/shard_map/ppermute | solution.py:64
  153.6 29.8 %all-to-all-start = ((bf16[4,512,256]{2,1,0:T(8,128)(2,1)}), bf16[4,512,256]{2,1,0:T(8,128)(2,1)}, u32[]{:S(2)}, u32[]{:S(2)}) async-start(bf16[4,512,256]{2,1,0:T(8,128)(2,1)} %broadcast_in_dim.5), calls=%async_computation | async-start | bytes 2097152 | tf_op jit(solution)/shard_map/all_to_all | solution.py:130
  159.3 98.3 %all-gather.11.cloned.1.call-start = ((), (), s32[]{:S(2)}) async-start(), calls=%async_computation.11 | async-start | bytes 9437184 | tf_op jit(solution)/shard_map/all_gather | solution.py:1113
  162.6 29.8 %collective-permute-start.13 = (bf16[256,2048]{1,0:T(8,128)(2,1)}, bf16[256,2048]{1,0:T(8,128)(2,1)}, u32[]{:S(2)}, u32[]{:S(2)}) collective-permute-start(bf16[256,2048]{1,0:T(8,128)(2,1)} %collective-permute-done.11.refs_5_), channel_id=1, source_target_pairs={{1,0},{5,4},{9,8},{13,12},{17,16},{21,20},{25,24},{29,28}} | collective-permute-start | bytes 3145736 | tf_op jit(solution)/shard_map/ppermute | solution.py:64
  192.4 278.3 %reduce-scatter.5.cloned.1.call-start = ((), (), s32[]{:S(2)}) async-start(), calls=%async_computation.12 | async-start | bytes 9437184 | tf_op jit(solution)/shard_map/reduce_scatter | solution.py:1146
  332.1 221.7 %reduce-scatter.7.cloned.1.call-start = ((), (), s32[]{:S(2)}) async-start(), calls=%async_computation.13 | async-start | bytes 18874368 | tf_op jit(solution)/shard_map/reduce_scatter | solution.py:1161
  376.0 29.7 %collective-permute-start.23 = (bf16[256,2048]{1,0:T(8,128)(2,1)}, bf16[256,2048]{1,0:T(8,128)(2,1)}, u32[]{:S(2)}, u32[]{:S(2)}) collective-permute-start(bf16[256,2048]{1,0:T(8,128)(2,1)} %get-tuple-element.430), channel_id=1, source_target_pairs={{2,1},{3,2},{6,5},{7,6},{10,9},{11,10},{14,13},{15,14},{18,17},{19... | collective-permute-start | bytes 3145736 | tf_op jit(solution)/shard_map/ppermute | solution.py:120
  377.3 28.4 %collective-permute-start.22 = (bf16[256,2048]{1,0:T(8,128)(2,1)}, bf16[256,2048]{1,0:T(8,128)(2,1)}, u32[]{:S(2)}, u32[]{:S(2)}) collective-permute-start(bf16[256,2048]{1,0:T(8,128)(2,1)} %get-tuple-element.431), channel_id=1, source_target_pairs={{0,1},{1,2},{4,5},{5,6},{8,9},{9,10},{12,13},{13,14},{16,17},{17,1... | collective-permute-start | bytes 3145736 | tf_op jit(solution)/shard_map/ppermute | solution.py:119
  450.1 158.6 %reduce-scatter.9.cloned.1.call-start = ((), (), s32[]{:S(2)}) async-start(), calls=%async_computation.14 | async-start | bytes 9437184 | tf_op jit(solution)/shard_map/reduce_scatter | solution.py:1177
  470.9 107.3 %all-to-all-start.2 = ((bf16[4,256,2048]{2,1,0:T(8,128)(2,1)}), bf16[4,256,2048]{2,1,0:T(8,128)(2,1)}, u32[]{:S(2)}, u32[]{:S(2)}) async-start(bf16[4,256,2048]{2,1,0:T(8,128)(2,1)} %bitcast.44), calls=%async_computation.4 | async-start | bytes 8388608 | tf_op jit(solution)/shard_map/all_to_all | solution.py:136
  479.0 196.9 %reduce-scatter.11.cloned.1.call-start = ((), (), s32[]{:S(2)}) async-start(), calls=%async_computation.15 | async-start | bytes 3538944 | tf_op jit(solution)/shard_map/reduce_scatter | solution.py:1212
  502.1 30.9 %collective-permute-start.27 = (bf16[1024,128]{1,0:T(8,128)(2,1)S(1)}, bf16[1024,128]{1,0:T(8,128)(2,1)S(1)}, u32[]{:S(2)}, u32[]{:S(2)}) collective-permute-start(bf16[1024,128]{1,0:T(8,128)(2,1)S(1)} %get-tuple-element.345), channel_id=1, source_target_pairs={{8,0},{12,4},{24,16},{28,20},{9,1},{13,5},{25,17},{29,21},{10,2},{... | collective-permute-start | bytes 786440 | tf_op jit(solution)/shard_map/ppermute | solution.py:173
  503.7 29.4 %collective-permute-start.26 = (bf16[1024,128]{1,0:T(8,128)(2,1)S(1)}, bf16[1024,128]{1,0:T(8,128)(2,1)S(1)}, u32[]{:S(2)}, u32[]{:S(2)}) collective-permute-start(bf16[1024,128]{1,0:T(8,128)(2,1)S(1)} %get-tuple-element.346), channel_id=1, source_target_pairs={{4,0},{8,4},{12,8},{20,16},{24,20},{28,24},{5,1},{9,5},{13,9},{21,... | collective-permute-start | bytes 786440 | tf_op jit(solution)/shard_map/ppermute | solution.py:173
  555.4 27.3 %collective-permute-start.30 = (bf16[256,2048]{1,0:T(8,128)(2,1)}, bf16[256,2048]{1,0:T(8,128)(2,1)}, u32[]{:S(2)}, u32[]{:S(2)}) collective-permute-start(bf16[256,2048]{1,0:T(8,128)(2,1)} %blocks_times.6), channel_id=1, source_target_pairs={{0,1},{4,5},{8,9},{12,13},{16,17},{20,21},{24,25},{28,29}} | collective-permute-start | bytes 3145736 | tf_op jit(solution)/shard_map/ppermute | solution.py:119
  614.1 52.1 %all-to-all-start.3 = ((bf16[4,512,256]{2,1,0:T(8,128)(2,1)}), bf16[4,512,256]{2,1,0:T(8,128)(2,1)}, u32[]{:S(2)}, u32[]{:S(2)}) async-start(bf16[4,512,256]{2,1,0:T(8,128)(2,1)} %bitcast.46), calls=%async_computation.6 | async-start | bytes 2097152 | tf_op jit(solution)/shard_map/all_to_all | solution.py:136
  622.9 43.2 %collective-permute-start.38 = (bf16[256,2048]{1,0:T(8,128)(2,1)}, bf16[256,2048]{1,0:T(8,128)(2,1)}, u32[]{:S(2)}, u32[]{:S(2)}) collective-permute-start(bf16[256,2048]{1,0:T(8,128)(2,1)} %get-tuple-element.432), channel_id=1, source_target_pairs={{1,0},{2,1},{3,2},{5,4},{6,5},{7,6},{9,8},{10,9},{11,10},{13,12},{... | collective-permute-start | bytes 3145736 | tf_op jit(solution)/shard_map/ppermute | solution.py:120
  624.9 41.2 %collective-permute-start.37 = (bf16[256,2048]{1,0:T(8,128)(2,1)}, bf16[256,2048]{1,0:T(8,128)(2,1)}, u32[]{:S(2)}, u32[]{:S(2)}) collective-permute-start(bf16[256,2048]{1,0:T(8,128)(2,1)} %get-tuple-element.433), channel_id=1, source_target_pairs={{0,1},{1,2},{2,3},{4,5},{5,6},{6,7},{8,9},{9,10},{10,11},{12,13},{... | collective-permute-start | bytes 3145736 | tf_op jit(solution)/shard_map/ppermute | solution.py:119
  (113 other events, 1874.5 us)
Sparse Core Ops, SparseCore 0:
  10.5 33.4 all-gather.4
  46.4 89.8 all-gather.6
  138.8 58.3 all-gather.8
  198.9 58.6 all-gather.10
  332.3 72.6 reduce-scatter.4
  408.8 121.1 reduce-scatter.6
  533.9 74.7 reduce-scatter.8
  612.1 46.1 reduce-scatter.10

commit v5 on v4

--- a/solution.py
+++ b/solution.py
@@ -1124,7 +1124,7 @@
                 (heads_line.moving, grad_rows, d_hidden, total)
             )
         elif index < heads_line.hops - 1:
-            heads_line.moving, w_out = close((heads_line.moving, w_out))
+            heads_line.moving = close(heads_line.moving)
         else:
             total = out_step(total, arrived, rank, w_out, own)
             heads_line.moving, total = close((heads_line.moving, total))

time: 697 us -> 697 us (level)
  the two profiles are of different devices: /device:TPU:10 before, /device:TPU:6 now
where the time goes in v5:
time: 697 us; the launch traced here: 691 us
  Pallas kernels  214 us (31%)
  waiting for transfers between devices  194 us (28%)
  starting transfers between devices  115 us (16%)
  matrix products  80.6 us (12%)
  other arithmetic  39.4 us (6%)
  local copies, waits for them, and re-layouts  29.6 us (4%)
  between operations  18 us (3%)
    ppermute x9, waiting for transfers between devices, hop(): self.from_high.append(lax.ppermute(self.from_high[-1], self.axis, down))  122 us
    dot_general x4, matrix products, contract_rows(): lax.dot_general(left, right, ROWS_BY_ROWS, preferred_element_type=jnp.flo...  47.3 us
    pallas_call x2, Pallas kernels, attend_back(): pl.pallas_call(functools.partial(attend_back_kernel, tk), grid_spec=pltpu...  43.1 us
    pallas_call x4, Pallas kernels, blocks_times(): pl.pallas_call(blocks_kernel, grid_spec=pltpu.PrefetchScalarGridSpec(num_...  38.4 us
    ppermute x6, starting transfers between devices, hop(): lax.ppermute(to_high, self.axis, [(i, i + 1) for i in range(step)])  25.7 us
    unnamed x154, local copies, waits for them, and re-layouts  24.9 us
    pallas_call x1, Pallas kernels, gate_and_back(): pl.pallas_call(gate_kernel, grid=(units // wide, tokens // tile), in_spec...  24.7 us
    pallas_call x2, Pallas kernels, out_step(): pl.pallas_call(functools.partial(out_step_kernel, distances, last), grid_...  24.2 us
  transfers between devices with their start and end apart: 54, of which 21 were waited for; matrix products, arithmetic and copies ran while one was open for 16% of the time, Pallas kernels for 26%

profile of v5, /device:TPU:6, one launch (start us, length us, event | category | flops | bytes accessed | tf_op | source)
XLA Modules:
  0.0 690.8 jit_solution(7437452668873210386)
XLA Ops:
  15.3 21.1 %collective-permute-done.1.refs_4_ = bf16[256,2048]{1,0:T(8,128)(2,1)S(1)} collective-permute-done((bf16[256,2048]{1,0:T(8,128)(2,1)}, bf16[256,2048]{1,0:T(8,128)(2,1)S(1)}, u32[]{:S(2)}, u32[]{:S(2)}) %collective-permute-start.1) | collective-permute-done | bytes 1048608 | tf_op jit(solution)/shard_map/ppermute | solution.py:64
  53.6 21.7 %collective-permute-done.3.refs_5_ = bf16[256,2048]{1,0:T(8,128)(2,1)} collective-permute-done((bf16[256,2048]{1,0:T(8,128)(2,1)}, bf16[256,2048]{1,0:T(8,128)(2,1)}, u32[]{:S(2)}, u32[]{:S(2)}) %collective-permute-start.3) | collective-permute-done | bytes 1048608 | tf_op jit(solution)/shard_map/ppermute | solution.py:64
  77.3 23.8 %collective-permute-done.5.refs_6_ = bf16[256,2048]{1,0:T(8,128)(2,1)} collective-permute-done((bf16[256,2048]{1,0:T(8,128)(2,1)}, bf16[256,2048]{1,0:T(8,128)(2,1)}, u32[]{:S(2)}, u32[]{:S(2)}) %collective-permute-start.5) | collective-permute-done | bytes 1048608 | tf_op jit(solution)/shard_map/ppermute | solution.py:64
  110.5 11.1 %project_qkv.1 = (bf16[1024,2048]{1,0:T(8,128)(2,1)}, bf16[1024,2048]{1,0:T(8,128)(2,1)}, bf16[1024,512]{1,0:T(8,128)(2,1)S(1)}, bf16[1024,256]{1,0:T(8,128)(2,1)S(1)}) custom-call(s32[1]{0:T(128)} %bitcast.2.rank_ref, bf16[2048,768]{1,0:T(8,128)(2,1)} %all-gather.5.cloned.1.call-done.w_ref.refs_1_.refs_3_, f32[1,2048]{1,0:T(1,128)S(1)} %get-tuple-element.435.gain_ref, ...), custom_call_target="tpu_custom_call" | custom-call | flops 10350000128 | bytes 27000000 | tf_op jit(solution)/shard_map/project_qkv/pallas_call | solution.py:255
  132.9 14.5 %attend_here.1 = (f32[2,4,128,1024]{3,2,1,0:T(8,128)S(1)}, f32[2,4,8,1024]{3,2,1,0:T(8,128)S(1)}) custom-call(s32[1024]{0:T(1024)S(1)} %copy-done.13, bf16[1024,512]{1,0:T(8,128)(2,1)S(1)} %copy-done.49, s32[8,1024]{1,0:T(8,128)S(1)} %broadcast_in_dim.4.back_ref, bf16[1024,256]{1,0:T(8,128)(2,1)S(1)} %get-tuple-element.254.here), custom_call_target="tpu_custom_call" | custom-call | flops 17250000896 | bytes 45000000 | tf_op jit(solution)/shard_map/attend_here/pallas_call | solution.py:417
  166.8 13.7 %attend_far.1 = (bf16[1024,512]{1,0:T(8,128)(2,1)S(1)}, f32[2,4,8,1024]{3,2,1,0:T(8,128)S(1)}) custom-call(s32[1024]{0:T(1024)S(1)} %copy-done.13, bf16[1024,512]{1,0:T(8,128)(2,1)S(1)} %copy-done.50, s32[8,1024]{1,0:T(8,128)S(1)} %broadcast_in_dim.4.back_ref, bf16[1024,256]{1,0:T(8,128)(2,1)S(1)} %copy-done.34, bf16[1024,256]{1,0:T(8,128)(2,1)S(1)} %copy-done.31, ...), custom_call_target="tpu_custom_call" | custom-call | flops 24149999616 | bytes 63000000 | tf_op jit(solution)/shard_map/attend_far/pallas_call | solution.py:446
  181.3 14.5 %collective-permute-done.13.refs_6_ = bf16[256,2048]{1,0:T(8,128)(2,1)} collective-permute-done((bf16[256,2048]{1,0:T(8,128)(2,1)}, bf16[256,2048]{1,0:T(8,128)(2,1)}, u32[]{:S(2)}, u32[]{:S(2)}) %collective-permute-start.13) | collective-permute-done | bytes 1048608 | tf_op jit(solution)/shard_map/ppermute | solution.py:64
  209.3 14.3 %convolution_convert_fusion.4.dh_ref = bf16[1024,2048]{1,0:T(8,128)(2,1)} fusion(bf16[1024,2048]{1,0:T(8,128)(2,1)} %place_rows.1, bf16[2048,2048]{1,0:T(8,128)(2,1)} %all-gather.9.cloned.1.call-done), kind=kOutput, calls=%fused_computation.5 | convolution fusion | flops 8592031744 | bytes 16777216 | tf_op jit(solution)/shard_map/dot_general | solution.py:45
  226.6 28.5 %collective-permute-done.17.refs_8_.refs_5_ = bf16[1024,512]{1,0:T(8,128)(2,1)} collective-permute-done((bf16[1024,512]{1,0:T(8,128)(2,1)S(1)}, bf16[1024,512]{1,0:T(8,128)(2,1)}, u32[]{:S(2)}, u32[]{:S(2)}) %collective-permute-start.17) | collective-permute-done | bytes 1048608 | tf_op jit(solution)/shard_map/ppermute | solution.py:64
  258.1 15.1 %out_step.2.refs_0_ = f32[1024,2048]{1,0:T(8,128)} custom-call(s32[1]{0:T(128)} %bitcast.2.rank_ref, bf16[1024,2048]{1,0:T(8,128)(2,1)} %get-tuple-element.288.refs_0_, bf16[1024,512]{1,0:T(8,128)(2,1)S(1)} %get-tuple-element.274.refs_1_.refs_0_.o_ref, bf16[2048,2048]{1,0:T(8,128)(2,1)} %all-gather.11.cloned.1.call-done.refs_2_.refs_4_.refs_6_.refs_9_, ...), custom_call_target="tpu_custom_call" | custom-call | flops 8049999872 | bytes 21000000 | tf_op jit(solution)/shard_map/out_step/pallas_call | solution.py:667
  273.2 9.7 %collective-permute-done.19.refs_3_.refs_6_ = bf16[1024,512]{1,0:T(8,128)(2,1)} collective-permute-done((bf16[1024,512]{1,0:T(8,128)(2,1)}, bf16[1024,512]{1,0:T(8,128)(2,1)}, u32[]{:S(2)}, u32[]{:S(2)}) %collective-permute-start.19) | collective-permute-done | bytes 1048608 | tf_op jit(solution)/shard_map/ppermute | solution.py:64
  282.9 9.1 %out_step.3 = (f32[256,2048]{1,0:T(8,128)S(1)}, bf16[1024,2048]{1,0:T(8,128)(2,1)}) custom-call(s32[1]{0:T(128)} %bitcast.2.rank_ref, f32[1024,2048]{1,0:T(8,128)} %out_step.2.refs_0_, f32[1,2048]{1,0:T(1,128)S(1)} %get-tuple-element.434.refs_1_.gain_ref, bf16[1024,512]{1,0:T(8,128)(2,1)} %collective-permute-done.18.refs_2_.refs_3_, ...), custom_call_target="tpu_custom_call" | custom-call | flops 8049999872 | bytes 21000000 | tf_op jit(solution)/shard_map/out_step/pallas_call | solution.py:667
  293.3 24.7 %gate_and_back.1 = (bf16[1024,2048]{1,0:T(8,128)(2,1)S(1)}, bf16[1024,4096]{1,0:T(8,128)(2,1)}) custom-call(bf16[1024,2048]{1,0:T(8,128)(2,1)} %get-tuple-element.321.n_ref, bf16[2048,4096]{1,0:T(8,128)(2,1)} %all-gather.7.cloned.1.call-done.w_ref.refs_1_.refs_3_, bf16[1024,2048]{1,0:T(8,128)(2,1)} %convolution_convert_fusion.4.dh_ref), custom_call_target="tpu_custom_call" | custom-call | flops 31050000384 | bytes 81000000 | tf_op jit(solution)/shard_map/gate_and_back/pallas_call | solution.py:727
  320.0 11.2 %convolution_convert_fusion.2 = bf16[2048,2048]{1,0:T(8,128)(2,1)} fusion(bf16[1024,2048]{1,0:T(8,128)(2,1)S(1)} %get-tuple-element.324, bf16[1024,2048]{1,0:T(8,128)(2,1)S(1)} %copy-done.75), kind=kOutput, calls=%fused_computation.3 | convolution fusion | flops 8594128896 | bytes 16777216 | tf_op jit(solution)/shard_map/dot_general | solution.py:41
  335.1 11.2 %blocks_times.4 = bf16[256,2048]{1,0:T(8,128)(2,1)S(1)} custom-call(s32[1]{0:T(128)S(1)} %bitcast.40, bf16[1024,4096]{1,0:T(8,128)(2,1)} %get-tuple-element.320.refs_0_.refs_1_.refs_2_, bf16[2048,4096]{1,0:T(8,128)(2,1)} %all-gather.7.cloned.1.call-done.w_ref.refs_1_.refs_3_), custom_call_target="tpu_custom_call" | custom-call | flops 10350000128 | bytes 27000000 | tf_op jit(solution)/shard_map/blocks_times/pallas_call | solution.py:764
  349.0 19.1 %blocks_times.5 = (bf16[256,2048]{1,0:T(8,128)(2,1)S(1)}, bf16[256,2048]{1,0:T(8,128)(2,1)S(1)}, bf16[256,2048]{1,0:T(8,128)(2,1)S(1)}) custom-call(s32[3]{0:T(128)S(1)} %slice_bitcast_fusion.chunks_ref, bf16[1024,4096]{1,0:T(8,128)(2,1)} %get-tuple-element.320.refs_0_.refs_1_.refs_2_, bf16[1024,4096]{1,0:T(8,128)(2,1)} %get-tuple-element.320.refs_0_.refs_1_.refs_2_, ...), custom_call_target="tpu_custom_call" | custom-call | flops 25300000768 | bytes 66000000 | tf_op jit(solution)/shard_map/blocks_times/pallas_call | solution.py:764
  377.3 23.8 %convolution_convert_fusion = bf16[2048,4096]{1,0:T(8,128)(2,1)} fusion(bf16[1024,2048]{1,0:T(8,128)(2,1)S(1)} %copy-done.76, bf16[1024,4096]{1,0:T(8,128)(2,1)} %get-tuple-element.320.refs_0_.refs_1_.refs_2_), kind=kOutput, calls=%fused_computation | convolution fusion | flops 17188257792 | bytes 29360128 | tf_op jit(solution)/shard_map/dot_general | solution.py:41
  411.5 13.3 %convolution_convert_fusion.3 = bf16[1024,2048]{1,0:T(8,128)(2,1)} fusion(bf16[1024,2048]{1,0:T(8,128)(2,1)S(1)} %copy-done.47, bf16[2048,2048]{1,0:T(8,128)(2,1)} %all-gather.9.cloned.1.call-done), kind=kOutput, calls=%fused_computation.4 | convolution fusion | flops 8592031744 | bytes 16777216 | tf_op jit(solution)/shard_map/dot_general | solution.py:1163
  454.1 15.1 %all-to-all-done.1 = bf16[256,4,512]{2,0,1:T(8,128)(2,1)} async-done(((bf16[256,4,512]{2,0,1:T(8,128)(2,1)}), bf16[256,4,512]{2,0,1:T(8,128)(2,1)}, u32[]{:S(2)}, u32[]{:S(2)}) %all-to-all-start.1) | async-done | bytes 1048608 | tf_op jit(solution)/shard_map/all_to_all | solution.py:1173
  476.0 21.6 %attend_back.2 = (bf16[1024,256]{1,0:T(8,128)(2,1)S(1)}, bf16[1024,128]{1,0:T(8,128)(2,1)S(1)}, bf16[1024,128]{1,0:T(8,128)(2,1)S(1)}, f32[1024,128]{1,0:T(8,128)S(1)}) custom-call(s32[1024]{0:T(1024)S(1)} %copy-done.14, bf16[1024,512]{1,0:T(8,128)(2,1)S(1)} %copy-done.51, bf16[1024,512]{1,0:T(8,128)(2,1)} %bitcast.9.do_ref, bf16[1024,512]{1,0:T(8,128)(2,1)} %copy-done.4, ...), custom_call_target="tpu_custom_call" | custom-call | flops 32199999488 | bytes 84000000 | tf_op jit(solution)/shard_map/attend_back/pallas_call | solution.py:541
  501.3 21.5 %attend_back.3 = (bf16[1024,256]{1,0:T(8,128)(2,1)S(1)}, bf16[1024,128]{1,0:T(8,128)(2,1)S(1)}, bf16[1024,128]{1,0:T(8,128)(2,1)S(1)}, f32[1024,128]{1,0:T(8,128)S(1)}) custom-call(s32[1024]{0:T(1024)S(1)} %copy-done.14, bf16[1024,512]{1,0:T(8,128)(2,1)S(1)} %copy-done.52, bf16[1024,512]{1,0:T(8,128)(2,1)} %bitcast.9.do_ref, bf16[1024,512]{1,0:T(8,128)(2,1)} %copy-done.4, ...), custom_call_target="tpu_custom_call" | custom-call | flops 32199999488 | bytes 84000000 | tf_op jit(solution)/shard_map/attend_back/pallas_call | solution.py:541
  534.1 15.8 %collective-permute-done.28.refs_6_ = bf16[1024,128]{1,0:T(8,128)(2,1)S(1)} collective-permute-done((bf16[1024,128]{1,0:T(8,128)(2,1)S(1)}, bf16[1024,128]{1,0:T(8,128)(2,1)S(1)}, u32[]{:S(2)}, u32[]{:S(2)}) %collective-permute-start.28) | collective-permute-done | bytes 262176 | tf_op jit(solution)/shard_map/ppermute | solution.py:173
  630.1 13.6 %adam_interleaved.1 = (f32[2,256,2048]{2,1,0:T(8,128)}, f32[2,256,2048]{2,1,0:T(8,128)}, f32[2,256,2048]{2,1,0:T(8,128)}, f32[2,256,2048]{2,1,0:T(8,128)}, bf16[2,256,2048]{2,1,0:T(8,128)(2,1)}) custom-call(bf16[256,4096]{1,0:T(8,128)(2,1)S(1)} %copy-done.18, f32[2,256,2048]{2,1,0:T(8,128)} %w_ref.2, f32[2,256,2048]{2,1,0:T(8,128)} %m_ref.1, ...), custom_call_target="tpu_custom_call" | custom-call | flops 14949999616 | bytes 39000000 | tf_op jit(solution)/shard_map/adam_interleaved/pallas_call | solution.py:1012
  651.6 11.5 %collective-permute-done.41 = f32[2,2048]{1,0:T(2,128)S(1)} collective-permute-done((f32[2,2048]{1,0:T(2,128)S(1)}, f32[2,2048]{1,0:T(2,128)S(1)}, u32[]{:S(2)}, u32[]{:S(2)}) %collective-permute-start.41) | collective-permute-done | bytes 16416 | tf_op jit(solution)/shard_map/ppermute | solution.py:157
  (310 shorter events, 273.5 us)
Async XLA Ops:
  7.2 94.0 %all-gather.5.cloned.1.call-start = ((), (), s32[]{:S(2)}) async-start(), calls=%async_computation.8 | async-start | bytes 3538944 | tf_op jit(solution)/shard_map/all_gather | solution.py:1076
  9.2 151.3 %all-gather.7.cloned.1.call-start = ((), (), s32[]{:S(2)}) async-start(), calls=%async_computation.9 | async-start | bytes 18874368 | tf_op jit(solution)/shard_map/all_gather | solution.py:1083
  44.2 165.1 %all-gather.9.cloned.1.call-start = ((), (), s32[]{:S(2)}) async-start(), calls=%async_computation.10 | async-start | bytes 9437184 | tf_op jit(solution)/shard_map/all_gather | solution.py:1098
  46.1 29.2 %collective-permute-start.3 = (bf16[256,2048]{1,0:T(8,128)(2,1)}, bf16[256,2048]{1,0:T(8,128)(2,1)}, u32[]{:S(2)}, u32[]{:S(2)}) collective-permute-start(bf16[256,2048]{1,0:T(8,128)(2,1)} %copy-done.70), channel_id=1, source_target_pairs={{1,0},{2,1},{5,4},{6,5},{9,8},{10,9},{13,12},{14,13},{17,16},{18,1... | collective-permute-start | bytes 3145736 | tf_op jit(solution)/shard_map/ppermute | solution.py:64
  126.2 32.7 %collective-permute-start.9 = (bf16[1024,256]{1,0:T(8,128)(2,1)S(1)}, bf16[1024,256]{1,0:T(8,128)(2,1)S(1)}, u32[]{:S(2)}, u32[]{:S(2)}) collective-permute-start(bf16[1024,256]{1,0:T(8,128)(2,1)S(1)} %get-tuple-element.254.here), channel_id=1, source_target_pairs={{0,4},{4,8},{8,12},{16,20},{20,24},{24,28},{1,5},{5,9},{9,13},{17,... | collective-permute-start | bytes 1572872 | tf_op jit(solution)/shard_map/ppermute | solution.py:173
  128.3 31.4 %collective-permute-start.8 = (bf16[1024,256]{1,0:T(8,128)(2,1)S(1)}, bf16[1024,256]{1,0:T(8,128)(2,1)S(1)}, u32[]{:S(2)}, u32[]{:S(2)}) collective-permute-start(bf16[1024,256]{1,0:T(8,128)(2,1)S(1)} %get-tuple-element.254.here), channel_id=1, source_target_pairs={{0,8},{4,12},{16,24},{20,28},{1,9},{5,13},{17,25},{21,29},{2,10},{... | collective-permute-start | bytes 1572872 | tf_op jit(solution)/shard_map/ppermute | solution.py:173
  129.6 30.9 %collective-permute-start.10 = (bf16[256,2048]{1,0:T(8,128)(2,1)}, bf16[256,2048]{1,0:T(8,128)(2,1)S(1)}, u32[]{:S(2)}, u32[]{:S(2)}) collective-permute-start(bf16[256,2048]{1,0:T(8,128)(2,1)} %collective-permute-done.6.refs_1_), channel_id=1, source_target_pairs={{1,2},{2,3},{5,6},{6,7},{9,10},{10,11},{13,14},{14,15},{17,18},{18... | collective-permute-start | bytes 3145736 | tf_op jit(solution)/shard_map/ppermute | solution.py:63
  130.3 30.2 %collective-permute-start.11 = (bf16[256,2048]{1,0:T(8,128)(2,1)}, bf16[256,2048]{1,0:T(8,128)(2,1)}, u32[]{:S(2)}, u32[]{:S(2)}) collective-permute-start(bf16[256,2048]{1,0:T(8,128)(2,1)} %collective-permute-done.7.refs_4_), channel_id=1, source_target_pairs={{1,0},{2,1},{5,4},{6,5},{9,8},{10,9},{13,12},{14,13},{17,16},{18,1... | collective-permute-start | bytes 3145736 | tf_op jit(solution)/shard_map/ppermute | solution.py:64
  150.5 30.8 %all-to-all-start = ((bf16[4,512,256]{2,1,0:T(8,128)(2,1)}), bf16[4,512,256]{2,1,0:T(8,128)(2,1)}, u32[]{:S(2)}, u32[]{:S(2)}) async-start(bf16[4,512,256]{2,1,0:T(8,128)(2,1)} %broadcast_in_dim.5), calls=%async_computation | async-start | bytes 2097152 | tf_op jit(solution)/shard_map/all_to_all | solution.py:130
  158.9 99.2 %all-gather.11.cloned.1.call-start = ((), (), s32[]{:S(2)}) async-start(), calls=%async_computation.11 | async-start | bytes 9437184 | tf_op jit(solution)/shard_map/all_gather | solution.py:1113
  162.2 33.5 %collective-permute-start.13 = (bf16[256,2048]{1,0:T(8,128)(2,1)}, bf16[256,2048]{1,0:T(8,128)(2,1)}, u32[]{:S(2)}, u32[]{:S(2)}) collective-permute-start(bf16[256,2048]{1,0:T(8,128)(2,1)} %collective-permute-done.11.refs_5_), channel_id=1, source_target_pairs={{1,0},{5,4},{9,8},{13,12},{17,16},{21,20},{25,24},{29,28}} | collective-permute-start | bytes 3145736 | tf_op jit(solution)/shard_map/ppermute | solution.py:64
  195.8 273.4 %reduce-scatter.5.cloned.1.call-start = ((), (), s32[]{:S(2)}) async-start(), calls=%async_computation.12 | async-start | bytes 9437184 | tf_op jit(solution)/shard_map/reduce_scatter | solution.py:1146
  195.8 27.8 %collective-permute-start.15 = (bf16[1024,512]{1,0:T(8,128)(2,1)S(1)}, bf16[1024,512]{1,0:T(8,128)(2,1)S(1)}, u32[]{:S(2)}, u32[]{:S(2)}) collective-permute-start(bf16[1024,512]{1,0:T(8,128)(2,1)S(1)} %get-tuple-element.274.refs_1_.refs_0_.o_ref), channel_id=1, source_target_pairs={{1,0},{2,1},{3,2},{5,4},{6,5},{7,6},{9,8},{10,9},{11,10},{13,12},{... | collective-permute-start | bytes 3145736 | tf_op jit(solution)/shard_map/ppermute | solution.py:64
  225.3 29.8 %collective-permute-start.17 = (bf16[1024,512]{1,0:T(8,128)(2,1)S(1)}, bf16[1024,512]{1,0:T(8,128)(2,1)}, u32[]{:S(2)}, u32[]{:S(2)}) collective-permute-start(bf16[1024,512]{1,0:T(8,128)(2,1)S(1)} %collective-permute-done.15.refs_5_.refs_4_), channel_id=1, source_target_pairs={{1,0},{2,1},{5,4},{6,5},{9,8},{10,9},{13,12},{14,13},{17,16},{18,1... | collective-permute-start | bytes 3145736 | tf_op jit(solution)/shard_map/ppermute | solution.py:64
  331.2 224.6 %reduce-scatter.7.cloned.1.call-start = ((), (), s32[]{:S(2)}) async-start(), calls=%async_computation.13 | async-start | bytes 18874368 | tf_op jit(solution)/shard_map/reduce_scatter | solution.py:1161
  370.7 30.5 %collective-permute-start.23 = (bf16[256,2048]{1,0:T(8,128)(2,1)}, bf16[256,2048]{1,0:T(8,128)(2,1)}, u32[]{:S(2)}, u32[]{:S(2)}) collective-permute-start(bf16[256,2048]{1,0:T(8,128)(2,1)} %get-tuple-element.428), channel_id=1, source_target_pairs={{2,1},{3,2},{6,5},{7,6},{10,9},{11,10},{14,13},{15,14},{18,17},{19... | collective-permute-start | bytes 3145736 | tf_op jit(solution)/shard_map/ppermute | solution.py:120
  372.3 28.9 %collective-permute-start.22 = (bf16[256,2048]{1,0:T(8,128)(2,1)}, bf16[256,2048]{1,0:T(8,128)(2,1)}, u32[]{:S(2)}, u32[]{:S(2)}) collective-permute-start(bf16[256,2048]{1,0:T(8,128)(2,1)} %get-tuple-element.429), channel_id=1, source_target_pairs={{0,1},{1,2},{4,5},{5,6},{8,9},{9,10},{12,13},{13,14},{16,17},{17,1... | collective-permute-start | bytes 3145736 | tf_op jit(solution)/shard_map/ppermute | solution.py:119
  446.6 157.3 %reduce-scatter.9.cloned.1.call-start = ((), (), s32[]{:S(2)}) async-start(), calls=%async_computation.14 | async-start | bytes 9437184 | tf_op jit(solution)/shard_map/reduce_scatter | solution.py:1177
  469.3 114.4 %all-to-all-start.2 = ((bf16[4,256,2048]{2,1,0:T(8,128)(2,1)}), bf16[4,256,2048]{2,1,0:T(8,128)(2,1)}, u32[]{:S(2)}, u32[]{:S(2)}) async-start(bf16[4,256,2048]{2,1,0:T(8,128)(2,1)} %bitcast.42), calls=%async_computation.4 | async-start | bytes 8388608 | tf_op jit(solution)/shard_map/all_to_all | solution.py:136
  474.5 205.6 %reduce-scatter.11.cloned.1.call-start = ((), (), s32[]{:S(2)}) async-start(), calls=%async_computation.15 | async-start | bytes 3538944 | tf_op jit(solution)/shard_map/reduce_scatter | solution.py:1212
  555.8 28.0 %collective-permute-start.31 = (bf16[256,2048]{1,0:T(8,128)(2,1)}, bf16[256,2048]{1,0:T(8,128)(2,1)}, u32[]{:S(2)}, u32[]{:S(2)}) collective-permute-start(bf16[256,2048]{1,0:T(8,128)(2,1)} %blocks_times.6), channel_id=1, source_target_pairs={{3,2},{7,6},{11,10},{15,14},{19,18},{23,22},{27,26},{31,30}} | collective-permute-start | bytes 3145736 | tf_op jit(solution)/shard_map/ppermute | solution.py:120
  612.9 57.4 %all-to-all-start.3 = ((bf16[4,512,256]{2,1,0:T(8,128)(2,1)}), bf16[4,512,256]{2,1,0:T(8,128)(2,1)}, u32[]{:S(2)}, u32[]{:S(2)}) async-start(bf16[4,512,256]{2,1,0:T(8,128)(2,1)} %bitcast.44), calls=%async_computation.6 | async-start | bytes 2097152 | tf_op jit(solution)/shard_map/all_to_all | solution.py:136
  623.3 47.0 %collective-permute-start.38 = (bf16[256,2048]{1,0:T(8,128)(2,1)}, bf16[256,2048]{1,0:T(8,128)(2,1)}, u32[]{:S(2)}, u32[]{:S(2)}) collective-permute-start(bf16[256,2048]{1,0:T(8,128)(2,1)} %get-tuple-element.430), channel_id=1, source_target_pairs={{1,0},{2,1},{3,2},{5,4},{6,5},{7,6},{9,8},{10,9},{11,10},{13,12},{... | collective-permute-start | bytes 3145736 | tf_op jit(solution)/shard_map/ppermute | solution.py:120
  624.6 45.7 %collective-permute-start.37 = (bf16[256,2048]{1,0:T(8,128)(2,1)}, bf16[256,2048]{1,0:T(8,128)(2,1)}, u32[]{:S(2)}, u32[]{:S(2)}) collective-permute-start(bf16[256,2048]{1,0:T(8,128)(2,1)} %get-tuple-element.431), channel_id=1, source_target_pairs={{0,1},{1,2},{2,3},{4,5},{5,6},{6,7},{8,9},{9,10},{10,11},{12,13},{... | collective-permute-start | bytes 3145736 | tf_op jit(solution)/shard_map/ppermute | solution.py:119
  (107 other events, 1798.8 us)
Sparse Core Ops, SparseCore 0:
  10.5 32.5 all-gather.4
  45.6 90.1 all-gather.6
  138.2 58.0 all-gather.8
  198.0 58.7 all-gather.10
  331.3 68.5 reduce-scatter.4
  403.7 122.2 reduce-scatter.6
  529.9 73.9 reduce-scatter.8
  607.2 46.2 reduce-scatter.10
